TPU v7x, 128 devices: a whole 4x4x4 slice. The times are simulated.
128 devices in a mesh: section: 2 (over z_hi), dp: 16 (over z_lo, x, core), tensor: 4 (over y).
Axes of the slice: x: 4, y: 4, z: 4 (z_hi: 2, z_lo: 2; z = z_hi * 2 + z_lo), core: 2. Of those that a mesh axis runs over, the one named last changes fastest.
Arguments:
- tokens: bfloat16 [2, 8192, 1024], P(None, ('dp', 'tensor')), may hold values from -6 to 6
- cotangent: bfloat16 [2, 8192, 1024], P(None, ('dp', 'tensor')), may hold values from -6 to 6
- lengths: int32 [2, 16, 4], P(None, 'dp'), may hold values from 1 to 386, 512 in all within a row
- gains: float32 [2, 2, 1024], P('section'), may hold values from 0.25 to 1.75
- w_qkv: bfloat16 [2, 1024, 3, 1024], P('section', None, None, 'tensor'), may hold values from -0.1875 to 0.1875
- w_out: bfloat16 [2, 1024, 1024], P('section', 'tensor'), may hold values from -1.5 to 1.5
- w_up: bfloat16 [2, 1024, 2, 2624], P('section', None, None, 'tensor'), may hold values from -0.1875 to 0.1875
- w_down: bfloat16 [2, 2624, 1024], P('section', 'tensor'), may hold values from -0.125 to 0.125
Outputs:
- section_out: bfloat16 [2, 2, 8192, 1024], P('section', None, ('dp', 'tensor'))
- input_grads: bfloat16 [2, 2, 8192, 1024], P('section', None, ('dp', 'tensor'))
- grad_gains: float32 [2, 2, 1024], P('section')
- grad_qkv: float32 [2, 1024, 3, 1024], P('section', None, None, 'tensor')
- grad_out: float32 [2, 1024, 1024], P('section', 'tensor')
- grad_up: float32 [2, 1024, 2, 2624], P('section', None, None, 'tensor')
- grad_down: float32 [2, 2624, 1024], P('section', 'tensor')
Inputs may be any that keep to these rules, and one draw needn't show every extreme that they name: `lengths`: in each group's micro-batch the 4 documents fill all 512 rows; the longest has exactly 386 rows.
All inputs are finite; a program needn't handle non-finite values.
Results may differ from a plain program's by a relative error of at most 0.03.
Values may be sent and summed in bfloat16 or wider, within the bound.
No kernel may reach another device: no remote copies, remote signals or barrier semaphores. Data moves between devices by JAX's collectives and lax.ppermute only.
A program may use at most 192 MiB of HBM per device.

v0:
```python
import functools

import jax
import jax.numpy as jnp
from jax import lax
from jax.experimental import pallas as pl
from jax.experimental.pallas import tpu as pltpu
from jax.sharding import Mesh
from jax.sharding import PartitionSpec as P

HEAD_DIM = 64
WINDOW = 128

epsilon = 1e-05
bf16 = jnp.bfloat16
f32 = jnp.float32

BLOCK = 256

DP = ("zlo", "x", "core")


def around(block, axis, distance):
    count = lax.axis_size(axis)
    return lax.ppermute(block, axis, [(i, (i + distance) % count) for i in range(count)])


def swap_core(block):
    return lax.ppermute(block, "core", [(0, 1), (1, 0)])


def swap_section(block):
    return lax.ppermute(block, "section", [(0, 1), (1, 0)])


def swap_layer(block):
    return lax.ppermute(block, ("section", "zlo"), [(0, 3), (1, 2), (2, 1), (3, 0)])


def gather_parts(block):
    far = around(block, "tensor", 2)
    ahead = around(block, "tensor", -1)
    behind = around(block, "tensor", 1)
    return [joined([block, ahead, behind]), far]


def scatter_parts(near, far):
    rows = far.shape[0]
    sent_far = around(far.astype(bf16), "tensor", 2)
    sent_ahead = around(near[rows : 2 * rows].astype(bf16), "tensor", 1)
    sent_behind = around(near[2 * rows :].astype(bf16), "tensor", -1)
    kept = near[:rows].astype(f32)
    return kept + sent_far.astype(f32) + sent_ahead.astype(f32) + sent_behind.astype(f32)


def joined(parts, axis=0):
    return jnp.concatenate(parts, axis=axis)


def after_all(values, *others):
    return lax.optimization_barrier((values,) + others)[0]


def sum_tensor(block):
    return (
        block
        + around(block, "tensor", 2)
        + around(block, "tensor", 1)
        + around(block, "tensor", -1)
    )


def layer_norm(values, gain_scale):
    centered = values - jnp.mean(values, axis=-1, keepdims=True)
    variance = jnp.mean(centered * centered, axis=-1, keepdims=True)
    return centered * lax.rsqrt(variance + epsilon) * gain_scale


def doc_layout(doc_lengths, indices):
    doc_ends = jnp.cumsum(doc_lengths)
    passed = indices[:, None] >= doc_ends[None, :]
    doc_ids = jnp.sum(passed.astype(jnp.int32), axis=1)
    starts = jnp.sum(jnp.where(passed, doc_lengths[None, :], 0), axis=1)
    return (doc_ids, indices - starts)


def rope_tables(positions, rope_base, heads):
    half_dim = HEAD_DIM // 2
    inverse = rope_base ** (-2.0 * jnp.arange(half_dim, dtype=f32) / HEAD_DIM)
    angles = positions.astype(f32)[:, None] * inverse
    cosine, sine = jnp.cos(angles), jnp.sin(angles)
    cosine = jnp.concatenate([cosine, cosine], axis=-1)
    sine = jnp.concatenate([-sine, sine], axis=-1)
    return (jnp.tile(cosine, (1, heads)), jnp.tile(sine, (1, heads)))


def contract_rows(left_rows, right_rows):
    return lax.dot_general(
        left_rows, right_rows, (((0,), (0,)), ((), ())), preferred_element_type=f32
    )


def contract_last(left_rows, weight):
    return lax.dot_general(
        left_rows, weight, (((1,), (1,)), ((), ())), preferred_element_type=f32
    )


def times(left_rows, weight):
    return jnp.dot(left_rows, weight, preferred_element_type=f32)


def gelu_product(first_half, second_half):
    return jax.nn.gelu(first_half, approximate=False) * second_half


def dot_nt(left, right):
    return lax.dot_general(left, right, (((1,), (1,)), ((), ())), preferred_element_type=f32)


def dot_tn(left, right):
    return lax.dot_general(left, right, (((0,), (0,)), ((), ())), preferred_element_type=f32)


def swap_halves(values):
    width = values.shape[1]
    lanes = lax.broadcasted_iota(jnp.int32, values.shape, 1)
    up = pltpu.roll(values, width - HEAD_DIM // 2, 1)
    down = pltpu.roll(values, HEAD_DIM // 2, 1)
    return jnp.where(lanes % HEAD_DIM < HEAD_DIM // 2, up, down)


def excluded_bias(marks_row, marks_col, start, windowed):
    docs = marks_row[0:1, pl.ds(start, BLOCK)]
    allowed = marks_col[:, 0:1] == docs
    if windowed:
        apart = marks_col[:, 1:2] - marks_row[1:2, pl.ds(start, BLOCK)]
        allowed = allowed & (jnp.abs(apart) <= WINDOW // 2)
    return jnp.where(allowed, 0.0, -1e30)


def attend_kernel(
    windowed,
    near, far, w_qkv, w_out, cosine, sine, marks_row, marks_col,
    queries, keys, values, logs, attended, near_term, far_term,
    projected,
):
    near_rows = near.shape[0]
    width = w_out.shape[0]
    projected[:near_rows] = jnp.dot(near[...], w_qkv[...], preferred_element_type=f32)
    projected[near_rows:] = jnp.dot(far[...], w_qkv[...], preferred_element_type=f32)
    for index, target in ((0, queries), (1, keys)):
        part = projected[:, index * width : (index + 1) * width]
        turned = part * cosine[...] + swap_halves(part) * sine[...]
        target[...] = turned.astype(bf16)
    values[...] = projected[:, 2 * width :].astype(bf16)
    heads = width // HEAD_DIM
    lanes = lax.broadcasted_iota(jnp.int32, (BLOCK, width), 1) // HEAD_DIM

    def step(index, carry):
        start = pl.multiple_of(index * BLOCK, BLOCK)
        bias = excluded_bias(marks_row, marks_col, start, windowed)
        block = queries[pl.ds(start, BLOCK)] * jnp.asarray(HEAD_DIM ** (-0.5), bf16)
        total = jnp.zeros((BLOCK, width), f32)
        for head in range(heads):
            own = jnp.where(lanes == head, block, jnp.zeros_like(block))
            scores = dot_nt(keys[...], own) + bias
            largest = jnp.max(scores, axis=0, keepdims=True)
            powers = jnp.exp(scores - largest)
            sums = jnp.sum(powers, axis=0, keepdims=True)
            soft = (powers * (1.0 / sums)).astype(bf16)
            logs[pl.ds(head, 1), pl.ds(start, BLOCK)] = largest + jnp.log(sums)
            total = jnp.where(lanes == head, dot_tn(soft, values[...]), total)
        attended[pl.ds(start, BLOCK)] = total.astype(bf16)
        return carry

    lax.fori_loop(0, queries.shape[0] // BLOCK, step, 0)
    far_term[...] = jnp.dot(
        attended[near_rows:], w_out[...], preferred_element_type=f32
    ).astype(bf16)
    near_term[...] = jnp.dot(
        attended[:near_rows], w_out[...], preferred_element_type=f32
    ).astype(bf16)


def attend_back_kernel(
    windowed,
    near, far, w_qkv, w_out, cosine, sine, marks_row, marks_col,
    queries, keys, values, logs,
    grad_projected, near_term, far_term,
    grad_attended, grad_queries, grad_keys, grad_values,
):
    near_rows = near.shape[0]
    width = w_out.shape[0]
    grad_attended[:near_rows] = dot_nt(near[...], w_out[...]).astype(bf16)
    grad_attended[near_rows:] = dot_nt(far[...], w_out[...]).astype(bf16)
    grad_keys[...] = jnp.zeros_like(grad_keys)
    grad_values[...] = jnp.zeros_like(grad_values)
    heads = width // HEAD_DIM
    lanes = lax.broadcasted_iota(jnp.int32, (BLOCK, width), 1) // HEAD_DIM
    all_lanes = lax.broadcasted_iota(jnp.int32, queries.shape, 1) // HEAD_DIM

    def step(index, carry):
        start = pl.multiple_of(index * BLOCK, BLOCK)
        bias = excluded_bias(marks_row, marks_col, start, windowed)
        block = queries[pl.ds(start, BLOCK)] * jnp.asarray(HEAD_DIM ** (-0.5), bf16)
        grad_block = grad_attended[pl.ds(start, BLOCK)]
        total = jnp.zeros((BLOCK, width), f32)
        more_keys = jnp.zeros(queries.shape, f32)
        more_values = jnp.zeros(queries.shape, f32)
        for head in range(heads):
            own = jnp.where(lanes == head, block, jnp.zeros_like(block))
            own_grad = jnp.where(lanes == head, grad_block, jnp.zeros_like(grad_block))
            scores = dot_nt(keys[...], own) + bias
            soft = jnp.exp(scores - logs[pl.ds(head, 1), pl.ds(start, BLOCK)])
            grad_soft = dot_nt(values[...], own_grad)
            dots = jnp.sum(soft * grad_soft, axis=0, keepdims=True)
            grad_scores = (soft * (grad_soft - dots)).astype(bf16)
            more_values += jnp.dot(soft.astype(bf16), own_grad, preferred_element_type=f32)
            more_keys += jnp.dot(grad_scores, own, preferred_element_type=f32)
            total = jnp.where(lanes == head, dot_tn(grad_scores, keys[...]), total)
        grad_queries[pl.ds(start, BLOCK)] = total * HEAD_DIM ** (-0.5)
        grad_keys[...] += more_keys
        grad_values[...] += more_values
        return carry

    lax.fori_loop(0, queries.shape[0] // BLOCK, step, 0)
    for index, source in ((0, grad_queries), (1, grad_keys)):
        part = source[...]
        back = part * cosine[...] - swap_halves(part) * sine[...]
        grad_projected[:, index * width : (index + 1) * width] = back.astype(bf16)
    grad_projected[:, 2 * width :] = grad_values[...].astype(bf16)
    far_term[...] = dot_nt(grad_projected[near_rows:], w_qkv[...]).astype(bf16)
    near_term[...] = dot_nt(grad_projected[:near_rows], w_qkv[...]).astype(bf16)


def whole_call(kernel, out_shapes, scratch_shapes, flops, *operands):
    whole = pl.BlockSpec(memory_space=pltpu.VMEM)
    return pl.pallas_call(
        kernel,
        out_shape=[jax.ShapeDtypeStruct(*shape) for shape in out_shapes],
        in_specs=[whole] * len(operands),
        out_specs=[whole] * len(out_shapes),
        scratch_shapes=scratch_shapes,
        compiler_params=pltpu.CompilerParams(vmem_limit_bytes=40 * 1024 * 1024),
        cost_estimate=pl.CostEstimate(flops=flops, bytes_accessed=8 << 20, transcendentals=1 << 20),
    )(*operands)


def in_turn(work, parts):
    first = work(0, parts[0])
    return first, work(1, after_all(parts[1], first))


def forward_layer(inputs, normed_parts, gain_mid, weights, allowed, tables, late, points):
    w_qkv, w_out = weights[0], weights[1]
    near_rows, model_width = normed_parts[0].shape
    far_rows = normed_parts[1].shape[0]
    full_rows = near_rows + far_rows
    width = w_out.shape[0]
    windowed, marks_row, marks_col = allowed
    queries, keys, values, logs, attended, near_term, far_term = whole_call(
        functools.partial(attend_kernel, windowed),
        [((full_rows, width), bf16)] * 3
        + [((8, full_rows), f32), ((full_rows, width), bf16)]
        + [((near_rows, model_width), bf16), ((far_rows, model_width), bf16)],
        [pltpu.VMEM((full_rows, 3 * width), f32)],
        3 << 30,
        *normed_parts, w_qkv, w_out, *tables, marks_row, marks_col,
    )
    points[1](far_term)
    resid_mid = inputs + scatter_parts(near_term, far_term)
    points[2](resid_mid)
    mid_parts = gather_parts(layer_norm(resid_mid, gain_mid).astype(bf16))
    points[3](mid_parts)
    w_up, w_down = weights[2], weights[3]

    def feed(k, part):
        hidden = contract_last(part, w_up)
        local_hidden = hidden.shape[1] // 2
        gelu_in = hidden[:, :local_hidden]
        gate_mult = hidden[:, local_hidden:]
        mixed = gelu_product(gelu_in, gate_mult).astype(bf16)
        return gelu_in, gate_mult, mixed, None if late else times(mixed, w_down).astype(bf16)

    fed = in_turn(feed, mid_parts)
    if late:

        def result(gate):
            held = after_all((fed[0][2], fed[1][2]), gate)
            return [times(mixed, w_down).astype(bf16) for mixed in held]

    else:
        result = resid_mid + scatter_parts(fed[0][3], fed[1][3])
    kept = dict(
        inputs=inputs,
        resid_mid=resid_mid,
        normed=normed_parts,
        queries=queries,
        keys=keys,
        values=values,
        logs=logs,
        attended=attended,
        normed_mid=mid_parts,
        gelu_in=(fed[0][0], fed[1][0]),
        gate_mult=(fed[0][1], fed[1][1]),
        mixed=(fed[0][2], fed[1][2]),
    )
    return (result, kept)


def backward_ffn(grad_result, kept, gain_mid, weights, gate):
    w_up, w_down = weights[2], weights[3]
    grad_parts = after_all(gather_parts(grad_result.astype(bf16)), gate)

    def feed_back(k, part):
        grad_mixed = contract_last(part, w_down)
        unused, pull_gelu = jax.vjp(gelu_product, kept["gelu_in"][k], kept["gate_mult"][k])
        terms = tuple(term.astype(bf16) for term in pull_gelu(grad_mixed))
        return terms[0], terms[1], times(joined(terms, 1), w_up).astype(bf16)

    near, far = in_turn(feed_back, grad_parts)
    grad_normed_mid = scatter_parts(near[2], far[2])
    unused, pull_norm = jax.vjp(layer_norm, kept["resid_mid"], gain_mid)
    grad_resid, grad_gain = pull_norm(grad_normed_mid)

    def weight_grads(gate):
        outer, inner, left, first, second = after_all(
            (grad_parts, kept["mixed"], kept["normed_mid"], (near[0], far[0]), (near[1], far[1])),
            gate,
        )
        outer, inner, left = joined(outer), joined(inner), joined(left)
        first, second = joined(first), joined(second)
        half = inner.shape[1] // 2
        front, back = inner[:, :half], inner[:, half:]
        sent_up, add_up = add_core(lambda core: contract_rows(core(first, second), left))
        sent_down, add_down = add_core(lambda core: contract_rows(core(front, back), outer))

        def pack(gate):
            up, down = add_up(gate), add_down(gate)
            rows = up.shape[0] + down.shape[0]
            blank = jnp.zeros((-rows % 128, up.shape[1]), bf16)
            return joined([up, down, blank])

        return (sent_up, sent_down), pack

    return (grad_result + grad_resid, weight_grads, grad_gain)


def backward_attn(grad_mid, kept, gain_first, weights, allowed, tables, gate, pack):
    w_qkv, w_out = weights[0], weights[1]
    grad_parts = gather_parts(grad_mid.astype(bf16))
    near, far = after_all(grad_parts, gate)
    full_rows, width = kept["queries"].shape
    windowed, marks_row, marks_col = allowed
    grad_projected, near_term, far_term = whole_call(
        functools.partial(attend_back_kernel, windowed),
        [((full_rows, 3 * width), bf16), (near.shape, bf16), (far.shape, bf16)],
        [pltpu.VMEM((full_rows, width), bf16)] + [pltpu.VMEM((full_rows, width), f32)] * 3,
        4 << 30,
        near, far, w_qkv, w_out, *tables, marks_row, marks_col,
        kept["queries"], kept["keys"], kept["values"], kept["logs"],
    )
    packed = pack(grad_projected)
    near_term, far_term = after_all((near_term, far_term), packed)
    grad_normed = scatter_parts(near_term, far_term)
    unused, pull_norm = jax.vjp(layer_norm, kept["inputs"], gain_first)
    grad_resid, grad_gain = pull_norm(grad_normed)

    def gain_before():
        total = 0.0
        for term, normed in zip((near_term, far_term), kept["normed"]):
            total = total + jnp.sum(term.astype(f32) * normed.astype(f32), axis=0)
        return total / gain_first

    def weight_grads(gate, gains):
        outer, inner, left, right = after_all(
            (grad_parts, kept["attended"], kept["normed"], grad_projected), gate
        )
        outer, left = joined(outer), joined(left)
        width = inner.shape[1]
        of_q, of_k, of_v = (right[:, i * width : (i + 1) * width] for i in range(3))
        one = add_core(lambda core: contract_rows(left, core(of_q, of_v)))[1](())
        two = add_core(lambda core: contract_rows(core(left, outer), core(of_k, inner)))[1](())
        extra = jnp.stack(gains).astype(bf16).reshape(-1, width)
        blank = jnp.zeros((-extra.shape[0] % 128, width), bf16)
        return joined([one, two, extra, blank])

    return (grad_mid + grad_resid, weight_grads, grad_gain, gain_before, packed)


def fetch_half(own, after):
    piece = own.shape[0] // 2
    start = lax.axis_index("core") * piece
    return swap_layer(lax.dynamic_slice_in_dim(after_all(own, after), start, piece))


def both_halves(half, after=()):
    half = after_all(half, after)
    return in_order(lax.axis_index("core"), half, swap_core(half))


def by_layer(is_first, own, other):
    return jnp.where(is_first, own, other), jnp.where(is_first, other, own)


def in_order(index, mine, other):
    low = jnp.where(index == 0, mine, other)
    high = jnp.where(index == 0, other, mine)
    return jnp.concatenate([low, high], axis=0)


def add_core(product):
    is_core0 = lax.axis_index("core") == 0
    sent = product(lambda one, two: jnp.where(is_core0, two, one)).astype(bf16)

    def add(gate):
        held = product(lambda one, two: after_all(jnp.where(is_core0, one, two), gate))
        return (held + swap_core(sent).astype(f32)).astype(bf16)

    return sent, add


def reduce_part(grads):
    return lax.psum_scatter(grads, ("zlo", "x"), scatter_dimension=0, tiled=True)


def reduce_part_now(grads):
    pieces = lax.all_to_all(grads, ("zlo", "x"), 0, 0, tiled=True)
    pieces = pieces.reshape(8, -1, pieces.shape[1])
    return jnp.sum(pieces.astype(f32), axis=0).astype(bf16)


def spread_part(part):
    copies = jnp.broadcast_to(part[None], (8,) + part.shape).reshape(-1, part.shape[1])
    return lax.all_to_all(copies, ("zlo", "x"), 0, 0, tiled=True)


def pick_sections(is_first, part_first, part_second):
    own = jnp.where(is_first, part_first, part_second)
    sent = jnp.where(is_first, part_second, part_first)
    return own, sent


def local(tokens, cotangent, lengths, gains, w_qkv, w_out, w_up, w_down):
    section_index = lax.axis_index("section")
    is_first = section_index == 0
    row_count = tokens.shape[1]
    full_rows = row_count * lax.axis_size("tensor")
    start_rows = jnp.where(is_first, tokens[0], tokens[1])
    end_grads = jnp.where(is_first, cotangent[0], cotangent[1])
    start_parts = gather_parts(start_rows)
    gains_other = swap_layer(gains[0])
    gains0 = jnp.where(is_first, gains[0], gains_other)
    gains1 = jnp.where(is_first, gains_other, gains[0])
    start_rows = start_rows.astype(f32)
    own = (
        jnp.transpose(w_qkv[0], (1, 0, 2)).reshape(-1, w_qkv.shape[3]),
        w_out[0],
        jnp.transpose(w_up[0], (1, 2, 0)).reshape(-1, w_up.shape[1]),
        w_down[0],
    )
    half_qkv = fetch_half(own[0], ())
    half_out = fetch_half(own[1], ())
    start_parts, lengths = after_all((start_parts, lengths), (half_qkv, half_out))
    first_parts = in_turn(
        lambda k, part: layer_norm(part.astype(f32), gains0[0]).astype(bf16), start_parts
    )
    qkv0, qkv1 = by_layer(is_first, own[0], both_halves(half_qkv))
    layer0 = [joined(jnp.split(qkv0, 3), 1)]
    layer1 = [joined(jnp.split(qkv1, 3), 1)]
    hidden_width = w_up.shape[3]
    moving = []

    out0, out1 = by_layer(is_first, own[1], both_halves(half_out))
    layer0.append(out0)
    layer1.append(out1)
    moving.append(fetch_half(own[2][:hidden_width], half_out))

    def at_far_term(far_term):
        moving.append(both_halves(moving[0], far_term))
        moving.append(fetch_half(own[2][hidden_width:], (moving[0], far_term)))

    def at_mid(resid_mid):
        moving.append(both_halves(moving[2], resid_mid))
        moving.append(fetch_half(own[3], (moving[2], resid_mid)))

    def at_gathered(parts):
        up0, up1 = by_layer(is_first, own[2], joined([moving[1], moving[3]]))
        down0, down1 = by_layer(is_first, own[3], both_halves(moving[4], parts))
        layer0.extend([up0, down0])
        layer1.extend([up1, down1])

    points = (None, at_far_term, at_mid, at_gathered)

    doc_lengths = jnp.where(is_first, lengths[0, 0], lengths[1, 0])
    indices = jnp.arange(full_rows, dtype=jnp.int32)
    blocks = jnp.array([0, 1, 3, 2], jnp.int32) + lax.axis_index("tensor")
    indices = (jnp.repeat(blocks, row_count) * row_count + indices % row_count) % full_rows
    doc_ids, positions = doc_layout(doc_lengths, indices)
    marks_row = jnp.stack([doc_ids, indices])
    marks_col = jnp.stack([doc_ids, indices], axis=1)
    allowed0 = (True, marks_row, marks_col)
    allowed1 = (False, marks_row, marks_col)
    heads = w_out.shape[1] // HEAD_DIM
    tables0 = rope_tables(positions, 10000.0, heads)
    tables1 = rope_tables(positions, 160000.0, heads)

    out0, kept0 = forward_layer(
        start_rows, first_parts, gains0[1], layer0, allowed0, tables0, False, points
    )
    out0 = out0.astype(bf16)
    second_rows = out0.astype(f32)
    second_parts = gather_parts(layer_norm(second_rows, gains1[0]).astype(bf16))
    out1_of, kept1 = forward_layer(
        second_rows, second_parts, gains1[1], layer1, allowed1, tables1, True, (lambda value: None,) * 4
    )
    mid1, ffn_grads1, gain_mid1 = backward_ffn(
        end_grads.astype(f32), kept1, gains1[1], layer1, ()
    )
    ffn_sent1, ffn_pack1 = ffn_grads1(mid1)
    in1, attn_grads1, gain_first1, unused, unused = backward_attn(
        mid1, kept1, gains1[0], layer1, allowed1, tables1, ffn_sent1, lambda gate: ()
    )
    in1 = in1.astype(bf16)
    ffn_pack1 = ffn_pack1(in1)
    mid0, ffn_grads0, gain_mid0 = backward_ffn(
        in1.astype(f32), kept0, gains0[1], layer0, ffn_pack1
    )
    model_width = w_qkv.shape[1]
    attn_pack1 = attn_grads1(in1, [gain_first1, gain_mid1])
    attn_width = attn_pack1.shape[1]
    pieces = [pack.reshape(8, -1, model_width) for pack in (ffn_pack1, attn_pack1)]
    ffn_rows, attn_rows = pieces[0].shape[1], pieces[1].shape[1]
    part_rows = ffn_rows + attn_rows
    blank = jnp.zeros((8, -part_rows % 16, model_width), bf16)
    part1 = reduce_part(joined(pieces + [blank], 1).reshape(-1, model_width))
    ffn_pack0 = ffn_grads0(mid0)[1](())
    in0, attn_grads0, unused, gain_before, unused = backward_attn(
        mid0, kept0, gains0[0], layer0, allowed0, tables0, (ffn_pack0, part1), lambda gate: ()
    )
    in0 = in0.astype(bf16)
    ffn0 = reduce_part(ffn_pack0)
    attn_pack0 = attn_grads0((), [gain_before(), gain_mid0])
    out1_terms = out1_of(ffn_pack0)
    out1 = (kept1["resid_mid"] + scatter_parts(*out1_terms)).astype(bf16)
    attn0 = reduce_part_now(attn_pack0)
    part0 = joined([ffn0, attn0.reshape(-1, model_width)])
    own_part, sent_part = pick_sections(is_first, part0, part1[:part_rows])
    sent_part = after_all(sent_part, in0, out1)
    part = (own_part.astype(f32) + swap_section(sent_part).astype(f32)).astype(bf16)
    part = joined([part, jnp.zeros((-part_rows % 16, model_width), bf16)])
    half = spread_part(part)
    halves = [both.reshape(8, -1, model_width) for both in (half, swap_core(half))]
    is_core0 = lax.axis_index("core") == 0

    def of_core(core, first_row, rows, width, start, count):
        mine, other = (
            both[:, first_row : first_row + rows].reshape(-1, width)[start : start + count]
            for both in halves
        )
        return jnp.where(is_core0 == (core == 0), mine, other).astype(f32)

    def of_ffn(core, start, count):
        return of_core(core, 0, ffn_rows, model_width, start, count)

    def of_attn(core, start, count):
        return of_core(core, ffn_rows, attn_rows, attn_width, start, count)

    down_rows = w_down.shape[1] // 2
    grad_up = jnp.stack([of_ffn(core, 0, hidden_width) for core in range(2)])
    grad_down = joined([of_ffn(core, hidden_width, down_rows) for core in range(2)])
    gain_rows = sum(of_attn(core, 2 * model_width, 8) for core in range(2))
    gain_total = sum_tensor(gain_rows).reshape(2, -1)
    grad_qkv = jnp.stack(
        [
            of_attn(0, 0, model_width),
            of_attn(0, model_width, model_width),
            of_attn(1, 0, model_width),
        ]
    )
    grad_out = of_attn(1, model_width, model_width).T
    got_out = swap_section(jnp.where(is_first, out1, out0))
    got_out, got_in_sent = after_all((got_out, jnp.where(is_first, in1, in0)), half)
    section_out = jnp.stack(
        [jnp.where(is_first, out0, got_out), jnp.where(is_first, got_out, out1)]
    )
    got_in = swap_section(got_in_sent)
    input_grads = jnp.stack(
        [jnp.where(is_first, in0, got_in), jnp.where(is_first, got_in, in1)]
    )
    return (
        section_out[None],
        input_grads[None],
        gain_total[None],
        jnp.transpose(grad_qkv, (1, 0, 2))[None],
        grad_out[None],
        jnp.transpose(grad_up, (2, 0, 1))[None],
        grad_down[None],
    )


def solution(mesh):
    sizes = dict(zip(mesh.axis_names, mesh.devices.shape))
    fine = Mesh(
        mesh.devices.reshape(sizes["section"], 2, sizes["dp"] // 4, 2, sizes["tensor"]),
        ("section", "zlo", "x", "core", "tensor"),
    )
    rows = ("zlo", "x", "core", "tensor")
    in_specs = (
        P(None, rows, None),
        P(None, rows, None),
        P(None, DP, None),
        P("section", None, None),
        P("section", None, None, "tensor"),
        P("section", "tensor", None),
        P("section", None, None, "tensor"),
        P("section", "tensor", None),
    )
    out_specs = (
        P("section", None, rows, None),
        P("section", None, rows, None),
        P("section", None, None),
        P("section", None, None, "tensor"),
        P("section", "tensor", None),
        P("section", None, None, "tensor"),
        P("section", "tensor", None),
    )
    return jax.shard_map(local, mesh=fine, in_specs=in_specs, out_specs=out_specs, check_vma=False)
```

profile of v0, /device:TPU:8, one launch (start us, length us, event | category | flops | bytes accessed | tf_op | source)
XLA Modules:
  0.0 534.9 jit_solution(6272122808376225826)
XLA Ops:
  14.2 4.1 collective-permute-start.4
  20.5 3.6 slice_bitcast_fusion.1
  24.2 3.2 collective-permute-start.3
  32.6 13.4 %collective-permute-done.3 = bf16[1536,256]{1,0:T(8,128)(2,1)} collective-permute-done((bf16[1536,256]{1,0:T(8,128)(2,1)S(1)}, bf16[1536,256]{1,0:T(8,128)(2,1)}, u32[]{:S(2)}, u32[]{:S(2)}) %collective-permute-start.3) | collective-permute-done | bytes 786464 | tf_op jit(solution)/shard_map/ppermute | solution.py:37
  58.6 4.8 shard_map.144
  68.1 3.2 collective-permute-start.15
  71.4 12.8 %collective-permute-start.14 = (bf16[328,1024]{1,0:T(8,128)(2,1)}, bf16[328,1024]{1,0:T(8,128)(2,1)S(1)}, u32[]{:S(2)}, u32[]{:S(2)}) collective-permute-start(bf16[328,1024]{1,0:T(8,128)(2,1)} %collective-permute-done.13), channel_id=1, source_target_pairs={{0,4},{4,0},{1,5},{5,1},{2,6},{6,2},{3,7},{7,3},{8,12},{12,8},{9,1... | collective-permute-start | bytes 2015240 | tf_op jit(solution)/shard_map/ppermute | solution.py:29
  89.4 4.3 collective-permute-done.12
  96.9 6.2 %collective-permute-done.18 = bf16[128,1024]{1,0:T(8,128)(2,1)S(1)} collective-permute-done((bf16[128,1024]{1,0:T(8,128)(2,1)S(1)}, bf16[128,1024]{1,0:T(8,128)(2,1)S(1)}, u32[]{:S(2)}, u32[]{:S(2)}) %collective-permute-start.18) | collective-permute-done | bytes 262176 | tf_op jit(solution)/shard_map/ppermute | solution.py:25
  105.4 2.6 bitcast_select_fusion
  109.7 3.0 multiply_convert_fusion.3
  126.3 3.8 collective-permute-done.20
  130.8 2.7 collective-permute-start.24
  142.9 4.2 collective-permute-done.25.far
  147.2 4.9 shard_map.145
  154.6 5.0 collective-permute-start.26
  161.7 3.1 collective-permute-done.28
  164.9 7.2 %collective-permute-start.34 = (bf16[128,1024]{1,0:T(8,128)(2,1)S(1)}, bf16[128,1024]{1,0:T(8,128)(2,1)S(1)}, u32[]{:S(2)}, u32[]{:S(2)}) collective-permute-start(bf16[128,1024]{1,0:T(8,128)(2,1)S(1)} %select_bitcast_fusion.9), channel_id=1, source_target_pairs={{0,2},{1,3},{2,0},{3,1},{4,6},{5,7},{6,4},{7,5},{8,10},{9,11},{10,... | collective-permute-start | bytes 786440 | tf_op jit(solution)/shard_map/ppermute | solution.py:25
  176.1 4.5 collective-permute-done.34
  180.6 3.2 collective-permute-start.31
  186.7 3.0 add_convert_fusion.5
  192.4 3.3 collective-permute-start.37
  217.9 2.8 collective-permute-done.40.far
  220.6 6.7 %shard_map.146 = (bf16[512,768]{1,0:T(8,128)(2,1)S(1)}, bf16[384,1024]{1,0:T(8,128)(2,1)S(1)}, bf16[128,1024]{1,0:T(8,128)(2,1)S(1)}) custom-call(bf16[384,1024]{1,0:T(8,128)(2,1)S(1)} %pad_maximum_fusion.10.near, bf16[128,1024]{1,0:T(8,128)(2,1)S(1)} %collective-permute-done.40.far, bf16[1024,768]{1,0:T(8,128)(2,1)S(1)} %pad_maximum_fusion.3.w_qkv, ...), custom_call_target="tpu_custom_call" | custom-call | flops 4294967296 | bytes 8388608 | tf_op jit(solution)/shard_map/pallas_call | solution.py:239
  229.5 4.3 collective-permute-start.41
  239.6 3.0 collective-permute-start.45
  256.5 4.4 collective-permute-start.51
  262.4 5.8 %collective-permute-start.49 = (bf16[128,1024]{1,0:T(8,128)(2,1)S(1)}, bf16[128,1024]{1,0:T(8,128)(2,1)S(1)}, u32[]{:S(2)}, u32[]{:S(2)}) collective-permute-start(bf16[128,1024]{1,0:T(8,128)(2,1)S(1)} %convolution_convert_fusion.14), channel_id=1, source_target_pairs={{0,2},{1,3},{2,0},{3,1},{4,6},{5,7},{6,4},{7,5},{8,10},{9,11},{10,... | collective-permute-start | bytes 786440 | tf_op jit(solution)/shard_map/ppermute | solution.py:25
  269.1 3.4 collective-permute-done.49
  278.8 2.7 collective-permute-done.53
  294.7 5.1 maximum_maximum_fusion
  306.1 3.3 collective-permute-start.56
  309.8 3.0 collective-permute-start.54
  313.6 3.9 collective-permute-done.56
  318.6 6.5 %collective-permute-done.54 = bf16[128,1024]{1,0:T(8,128)(2,1)S(1)} collective-permute-done((bf16[128,1024]{1,0:T(8,128)(2,1)S(1)}, bf16[128,1024]{1,0:T(8,128)(2,1)S(1)}, u32[]{:S(2)}, u32[]{:S(2)}) %collective-permute-start.54) | collective-permute-done | bytes 262176 | tf_op jit(solution)/shard_map/ppermute | solution.py:25
  330.5 46.2 %reduce-scatter.3.cloned.1.call-done = bf16[208,1024]{1,0:T(8,128)(2,1)} async-done(((bf16[1664,1024]{1,0:T(8,128)(2,1)}), bf16[208,1024]{1,0:T(8,128)(2,1)}) %reduce-scatter.3.cloned.1.call-update) | async-done | bytes 426000 | tf_op jit(solution)/shard_map/reduce_scatter | solution.py:425
  384.1 6.8 %shard_map.147 = (bf16[512,768]{1,0:T(8,128)(2,1)S(1)}, bf16[384,1024]{1,0:T(8,128)(2,1)S(1)}, bf16[128,1024]{1,0:T(8,128)(2,1)}) custom-call(bf16[384,1024]{1,0:T(8,128)(2,1)S(1)} %pad_maximum_fusion.12.near, bf16[128,1024]{1,0:T(8,128)(2,1)S(1)} %copy-done.21, bf16[1024,768]{1,0:T(8,128)(2,1)S(1)} %copy-done.1, bf16[256,1024]{1,0:T(8,128)(2,1)S(1)} %copy-done.3, ...), custom_call_target="tpu_custom_call" | custom-call | flops 4294967296 | bytes 8388608 | tf_op jit(solution)/shard_map/pallas_call | solution.py:239
  403.8 3.5 collective-permute-done.65
  413.0 3.9 all-to-all-start
  419.2 10.6 %all-to-all-done = bf16[8,272,256]{2,1,0:T(8,128)(2,1)S(1)} async-done(((bf16[8,272,256]{2,1,0:T(8,128)(2,1)}), bf16[8,272,256]{2,1,0:T(8,128)(2,1)S(1)}, u32[]{:S(2)}, u32[]{:S(2)}) %all-to-all-start) | async-done | bytes 1114144 | tf_op jit(solution)/shard_map/all_to_all | solution.py:429
  430.2 3.1 collective-permute-start.68
  433.3 7.8 %collective-permute-done.68 = bf16[196,1024]{1,0:T(8,128)(2,1)S(1)} collective-permute-done((bf16[196,1024]{1,0:T(8,128)(2,1)S(1)}, bf16[196,1024]{1,0:T(8,128)(2,1)S(1)}, u32[]{:S(2)}, u32[]{:S(2)}) %collective-permute-start.68) | collective-permute-done | bytes 401440 | tf_op jit(solution)/shard_map/ppermute | solution.py:33
  441.8 43.2 %all_to_all.18 = bf16[8,208,1024]{2,1,0:T(8,128)(2,1)S(1)} all-to-all(bf16[8,208,1024]{2,1,0:T(8,128)(2,1)S(1)} %broadcast_in_dim.116), channel_id=1, replica_groups=mesh['section'=2,'zlo'=2,'x'=4,'core'=2,'tensor'=4] {'zlo','x'}, dimensions={0} | all-to-all | bytes 6815744 | tf_op jit(solution)/shard_map/all_to_all | solution.py:436
  485.0 3.0 collective-permute-start.57
  487.9 7.6 %collective-permute-done.57 = bf16[128,1024]{1,0:T(8,128)(2,1)} collective-permute-done((bf16[128,1024]{1,0:T(8,128)(2,1)}, bf16[128,1024]{1,0:T(8,128)(2,1)}, u32[]{:S(2)}, u32[]{:S(2)}) %collective-permute-start.57) | collective-permute-done | bytes 262176 | tf_op jit(solution)/shard_map/ppermute | solution.py:33
  495.5 3.0 collective-permute-start.69
  512.2 4.6 collective-permute-start.71
  519.5 2.8 convert_bitcast_fusion
  (557 shorter events, 211.9 us)
Async XLA Ops:
  7.2 320.9 %reduce-scatter.5.cloned.1.call-start = ((), (), s32[]{:S(2)}) async-start(), calls=%async_computation.5 | async-start | bytes 2359296 | tf_op jit(solution)/shard_map/reduce_scatter | solution.py:425
  8.9 20.6 %collective-permute-start.1 = (bf16[128,1024]{1,0:T(8,128)(2,1)S(1)}, bf16[128,1024]{1,0:T(8,128)(2,1)S(1)}, u32[]{:S(2)}, u32[]{:S(2)}) collective-permute-start(bf16[128,1024]{1,0:T(8,128)(2,1)S(1)} %get-tuple-element.215), channel_id=1, source_target_pairs={{0,1},{1,2},{2,3},{3,0},{4,5},{5,6},{6,7},{7,4},{8,9},{9,10},{10,1... | collective-permute-start | bytes 786440 | tf_op jit(solution)/shard_map/ppermute | solution.py:25
  10.5 19.5 %collective-permute-start = (bf16[128,1024]{1,0:T(8,128)(2,1)S(1)}, bf16[128,1024]{1,0:T(8,128)(2,1)}, u32[]{:S(2)}, u32[]{:S(2)}) collective-permute-start(bf16[128,1024]{1,0:T(8,128)(2,1)S(1)} %get-tuple-element.215), channel_id=1, source_target_pairs={{0,3},{1,0},{2,1},{3,2},{4,7},{5,4},{6,5},{7,6},{8,11},{9,8},{10,9... | collective-permute-start | bytes 786440 | tf_op jit(solution)/shard_map/ppermute | solution.py:25
  11.0 21.6 %collective-permute-start.2 = (bf16[128,1024]{1,0:T(8,128)(2,1)S(1)}, bf16[128,1024]{1,0:T(8,128)(2,1)S(1)}, u32[]{:S(2)}, u32[]{:S(2)}) collective-permute-start(bf16[128,1024]{1,0:T(8,128)(2,1)S(1)} %get-tuple-element.215), channel_id=1, source_target_pairs={{0,2},{1,3},{2,0},{3,1},{4,6},{5,7},{6,4},{7,5},{8,10},{9,11},{10,... | collective-permute-start | bytes 786440 | tf_op jit(solution)/shard_map/ppermute | solution.py:25
  14.2 13.2 %collective-permute-start.4 = (bf16[128,1024]{1,0:T(8,128)(2,1)S(1)}, bf16[128,1024]{1,0:T(8,128)(2,1)}, u32[]{:S(2)}, u32[]{:S(2)}) collective-permute-start(bf16[128,1024]{1,0:T(8,128)(2,1)S(1)} %constant_dynamic-slice_fusion.3), channel_id=1, source_target_pairs={{0,96},{32,64},{64,32},{96,0},{1,97},{33,65},{65,33},{97,1},{2,98}... | collective-permute-start | bytes 786440 | tf_op jit(solution)/shard_map/ppermute | solution.py:37
  24.2 21.9 %collective-permute-start.3 = (bf16[1536,256]{1,0:T(8,128)(2,1)S(1)}, bf16[1536,256]{1,0:T(8,128)(2,1)}, u32[]{:S(2)}, u32[]{:S(2)}) collective-permute-start(bf16[1536,256]{1,0:T(8,128)(2,1)S(1)} %constant_dynamic-slice_fusion.4), channel_id=1, source_target_pairs={{0,96},{32,64},{64,32},{96,0},{1,97},{33,65},{65,33},{97,1},{2,98}... | collective-permute-start | bytes 2359304 | tf_op jit(solution)/shard_map/ppermute | solution.py:37
  29.5 38.6 %collective-permute-start.13 = (bf16[328,1024]{1,0:T(8,128)(2,1)}, bf16[328,1024]{1,0:T(8,128)(2,1)}, u32[]{:S(2)}, u32[]{:S(2)}) collective-permute-start(bf16[328,1024]{1,0:T(8,128)(2,1)} %constant_dynamic-slice_fusion.2), channel_id=1, source_target_pairs={{0,96},{32,64},{64,32},{96,0},{1,97},{33,65},{65,33},{97,1},{2,98}... | collective-permute-start | bytes 2015240 | tf_op jit(solution)/shard_map/ppermute | solution.py:37
  63.5 20.6 %collective-permute-start.10 = (bf16[128,1024]{1,0:T(8,128)(2,1)S(1)}, bf16[128,1024]{1,0:T(8,128)(2,1)S(1)}, u32[]{:S(2)}, u32[]{:S(2)}) collective-permute-start(bf16[128,1024]{1,0:T(8,128)(2,1)S(1)} %get-tuple-element.299), channel_id=1, source_target_pairs={{0,3},{1,0},{2,1},{3,2},{4,7},{5,4},{6,5},{7,6},{8,11},{9,8},{10,9... | collective-permute-start | bytes 786440 | tf_op jit(solution)/shard_map/ppermute | solution.py:25
  65.0 19.2 %collective-permute-start.9 = (bf16[128,1024]{1,0:T(8,128)(2,1)S(1)}, bf16[128,1024]{1,0:T(8,128)(2,1)S(1)}, u32[]{:S(2)}, u32[]{:S(2)}) collective-permute-start(bf16[128,1024]{1,0:T(8,128)(2,1)S(1)} %get-tuple-element.298), channel_id=1, source_target_pairs={{0,1},{1,2},{2,3},{3,0},{4,5},{5,6},{6,7},{7,4},{8,9},{9,10},{10,1... | collective-permute-start | bytes 786440 | tf_op jit(solution)/shard_map/ppermute | solution.py:25
  65.6 18.5 %collective-permute-start.8 = (bf16[128,1024]{1,0:T(8,128)(2,1)S(1)}, bf16[128,1024]{1,0:T(8,128)(2,1)S(1)}, u32[]{:S(2)}, u32[]{:S(2)}) collective-permute-start(bf16[128,1024]{1,0:T(8,128)(2,1)S(1)} %get-tuple-element.97), channel_id=1, source_target_pairs={{0,2},{1,3},{2,0},{3,1},{4,6},{5,7},{6,4},{7,5},{8,10},{9,11},{10,... | collective-permute-start | bytes 786440 | tf_op jit(solution)/shard_map/ppermute | solution.py:25
  68.1 18.9 %collective-permute-start.15 = (bf16[328,1024]{1,0:T(8,128)(2,1)S(1)}, bf16[328,1024]{1,0:T(8,128)(2,1)S(1)}, u32[]{:S(2)}, u32[]{:S(2)}) collective-permute-start(bf16[328,1024]{1,0:T(8,128)(2,1)S(1)} %constant_dynamic-slice_fusion.1), channel_id=1, source_target_pairs={{0,96},{32,64},{64,32},{96,0},{1,97},{33,65},{65,33},{97,1},{2,98}... | collective-permute-start | bytes 2015240 | tf_op jit(solution)/shard_map/ppermute | solution.py:37
  71.4 24.4 %collective-permute-start.14 = (bf16[328,1024]{1,0:T(8,128)(2,1)}, bf16[328,1024]{1,0:T(8,128)(2,1)S(1)}, u32[]{:S(2)}, u32[]{:S(2)}) collective-permute-start(bf16[328,1024]{1,0:T(8,128)(2,1)} %collective-permute-done.13), channel_id=1, source_target_pairs={{0,4},{4,0},{1,5},{5,1},{2,6},{6,2},{3,7},{7,3},{8,12},{12,8},{9,1... | collective-permute-start | bytes 2015240 | tf_op jit(solution)/shard_map/ppermute | solution.py:29
  87.1 18.2 %collective-permute-start.17 = (bf16[328,1024]{1,0:T(8,128)(2,1)S(1)}, bf16[328,1024]{1,0:T(8,128)(2,1)S(1)}, u32[]{:S(2)}, u32[]{:S(2)}) collective-permute-start(bf16[328,1024]{1,0:T(8,128)(2,1)S(1)} %constant_dynamic-slice_fusion), channel_id=1, source_target_pairs={{0,96},{32,64},{64,32},{96,0},{1,97},{33,65},{65,33},{97,1},{2,98}... | collective-permute-start | bytes 2015240 | tf_op jit(solution)/shard_map/ppermute | solution.py:37
  89.4 15.9 %collective-permute-start.16 = (bf16[328,1024]{1,0:T(8,128)(2,1)S(1)}, bf16[328,1024]{1,0:T(8,128)(2,1)S(1)}, u32[]{:S(2)}, u32[]{:S(2)}) collective-permute-start(bf16[328,1024]{1,0:T(8,128)(2,1)S(1)} %collective-permute-done.15), channel_id=1, source_target_pairs={{0,4},{4,0},{1,5},{5,1},{2,6},{6,2},{3,7},{7,3},{8,12},{12,8},{9,1... | collective-permute-start | bytes 2015240 | tf_op jit(solution)/shard_map/ppermute | solution.py:29
  120.3 9.7 %collective-permute-start.20 = (bf16[128,1024]{1,0:T(8,128)(2,1)S(1)}, bf16[128,1024]{1,0:T(8,128)(2,1)S(1)}, u32[]{:S(2)}, u32[]{:S(2)}) collective-permute-start(bf16[128,1024]{1,0:T(8,128)(2,1)S(1)} %convolution_convert_fusion.13), channel_id=1, source_target_pairs={{0,2},{1,3},{2,0},{3,1},{4,6},{5,7},{6,4},{7,5},{8,10},{9,11},{10,... | collective-permute-start | bytes 786440 | tf_op jit(solution)/shard_map/ppermute | solution.py:25
  130.8 10.3 %collective-permute-start.24 = (bf16[128,1024]{1,0:T(8,128)(2,1)S(1)}, bf16[128,1024]{1,0:T(8,128)(2,1)}, u32[]{:S(2)}, u32[]{:S(2)}) collective-permute-start(bf16[128,1024]{1,0:T(8,128)(2,1)S(1)} %fusion.47), channel_id=1, source_target_pairs={{0,1},{1,2},{2,3},{3,0},{4,5},{5,6},{6,7},{7,4},{8,9},{9,10},{10,1... | collective-permute-start | bytes 786440 | tf_op jit(solution)/shard_map/ppermute | solution.py:25
  135.3 11.8 %collective-permute-start.25 = (bf16[128,1024]{1,0:T(8,128)(2,1)S(1)}, bf16[128,1024]{1,0:T(8,128)(2,1)S(1)}, u32[]{:S(2)}, u32[]{:S(2)}) collective-permute-start(bf16[128,1024]{1,0:T(8,128)(2,1)S(1)} %fusion.47), channel_id=1, source_target_pairs={{0,2},{1,3},{2,0},{3,1},{4,6},{5,7},{6,4},{7,5},{8,10},{9,11},{10,... | collective-permute-start | bytes 786440 | tf_op jit(solution)/shard_map/ppermute | solution.py:25
  152.1 12.8 %collective-permute-start.28 = (bf16[128,1024]{1,0:T(8,128)(2,1)S(1)}, bf16[128,1024]{1,0:T(8,128)(2,1)S(1)}, u32[]{:S(2)}, u32[]{:S(2)}) collective-permute-start(bf16[128,1024]{1,0:T(8,128)(2,1)S(1)} %get-tuple-element.295), channel_id=1, source_target_pairs={{0,3},{1,0},{2,1},{3,2},{4,7},{5,4},{6,5},{7,6},{8,11},{9,8},{10,9... | collective-permute-start | bytes 786440 | tf_op jit(solution)/shard_map/ppermute | solution.py:25
  154.6 17.5 %collective-permute-start.27 = (bf16[128,1024]{1,0:T(8,128)(2,1)S(1)}, bf16[128,1024]{1,0:T(8,128)(2,1)S(1)}, u32[]{:S(2)}, u32[]{:S(2)}) collective-permute-start(bf16[128,1024]{1,0:T(8,128)(2,1)S(1)} %get-tuple-element.294), channel_id=1, source_target_pairs={{0,1},{1,2},{2,3},{3,0},{4,5},{5,6},{6,7},{7,4},{8,9},{9,10},{10,1... | collective-permute-start | bytes 786440 | tf_op jit(solution)/shard_map/ppermute | solution.py:25
  154.6 17.5 %collective-permute-start.26 = (bf16[128,1024]{1,0:T(8,128)(2,1)S(1)}, bf16[128,1024]{1,0:T(8,128)(2,1)S(1)}, u32[]{:S(2)}, u32[]{:S(2)}) collective-permute-start(bf16[128,1024]{1,0:T(8,128)(2,1)S(1)} %get-tuple-element.106), channel_id=1, source_target_pairs={{0,2},{1,3},{2,0},{3,1},{4,6},{5,7},{6,4},{7,5},{8,10},{9,11},{10,... | collective-permute-start | bytes 786440 | tf_op jit(solution)/shard_map/ppermute | solution.py:25
  159.6 16.4 %collective-permute-start.33 = (bf16[128,1024]{1,0:T(8,128)(2,1)S(1)}, bf16[128,1024]{1,0:T(8,128)(2,1)S(1)}, u32[]{:S(2)}, u32[]{:S(2)}) collective-permute-start(bf16[128,1024]{1,0:T(8,128)(2,1)S(1)} %select_bitcast_fusion.9), channel_id=1, source_target_pairs={{0,1},{1,2},{2,3},{3,0},{4,5},{5,6},{6,7},{7,4},{8,9},{9,10},{10,1... | collective-permute-start | bytes 786440 | tf_op jit(solution)/shard_map/ppermute | solution.py:25
  159.7 16.3 %collective-permute-start.32 = (bf16[128,1024]{1,0:T(8,128)(2,1)S(1)}, bf16[128,1024]{1,0:T(8,128)(2,1)S(1)}, u32[]{:S(2)}, u32[]{:S(2)}) collective-permute-start(bf16[128,1024]{1,0:T(8,128)(2,1)S(1)} %select_bitcast_fusion.9), channel_id=1, source_target_pairs={{0,3},{1,0},{2,1},{3,2},{4,7},{5,4},{6,5},{7,6},{8,11},{9,8},{10,9... | collective-permute-start | bytes 786440 | tf_op jit(solution)/shard_map/ppermute | solution.py:25
  164.9 15.7 %collective-permute-start.34 = (bf16[128,1024]{1,0:T(8,128)(2,1)S(1)}, bf16[128,1024]{1,0:T(8,128)(2,1)S(1)}, u32[]{:S(2)}, u32[]{:S(2)}) collective-permute-start(bf16[128,1024]{1,0:T(8,128)(2,1)S(1)} %select_bitcast_fusion.9), channel_id=1, source_target_pairs={{0,2},{1,3},{2,0},{3,1},{4,6},{5,7},{6,4},{7,5},{8,10},{9,11},{10,... | collective-permute-start | bytes 786440 | tf_op jit(solution)/shard_map/ppermute | solution.py:25
  172.9 12.3 %collective-permute-start.30 = (bf16[128,1024]{1,0:T(8,128)(2,1)S(1)}, bf16[128,1024]{1,0:T(8,128)(2,1)S(1)}, u32[]{:S(2)}, u32[]{:S(2)}) collective-permute-start(bf16[128,1024]{1,0:T(8,128)(2,1)S(1)} %multiply_convert_fusion.4), channel_id=1, source_target_pairs={{0,1},{1,2},{2,3},{3,0},{4,5},{5,6},{6,7},{7,4},{8,9},{9,10},{10,1... | collective-permute-start | bytes 786440 | tf_op jit(solution)/shard_map/ppermute | solution.py:25
  172.9 12.2 %collective-permute-start.29 = (bf16[128,1024]{1,0:T(8,128)(2,1)S(1)}, bf16[128,1024]{1,0:T(8,128)(2,1)S(1)}, u32[]{:S(2)}, u32[]{:S(2)}) collective-permute-start(bf16[128,1024]{1,0:T(8,128)(2,1)S(1)} %multiply_convert_fusion.4), channel_id=1, source_target_pairs={{0,3},{1,0},{2,1},{3,2},{4,7},{5,4},{6,5},{7,6},{8,11},{9,8},{10,9... | collective-permute-start | bytes 786440 | tf_op jit(solution)/shard_map/ppermute | solution.py:25
  180.6 9.5 %collective-permute-start.31 = (bf16[128,1024]{1,0:T(8,128)(2,1)S(1)}, bf16[128,1024]{1,0:T(8,128)(2,1)S(1)}, u32[]{:S(2)}, u32[]{:S(2)}) collective-permute-start(bf16[128,1024]{1,0:T(8,128)(2,1)S(1)} %multiply_convert_fusion.4), channel_id=1, source_target_pairs={{0,2},{1,3},{2,0},{3,1},{4,6},{5,7},{6,4},{7,5},{8,10},{9,11},{10,... | collective-permute-start | bytes 786440 | tf_op jit(solution)/shard_map/ppermute | solution.py:25
  192.4 9.8 %collective-permute-start.37 = (bf16[128,1024]{1,0:T(8,128)(2,1)S(1)}, bf16[128,1024]{1,0:T(8,128)(2,1)S(1)}, u32[]{:S(2)}, u32[]{:S(2)}) collective-permute-start(bf16[128,1024]{1,0:T(8,128)(2,1)S(1)} %get-tuple-element.293), channel_id=1, source_target_pairs={{0,3},{1,0},{2,1},{3,2},{4,7},{5,4},{6,5},{7,6},{8,11},{9,8},{10,9... | collective-permute-start | bytes 786440 | tf_op jit(solution)/shard_map/ppermute | solution.py:25
  206.5 9.5 %collective-permute-start.39 = (bf16[128,1024]{1,0:T(8,128)(2,1)S(1)}, bf16[128,1024]{1,0:T(8,128)(2,1)S(1)}, u32[]{:S(2)}, u32[]{:S(2)}) collective-permute-start(bf16[128,1024]{1,0:T(8,128)(2,1)S(1)} %get-tuple-element.222), channel_id=1, source_target_pairs={{0,1},{1,2},{2,3},{3,0},{4,5},{5,6},{6,7},{7,4},{8,9},{9,10},{10,1... | collective-permute-start | bytes 786440 | tf_op jit(solution)/shard_map/ppermute | solution.py:25
  209.8 10.8 %collective-permute-start.40 = (bf16[128,1024]{1,0:T(8,128)(2,1)S(1)}, bf16[128,1024]{1,0:T(8,128)(2,1)S(1)}, u32[]{:S(2)}, u32[]{:S(2)}) collective-permute-start(bf16[128,1024]{1,0:T(8,128)(2,1)S(1)} %get-tuple-element.222), channel_id=1, source_target_pairs={{0,2},{1,3},{2,0},{3,1},{4,6},{5,7},{6,4},{7,5},{8,10},{9,11},{10,... | collective-permute-start | bytes 786440 | tf_op jit(solution)/shard_map/ppermute | solution.py:25
  212.9 33.1 %collective-permute-start.48 = (bf16[328,1024]{1,0:T(8,128)(2,1)S(1)}, bf16[328,1024]{1,0:T(8,128)(2,1)S(1)}, u32[]{:S(2)}, u32[]{:S(2)}) collective-permute-start(bf16[328,1024]{1,0:T(8,128)(2,1)S(1)} %convolution_convert_fusion.7), channel_id=1, source_target_pairs={{0,4},{4,0},{1,5},{5,1},{2,6},{6,2},{3,7},{7,3},{8,12},{12,8},{9,1... | collective-permute-start | bytes 2015240 | tf_op jit(solution)/shard_map/ppermute | solution.py:29
  214.2 34.8 %collective-permute-start.47 = (bf16[656,1024]{1,0:T(8,128)(2,1)S(1)}, bf16[656,1024]{1,0:T(8,128)(2,1)S(1)}, u32[]{:S(2)}, u32[]{:S(2)}) collective-permute-start(bf16[656,1024]{1,0:T(8,128)(2,1)S(1)} %convolution_convert_fusion.1), channel_id=1, source_target_pairs={{0,4},{4,0},{1,5},{5,1},{2,6},{6,2},{3,7},{7,3},{8,12},{12,8},{9,1... | collective-permute-start | bytes 4030472 | tf_op jit(solution)/shard_map/ppermute | solution.py:29
  256.5 11.7 %collective-permute-start.51 = (bf16[128,1024]{1,0:T(8,128)(2,1)S(1)}, bf16[128,1024]{1,0:T(8,128)(2,1)S(1)}, u32[]{:S(2)}, u32[]{:S(2)}) collective-permute-start(bf16[128,1024]{1,0:T(8,128)(2,1)S(1)} %get-tuple-element.289), channel_id=1, source_target_pairs={{0,3},{1,0},{2,1},{3,2},{4,7},{5,4},{6,5},{7,6},{8,11},{9,8},{10,9... | collective-permute-start | bytes 786440 | tf_op jit(solution)/shard_map/ppermute | solution.py:25
  262.4 10.2 %collective-permute-start.49 = (bf16[128,1024]{1,0:T(8,128)(2,1)S(1)}, bf16[128,1024]{1,0:T(8,128)(2,1)S(1)}, u32[]{:S(2)}, u32[]{:S(2)}) collective-permute-start(bf16[128,1024]{1,0:T(8,128)(2,1)S(1)} %convolution_convert_fusion.14), channel_id=1, source_target_pairs={{0,2},{1,3},{2,0},{3,1},{4,6},{5,7},{6,4},{7,5},{8,10},{9,11},{10,... | collective-permute-start | bytes 786440 | tf_op jit(solution)/shard_map/ppermute | solution.py:25
  284.6 92.1 %reduce-scatter.3.cloned.1.call-start = ((), (), s32[]{:S(2)}) async-start(), calls=%async_computation.4 | async-start | bytes 3833856 | tf_op jit(solution)/shard_map/reduce_scatter | solution.py:425
  300.8 12.0 %collective-permute-start.59 = (bf16[128,1024]{1,0:T(8,128)(2,1)S(1)}, bf16[128,1024]{1,0:T(8,128)(2,1)S(1)}, u32[]{:S(2)}, u32[]{:S(2)}) collective-permute-start(bf16[128,1024]{1,0:T(8,128)(2,1)S(1)} %copy-done.87), channel_id=1, source_target_pairs={{0,1},{1,2},{2,3},{3,0},{4,5},{5,6},{6,7},{7,4},{8,9},{9,10},{10,1... | collective-permute-start | bytes 786440 | tf_op jit(solution)/shard_map/ppermute | solution.py:25
  301.8 11.7 %collective-permute-start.58 = (bf16[128,1024]{1,0:T(8,128)(2,1)S(1)}, bf16[128,1024]{1,0:T(8,128)(2,1)S(1)}, u32[]{:S(2)}, u32[]{:S(2)}) collective-permute-start(bf16[128,1024]{1,0:T(8,128)(2,1)S(1)} %copy-done.87), channel_id=1, source_target_pairs={{0,3},{1,0},{2,1},{3,2},{4,7},{5,4},{6,5},{7,6},{8,11},{9,8},{10,9... | collective-permute-start | bytes 786440 | tf_op jit(solution)/shard_map/ppermute | solution.py:25
  306.1 11.4 %collective-permute-start.56 = (bf16[128,1024]{1,0:T(8,128)(2,1)S(1)}, bf16[128,1024]{1,0:T(8,128)(2,1)S(1)}, u32[]{:S(2)}, u32[]{:S(2)}) collective-permute-start(bf16[128,1024]{1,0:T(8,128)(2,1)S(1)} %get-tuple-element.287), channel_id=1, source_target_pairs={{0,3},{1,0},{2,1},{3,2},{4,7},{5,4},{6,5},{7,6},{8,11},{9,8},{10,9... | collective-permute-start | bytes 786440 | tf_op jit(solution)/shard_map/ppermute | solution.py:25
  309.8 15.3 %collective-permute-start.54 = (bf16[128,1024]{1,0:T(8,128)(2,1)S(1)}, bf16[128,1024]{1,0:T(8,128)(2,1)S(1)}, u32[]{:S(2)}, u32[]{:S(2)}) collective-permute-start(bf16[128,1024]{1,0:T(8,128)(2,1)S(1)} %convolution_convert_fusion.12), channel_id=1, source_target_pairs={{0,2},{1,3},{2,0},{3,1},{4,6},{5,7},{6,4},{7,5},{8,10},{9,11},{10,... | collective-permute-start | bytes 786440 | tf_op jit(solution)/shard_map/ppermute | solution.py:25
  312.8 17.1 %collective-permute-start.60 = (bf16[128,1024]{1,0:T(8,128)(2,1)S(1)}, bf16[128,1024]{1,0:T(8,128)(2,1)S(1)}, u32[]{:S(2)}, u32[]{:S(2)}) collective-permute-start(bf16[128,1024]{1,0:T(8,128)(2,1)S(1)} %copy-done.87), channel_id=1, source_target_pairs={{0,2},{1,3},{2,0},{3,1},{4,6},{5,7},{6,4},{7,5},{8,10},{9,11},{10,... | collective-permute-start | bytes 786440 | tf_op jit(solution)/shard_map/ppermute | solution.py:25
  392.5 16.1 %collective-permute-start.63 = (bf16[128,1024]{1,0:T(8,128)(2,1)}, bf16[128,1024]{1,0:T(8,128)(2,1)S(1)}, u32[]{:S(2)}, u32[]{:S(2)}) collective-permute-start(bf16[128,1024]{1,0:T(8,128)(2,1)} %get-tuple-element.165), channel_id=1, source_target_pairs={{0,2},{1,3},{2,0},{3,1},{4,6},{5,7},{6,4},{7,5},{8,10},{9,11},{10,... | collective-permute-start | bytes 786440 | tf_op jit(solution)/shard_map/ppermute | solution.py:25
  413.0 16.8 %all-to-all-start = ((bf16[8,272,256]{2,1,0:T(8,128)(2,1)}), bf16[8,272,256]{2,1,0:T(8,128)(2,1)S(1)}, u32[]{:S(2)}, u32[]{:S(2)}) async-start(bf16[8,272,256]{2,1,0:T(8,128)(2,1)} %bitcast.36), calls=%async_computation.2 | async-start | bytes 2228224 | tf_op jit(solution)/shard_map/all_to_all | solution.py:429
  430.2 10.9 %collective-permute-start.68 = (bf16[196,1024]{1,0:T(8,128)(2,1)S(1)}, bf16[196,1024]{1,0:T(8,128)(2,1)S(1)}, u32[]{:S(2)}, u32[]{:S(2)}) collective-permute-start(bf16[196,1024]{1,0:T(8,128)(2,1)S(1)} %broadcast_select_fusion.20), channel_id=1, source_target_pairs={{0,64},{64,0},{1,65},{65,1},{2,66},{66,2},{3,67},{67,3},{4,68},{68... | collective-permute-start | bytes 1204232 | tf_op jit(solution)/shard_map/ppermute | solution.py:33
  485.0 22.6 %collective-permute-start.70 = (bf16[1664,1024]{1,0:T(8,128)(2,1)S(1)}, bf16[1664,1024]{1,0:T(8,128)(2,1)}, u32[]{:S(2)}, u32[]{:S(2)}) collective-permute-start(bf16[1664,1024]{1,0:T(8,128)(2,1)S(1)} %bitcast.153), channel_id=1, source_target_pairs={{0,4},{4,0},{1,5},{5,1},{2,6},{6,2},{3,7},{7,3},{8,12},{12,8},{9,1... | collective-permute-start | bytes 10223624 | tf_op jit(solution)/shard_map/ppermute | solution.py:29
  485.0 10.5 %collective-permute-start.57 = (bf16[128,1024]{1,0:T(8,128)(2,1)}, bf16[128,1024]{1,0:T(8,128)(2,1)}, u32[]{:S(2)}, u32[]{:S(2)}) collective-permute-start(bf16[128,1024]{1,0:T(8,128)(2,1)} %get-tuple-element.216), channel_id=1, source_target_pairs={{0,64},{64,0},{1,65},{65,1},{2,66},{66,2},{3,67},{67,3},{4,68},{68... | collective-permute-start | bytes 786440 | tf_op jit(solution)/shard_map/ppermute | solution.py:33
  495.5 10.2 %collective-permute-start.69 = (bf16[128,1024]{1,0:T(8,128)(2,1)}, bf16[128,1024]{1,0:T(8,128)(2,1)}, u32[]{:S(2)}, u32[]{:S(2)}) collective-permute-start(bf16[128,1024]{1,0:T(8,128)(2,1)} %get-tuple-element.176), channel_id=1, source_target_pairs={{0,64},{64,0},{1,65},{65,1},{2,66},{66,2},{3,67},{67,3},{4,68},{68... | collective-permute-start | bytes 786440 | tf_op jit(solution)/shard_map/ppermute | solution.py:33
  510.2 17.1 %collective-permute-start.73 = (f32[8,256]{1,0:T(8,128)S(1)}, f32[8,256]{1,0:T(8,128)S(1)}, u32[]{:S(2)}, u32[]{:S(2)}) collective-permute-start(f32[8,256]{1,0:T(8,128)S(1)} %convert_add_fusion.5), channel_id=1, source_target_pairs={{0,3},{1,0},{2,1},{3,2},{4,7},{5,4},{6,5},{7,6},{8,11},{9,8},{10,9... | collective-permute-start | bytes 24584 | tf_op jit(solution)/shard_map/ppermute | solution.py:25
  510.2 17.1 %collective-permute-start.72 = (f32[8,256]{1,0:T(8,128)S(1)}, f32[8,256]{1,0:T(8,128)S(1)}, u32[]{:S(2)}, u32[]{:S(2)}) collective-permute-start(f32[8,256]{1,0:T(8,128)S(1)} %convert_add_fusion.5), channel_id=1, source_target_pairs={{0,1},{1,2},{2,3},{3,0},{4,5},{5,6},{6,7},{7,4},{8,9},{9,10},{10,1... | collective-permute-start | bytes 24584 | tf_op jit(solution)/shard_map/ppermute | solution.py:25
  512.2 15.1 %collective-permute-start.71 = (f32[8,256]{1,0:T(8,128)S(1)}, f32[8,256]{1,0:T(8,128)S(1)}, u32[]{:S(2)}, u32[]{:S(2)}) collective-permute-start(f32[8,256]{1,0:T(8,128)S(1)} %convert_add_fusion.5), channel_id=1, source_target_pairs={{0,2},{1,3},{2,0},{3,1},{4,6},{5,7},{6,4},{7,5},{8,10},{9,11},{10,... | collective-permute-start | bytes 24584 | tf_op jit(solution)/shard_map/ppermute | solution.py:25
  (133 other events, 1426.0 us)
Sparse Core Ops, SparseCore 0:
  284.8 43.2 reduce-scatter.4
  331.0 45.6 reduce-scatter.2
where the time goes:
time: 545 us; the launch traced here: 535 us
  waiting for transfers between devices  170 us (31%)
  starting transfers between devices  141 us (26%)
  other arithmetic  64.9 us (12%)
  local copies, waits for them, and re-layouts  46 us (8%)
  blocking collectives  43.2 us (8%)
  matrix products  31 us (6%)
  Pallas kernels  23.1 us (4%)
  between operations  16.3 us (3%)
    ppermute x51, starting transfers between devices, around(): lax.ppermute(block, axis, [(i, (i + distance) % count) for i in range(cou...  98.9 us
    ppermute x51, waiting for transfers between devices, around(): lax.ppermute(block, axis, [(i, (i + distance) % count) for i in range(cou...  76.2 us
    reduce_scatter x2, waiting for transfers between devices, reduce_part(): lax.psum_scatter(grads, ('zlo', 'x'), scatter_dimension=0, tiled=True)  48.1 us
    all_to_all x1, blocking collectives, spread_part(): return lax.all_to_all(copies, ('zlo', 'x'), 0, 0, tiled=True)  43.2 us
    pallas_call x4, Pallas kernels, whole_call(): pl.pallas_call(kernel, out_shape=[jax.ShapeDtypeStruct(*shape) for shape...  23.1 us
    unnamed x224, local copies, waits for them, and re-layouts  20.5 us
    concatenate x15, other arithmetic, joined(): return jnp.concatenate(parts, axis=axis)  16.1 us
    ppermute x6, waiting for transfers between devices, swap_layer(): lax.ppermute(block, ('section', 'zlo'), [(0, 3), (1, 2), (2, 1), (3, 0)])  15.6 us
  transfers between devices with their start and end apart: 77, of which 42 were waited for; matrix products, arithmetic and copies ran while one was open for 19% of the time, Pallas kernels for 2%

commit v1 on v0

--- a/solution.py
+++ b/solution.py
@@ -528,64 +528,62 @@
         in1.astype(f32), kept0, gains0[1], layer0, ffn_pack1
     )
     model_width = w_qkv.shape[1]
-    attn_pack1 = attn_grads1(in1, [gain_first1, gain_mid1])
-    attn_width = attn_pack1.shape[1]
-    pieces = [pack.reshape(8, -1, model_width) for pack in (ffn_pack1, attn_pack1)]
-    ffn_rows, attn_rows = pieces[0].shape[1], pieces[1].shape[1]
-    part_rows = ffn_rows + attn_rows
-    blank = jnp.zeros((8, -part_rows % 16, model_width), bf16)
-    part1 = reduce_part(joined(pieces + [blank], 1).reshape(-1, model_width))
+    ffn1 = reduce_part(ffn_pack1)
     ffn_pack0 = ffn_grads0(mid0)[1](())
     in0, attn_grads0, unused, gain_before, unused = backward_attn(
-        mid0, kept0, gains0[0], layer0, allowed0, tables0, (ffn_pack0, part1), lambda gate: ()
+        mid0, kept0, gains0[0], layer0, allowed0, tables0, ffn_pack0, lambda gate: ()
     )
     in0 = in0.astype(bf16)
     ffn0 = reduce_part(ffn_pack0)
+    attn_pack1 = attn_grads1(in1, [gain_first1, gain_mid1])
     attn_pack0 = attn_grads0((), [gain_before(), gain_mid0])
     out1_terms = out1_of(ffn_pack0)
     out1 = (kept1["resid_mid"] + scatter_parts(*out1_terms)).astype(bf16)
-    attn0 = reduce_part_now(attn_pack0)
-    part0 = joined([ffn0, attn0.reshape(-1, model_width)])
-    own_part, sent_part = pick_sections(is_first, part0, part1[:part_rows])
+    attn_width = attn_pack0.shape[1]
+    packs = [pack.reshape(8, -1, attn_width) for pack in (attn_pack0, attn_pack1)]
+    attn_rows = packs[0].shape[1]
+    attn_both = reduce_part_now(joined(packs, 1).reshape(-1, attn_width))
+    part0 = joined([ffn0, attn_both[:attn_rows].reshape(-1, model_width)])
+    part1 = joined([ffn1, attn_both[attn_rows:].reshape(-1, model_width)])
+    own_part, sent_part = pick_sections(is_first, part0, part1)
     sent_part = after_all(sent_part, in0, out1)
     part = (own_part.astype(f32) + swap_section(sent_part).astype(f32)).astype(bf16)
-    part = joined([part, jnp.zeros((-part_rows % 16, model_width), bf16)])
-    half = spread_part(part)
-    halves = [both.reshape(8, -1, model_width) for both in (half, swap_core(half))]
+    ffn_rows = ffn0.shape[0]
+    ffn_half = spread_part(part[:ffn_rows])
+    attn_part = after_all(part[ffn_rows:].reshape(-1, attn_width), ffn_half)
+    attn_half = spread_part(attn_part)
     is_core0 = lax.axis_index("core") == 0
 
-    def of_core(core, first_row, rows, width, start, count):
-        mine, other = (
-            both[:, first_row : first_row + rows].reshape(-1, width)[start : start + count]
-            for both in halves
-        )
+    def of_core(core, halves, start, count):
+        mine, other = (both[start : start + count] for both in halves)
         return jnp.where(is_core0 == (core == 0), mine, other).astype(f32)
 
-    def of_ffn(core, start, count):
-        return of_core(core, 0, ffn_rows, model_width, start, count)
-
-    def of_attn(core, start, count):
-        return of_core(core, ffn_rows, attn_rows, attn_width, start, count)
-
+    ffn_halves = (ffn_half, swap_core(ffn_half))
     down_rows = w_down.shape[1] // 2
-    grad_up = jnp.stack([of_ffn(core, 0, hidden_width) for core in range(2)])
-    grad_down = joined([of_ffn(core, hidden_width, down_rows) for core in range(2)])
-    gain_rows = sum(of_attn(core, 2 * model_width, 8) for core in range(2))
+    grad_up = jnp.stack([of_core(core, ffn_halves, 0, hidden_width) for core in range(2)])
+    grad_down = joined(
+        [of_core(core, ffn_halves, hidden_width, down_rows) for core in range(2)]
+    )
+    attn_half, grad_up, grad_down = lax.optimization_barrier((attn_half, grad_up, grad_down))
+    attn_halves = (attn_half, swap_core(attn_half))
+    gain_rows = sum(of_core(core, attn_halves, 2 * model_width, 8) for core in range(2))
     gain_total = sum_tensor(gain_rows).reshape(2, -1)
     grad_qkv = jnp.stack(
         [
-            of_attn(0, 0, model_width),
-            of_attn(0, model_width, model_width),
-            of_attn(1, 0, model_width),
+            of_core(0, attn_halves, 0, model_width),
+            of_core(0, attn_halves, model_width, model_width),
+            of_core(1, attn_halves, 0, model_width),
         ]
     )
-    grad_out = of_attn(1, model_width, model_width).T
-    got_out = swap_section(jnp.where(is_first, out1, out0))
-    got_out, got_in_sent = after_all((got_out, jnp.where(is_first, in1, in0)), half)
+    grad_out = of_core(1, attn_halves, model_width, model_width).T
+
+    sent_out, sent_in = after_all(
+        (jnp.where(is_first, out1, out0), jnp.where(is_first, in1, in0)), ffn_half
+    )
+    got_out, got_in = swap_section(sent_out), swap_section(sent_in)
     section_out = jnp.stack(
         [jnp.where(is_first, out0, got_out), jnp.where(is_first, got_out, out1)]
     )
-    got_in = swap_section(got_in_sent)
     input_grads = jnp.stack(
         [jnp.where(is_first, in0, got_in), jnp.where(is_first, got_in, in1)]
     )

time: 545 us -> 529 us (0.971)
  matrix products: 31 us -> 50.2 us
  waiting for transfers between devices: 170 us -> 155 us
  blocking collectives: 43.2 us -> 29.7 us
  starting transfers between devices: 141 us -> 129 us
  other arithmetic: 64.9 us -> 70.8 us
    reduce_scatter x2, waiting for transfers between devices: 48.1 us -> 10.2 us  [reduce_part(): lax.psum_scatter(grads, ('zlo', 'x'), scatter_dimension=0, tiled=True)]
    dot_general x16, matrix products: 12.4 us -> 27.2 us  [contract_rows(): lax.dot_general(left_rows, right_rows, (((0,), (0,)), ((), ())), preferre...]
    all_to_all x1, blocking collectives: 43.2 us -> 29.7 us  [spread_part(): return lax.all_to_all(copies, ('zlo', 'x'), 0, 0, tiled=True)]
    ppermute x14 -> x15, starting transfers between devices: 15.5 us -> 2.81 us  [swap_core(): return lax.ppermute(block, 'core', [(0, 1), (1, 0)])]
    all_to_all x1, waiting for transfers between devices: 10.6 us -> 21.3 us  [reduce_part_now(): pieces = lax.all_to_all(grads, ('zlo', 'x'), 0, 0, tiled=True)]
    all_to_all x0 -> x1, waiting for transfers between devices: none -> 10 us  [spread_part(): return lax.all_to_all(copies, ('zlo', 'x'), 0, 0, tiled=True)]
    ppermute x6, waiting for transfers between devices: 15.6 us -> 23.3 us  [swap_layer(): lax.ppermute(block, ('section', 'zlo'), [(0, 3), (1, 2), (2, 1), (3, 0)])]
    slice x4 -> x5, local copies, waits for them, and re-layouts: 6.08 us -> 0.05 us  [the longest x1 0.02 us: local(): part0 = joined([ffn0, attn_both[:attn_rows].reshape(-1, model_width)])]
  transfers between devices with their start and end apart: 77 -> 79, of which waited for: 42 -> 31; matrix products, arithmetic and copies ran while one was open for 19% -> 26% of each run, Pallas kernels for 2% -> 4%
where the time goes in v1:
time: 529 us; the launch traced here: 519 us
  waiting for transfers between devices  155 us (29%)
  starting transfers between devices  129 us (24%)
  other arithmetic  70.8 us (13%)
  matrix products  50.2 us (9%)
  local copies, waits for them, and re-layouts  45.3 us (9%)
  blocking collectives  29.7 us (6%)
  Pallas kernels  23.3 us (4%)
  between operations  16.4 us (3%)
    ppermute x51, starting transfers between devices, around(): lax.ppermute(block, axis, [(i, (i + distance) % count) for i in range(cou...  97.2 us
    ppermute x51, waiting for transfers between devices, around(): lax.ppermute(block, axis, [(i, (i + distance) % count) for i in range(cou...  70.5 us
    all_to_all x1, blocking collectives, spread_part(): return lax.all_to_all(copies, ('zlo', 'x'), 0, 0, tiled=True)  29.7 us
    dot_general x16, matrix products, contract_rows(): lax.dot_general(left_rows, right_rows, (((0,), (0,)), ((), ())), preferre...  27.2 us
    ppermute x6, waiting for transfers between devices, swap_layer(): lax.ppermute(block, ('section', 'zlo'), [(0, 3), (1, 2), (2, 1), (3, 0)])  23.3 us
    pallas_call x4, Pallas kernels, whole_call(): pl.pallas_call(kernel, out_shape=[jax.ShapeDtypeStruct(*shape) for shape...  23.3 us
    unnamed x231, local copies, waits for them, and re-layouts  22.8 us
    all_to_all x1, waiting for transfers between devices, reduce_part_now(): pieces = lax.all_to_all(grads, ('zlo', 'x'), 0, 0, tiled=True)  21.3 us
  transfers between devices with their start and end apart: 79, of which 31 were waited for; matrix products, arithmetic and copies ran while one was open for 26% of the time, Pallas kernels for 4%

profile of v1, /device:TPU:8, one launch (start us, length us, event | category | flops | bytes accessed | tf_op | source)
XLA Modules:
  0.0 519.1 jit_solution(6236925992451271129)
XLA Ops:
  13.8 4.1 collective-permute-start.4
  18.8 3.5 slice_bitcast_fusion.1
  23.6 3.2 collective-permute-start.3
  30.2 15.2 %collective-permute-done.3 = bf16[1536,256]{1,0:T(8,128)(2,1)} collective-permute-done((bf16[1536,256]{1,0:T(8,128)(2,1)S(1)}, bf16[1536,256]{1,0:T(8,128)(2,1)}, u32[]{:S(2)}, u32[]{:S(2)}) %collective-permute-start.3) | collective-permute-done | bytes 786464 | tf_op jit(solution)/shard_map/ppermute | solution.py:37
  58.9 4.9 shard_map.144
  68.5 3.2 collective-permute-start.15
  74.4 4.1 collective-permute-done.8
  82.5 4.1 collective-permute-done.15
  86.6 3.0 collective-permute-start.17
  92.9 7.0 %collective-permute-done.18 = bf16[128,1024]{1,0:T(8,128)(2,1)S(1)} collective-permute-done((bf16[128,1024]{1,0:T(8,128)(2,1)S(1)}, bf16[128,1024]{1,0:T(8,128)(2,1)S(1)}, u32[]{:S(2)}, u32[]{:S(2)}) %collective-permute-start.18) | collective-permute-done | bytes 262176 | tf_op jit(solution)/shard_map/ppermute | solution.py:25
  99.9 4.0 collective-permute-done.17
  104.0 2.7 bitcast_select_fusion
  108.3 3.0 multiply_convert_fusion.3
  126.3 4.2 collective-permute-done.20
  137.4 4.6 collective-permute-done.24
  142.1 6.0 %collective-permute-done.25.far = bf16[128,1024]{1,0:T(8,128)(2,1)S(1)} collective-permute-done((bf16[128,1024]{1,0:T(8,128)(2,1)S(1)}, bf16[128,1024]{1,0:T(8,128)(2,1)S(1)}, u32[]{:S(2)}, u32[]{:S(2)}) %collective-permute-start.25) | collective-permute-done | bytes 262176 | tf_op jit(solution)/shard_map/ppermute | solution.py:25
  148.1 4.8 shard_map.145
  155.1 4.3 collective-permute-start.26
  161.5 4.9 collective-permute-done.28
  166.4 5.6 %collective-permute-start.34 = (bf16[128,1024]{1,0:T(8,128)(2,1)S(1)}, bf16[128,1024]{1,0:T(8,128)(2,1)S(1)}, u32[]{:S(2)}, u32[]{:S(2)}) collective-permute-start(bf16[128,1024]{1,0:T(8,128)(2,1)S(1)} %select_bitcast_fusion.9), channel_id=1, source_target_pairs={{0,2},{1,3},{2,0},{3,1},{4,6},{5,7},{6,4},{7,5},{8,10},{9,11},{10,... | collective-permute-start | bytes 786440 | tf_op jit(solution)/shard_map/ppermute | solution.py:25
  180.2 4.9 collective-permute-start.31
  187.5 3.0 add_convert_fusion.5
  192.3 2.9 collective-permute-start.37
  197.9 3.0 collective-permute-start.35
  220.2 6.7 %shard_map.146 = (bf16[512,768]{1,0:T(8,128)(2,1)S(1)}, bf16[384,1024]{1,0:T(8,128)(2,1)S(1)}, bf16[128,1024]{1,0:T(8,128)(2,1)S(1)}) custom-call(bf16[384,1024]{1,0:T(8,128)(2,1)S(1)} %pad_maximum_fusion.11.near, bf16[128,1024]{1,0:T(8,128)(2,1)S(1)} %collective-permute-done.40.far, bf16[1024,768]{1,0:T(8,128)(2,1)S(1)} %pad_maximum_fusion.4.w_qkv, ...), custom_call_target="tpu_custom_call" | custom-call | flops 4294967296 | bytes 8388608 | tf_op jit(solution)/shard_map/pallas_call | solution.py:239
  229.0 3.8 collective-permute-start.41
  237.8 3.8 collective-permute-done.41
  251.1 2.8 fusion.150
  263.8 3.4 multiply_convert_fusion
  273.7 3.6 collective-permute-start.49
  279.7 5.1 collective-permute-done.49
  301.1 4.7 collective-permute-done.58
  322.6 6.8 %shard_map.147 = (bf16[512,768]{1,0:T(8,128)(2,1)S(1)}, bf16[384,1024]{1,0:T(8,128)(2,1)S(1)}, bf16[128,1024]{1,0:T(8,128)(2,1)}) custom-call(bf16[384,1024]{1,0:T(8,128)(2,1)S(1)} %pad_maximum_fusion.13.near, bf16[128,1024]{1,0:T(8,128)(2,1)S(1)} %copy-done.15, bf16[1024,768]{1,0:T(8,128)(2,1)S(1)} %copy-done.1, bf16[256,1024]{1,0:T(8,128)(2,1)S(1)} %copy-done.3, ...), custom_call_target="tpu_custom_call" | custom-call | flops 4294967296 | bytes 8388608 | tf_op jit(solution)/shard_map/pallas_call | solution.py:239
  330.3 7.8 %collective-permute-start.62 = (bf16[128,1024]{1,0:T(8,128)(2,1)}, bf16[128,1024]{1,0:T(8,128)(2,1)}, u32[]{:S(2)}, u32[]{:S(2)}) collective-permute-start(bf16[128,1024]{1,0:T(8,128)(2,1)} %get-tuple-element.293), channel_id=1, source_target_pairs={{0,3},{1,0},{2,1},{3,2},{4,7},{5,4},{6,5},{7,6},{8,11},{9,8},{10,9... | collective-permute-start | bytes 786440 | tf_op jit(solution)/shard_map/ppermute | solution.py:25
  338.1 5.0 collective-permute-start.60
  351.7 2.8 convolution_convert_fusion.2
  358.0 3.4 maximum_maximum_fusion.2
  362.9 4.5 all-to-all-start
  376.3 6.7 %collective-permute-done.56 = bf16[128,1024]{1,0:T(8,128)(2,1)S(1)} collective-permute-done((bf16[128,1024]{1,0:T(8,128)(2,1)S(1)}, bf16[128,1024]{1,0:T(8,128)(2,1)S(1)}, u32[]{:S(2)}, u32[]{:S(2)}) %collective-permute-start.56) | collective-permute-done | bytes 262176 | tf_op jit(solution)/shard_map/ppermute | solution.py:25
  385.0 21.3 %all-to-all-done = bf16[8,544,256]{2,1,0:T(8,128)(2,1)} async-done(((bf16[8,544,256]{2,1,0:T(8,128)(2,1)}), bf16[8,544,256]{2,1,0:T(8,128)(2,1)}, u32[]{:S(2)}, u32[]{:S(2)}) %all-to-all-start) | async-done | bytes 2228256 | tf_op jit(solution)/shard_map/all_to_all | solution.py:429
  409.6 10.2 %reduce-scatter.3.cloned.1.call-done = bf16[128,1024]{1,0:T(8,128)(2,1)} async-done(((bf16[1024,1024]{1,0:T(8,128)(2,1)}), bf16[128,1024]{1,0:T(8,128)(2,1)}) %reduce-scatter.3.cloned.1.call-update) | async-done | bytes 262160 | tf_op jit(solution)/shard_map/reduce_scatter | solution.py:425
  423.2 7.1 %collective-permute-done.67 = bf16[196,1024]{1,0:T(8,128)(2,1)S(1)} collective-permute-done((bf16[196,1024]{1,0:T(8,128)(2,1)S(1)}, bf16[196,1024]{1,0:T(8,128)(2,1)S(1)}, u32[]{:S(2)}, u32[]{:S(2)}) %collective-permute-start.67) | collective-permute-done | bytes 401440 | tf_op jit(solution)/shard_map/ppermute | solution.py:33
  431.6 29.7 %all_to_all.24 = bf16[8,128,1024]{2,1,0:T(8,128)(2,1)S(1)} all-to-all(bf16[8,128,1024]{2,1,0:T(8,128)(2,1)S(1)} %broadcast_in_dim.111), channel_id=1, replica_groups=mesh['section'=2,'zlo'=2,'x'=4,'core'=2,'tensor'=4] {'zlo','x'}, dimensions={0} | all-to-all | bytes 4194304 | tf_op jit(solution)/shard_map/all_to_all | solution.py:436
  462.5 4.2 all-to-all-start.2
  471.3 2.8 maximum_convert_fusion
  474.1 10.0 %all-to-all-done.2 = bf16[8,272,256]{2,1,0:T(8,128)(2,1)} async-done(((bf16[8,272,256]{2,1,0:T(8,128)(2,1)}), bf16[8,272,256]{2,1,0:T(8,128)(2,1)}, u32[]{:S(2)}, u32[]{:S(2)}) %all-to-all-start.2) | async-done | bytes 1114144 | tf_op jit(solution)/shard_map/all_to_all | solution.py:436
  487.7 7.1 %collective-permute-done.69 = bf16[128,1024]{1,0:T(8,128)(2,1)S(1)} collective-permute-done((bf16[128,1024]{1,0:T(8,128)(2,1)S(1)}, bf16[128,1024]{1,0:T(8,128)(2,1)S(1)}, u32[]{:S(2)}, u32[]{:S(2)}) %collective-permute-start.69) | collective-permute-done | bytes 262176 | tf_op jit(solution)/shard_map/ppermute | solution.py:33
  494.7 5.2 %collective-permute-done.68 = bf16[128,1024]{1,0:T(8,128)(2,1)S(1)} collective-permute-done((bf16[128,1024]{1,0:T(8,128)(2,1)S(1)}, bf16[128,1024]{1,0:T(8,128)(2,1)S(1)}, u32[]{:S(2)}, u32[]{:S(2)}) %collective-permute-start.68) | collective-permute-done | bytes 262176 | tf_op jit(solution)/shard_map/ppermute | solution.py:33
  (568 shorter events, 223.7 us)
Async XLA Ops:
  7.2 401.4 %reduce-scatter.5.cloned.1.call-start = ((), (), s32[]{:S(2)}) async-start(), calls=%async_computation.6 | async-start | bytes 2359296 | tf_op jit(solution)/shard_map/reduce_scatter | solution.py:425
  8.4 20.5 %collective-permute-start.1 = (bf16[128,1024]{1,0:T(8,128)(2,1)S(1)}, bf16[128,1024]{1,0:T(8,128)(2,1)S(1)}, u32[]{:S(2)}, u32[]{:S(2)}) collective-permute-start(bf16[128,1024]{1,0:T(8,128)(2,1)S(1)} %get-tuple-element.223), channel_id=1, source_target_pairs={{0,1},{1,2},{2,3},{3,0},{4,5},{5,6},{6,7},{7,4},{8,9},{9,10},{10,1... | collective-permute-start | bytes 786440 | tf_op jit(solution)/shard_map/ppermute | solution.py:25
  10.1 19.0 %collective-permute-start = (bf16[128,1024]{1,0:T(8,128)(2,1)S(1)}, bf16[128,1024]{1,0:T(8,128)(2,1)S(1)}, u32[]{:S(2)}, u32[]{:S(2)}) collective-permute-start(bf16[128,1024]{1,0:T(8,128)(2,1)S(1)} %get-tuple-element.223), channel_id=1, source_target_pairs={{0,3},{1,0},{2,1},{3,2},{4,7},{5,4},{6,5},{7,6},{8,11},{9,8},{10,9... | collective-permute-start | bytes 786440 | tf_op jit(solution)/shard_map/ppermute | solution.py:25
  10.5 19.7 %collective-permute-start.2 = (bf16[128,1024]{1,0:T(8,128)(2,1)S(1)}, bf16[128,1024]{1,0:T(8,128)(2,1)S(1)}, u32[]{:S(2)}, u32[]{:S(2)}) collective-permute-start(bf16[128,1024]{1,0:T(8,128)(2,1)S(1)} %get-tuple-element.223), channel_id=1, source_target_pairs={{0,2},{1,3},{2,0},{3,1},{4,6},{5,7},{6,4},{7,5},{8,10},{9,11},{10,... | collective-permute-start | bytes 786440 | tf_op jit(solution)/shard_map/ppermute | solution.py:25
  13.8 13.0 %collective-permute-start.4 = (bf16[128,1024]{1,0:T(8,128)(2,1)S(1)}, bf16[128,1024]{1,0:T(8,128)(2,1)S(1)}, u32[]{:S(2)}, u32[]{:S(2)}) collective-permute-start(bf16[128,1024]{1,0:T(8,128)(2,1)S(1)} %constant_dynamic-slice_fusion.3), channel_id=1, source_target_pairs={{0,96},{32,64},{64,32},{96,0},{1,97},{33,65},{65,33},{97,1},{2,98}... | collective-permute-start | bytes 786440 | tf_op jit(solution)/shard_map/ppermute | solution.py:37
  23.6 21.9 %collective-permute-start.3 = (bf16[1536,256]{1,0:T(8,128)(2,1)S(1)}, bf16[1536,256]{1,0:T(8,128)(2,1)}, u32[]{:S(2)}, u32[]{:S(2)}) collective-permute-start(bf16[1536,256]{1,0:T(8,128)(2,1)S(1)} %constant_dynamic-slice_fusion.4), channel_id=1, source_target_pairs={{0,96},{32,64},{64,32},{96,0},{1,97},{33,65},{65,33},{97,1},{2,98}... | collective-permute-start | bytes 2359304 | tf_op jit(solution)/shard_map/ppermute | solution.py:37
  28.9 39.5 %collective-permute-start.13 = (bf16[328,1024]{1,0:T(8,128)(2,1)}, bf16[328,1024]{1,0:T(8,128)(2,1)}, u32[]{:S(2)}, u32[]{:S(2)}) collective-permute-start(bf16[328,1024]{1,0:T(8,128)(2,1)} %constant_dynamic-slice_fusion.2), channel_id=1, source_target_pairs={{0,96},{32,64},{64,32},{96,0},{1,97},{33,65},{65,33},{97,1},{2,98}... | collective-permute-start | bytes 2015240 | tf_op jit(solution)/shard_map/ppermute | solution.py:37
  65.9 12.6 %collective-permute-start.8 = (bf16[128,1024]{1,0:T(8,128)(2,1)S(1)}, bf16[128,1024]{1,0:T(8,128)(2,1)S(1)}, u32[]{:S(2)}, u32[]{:S(2)}) collective-permute-start(bf16[128,1024]{1,0:T(8,128)(2,1)S(1)} %get-tuple-element.101), channel_id=1, source_target_pairs={{0,2},{1,3},{2,0},{3,1},{4,6},{5,7},{6,4},{7,5},{8,10},{9,11},{10,... | collective-permute-start | bytes 786440 | tf_op jit(solution)/shard_map/ppermute | solution.py:25
  68.5 18.1 %collective-permute-start.15 = (bf16[328,1024]{1,0:T(8,128)(2,1)S(1)}, bf16[328,1024]{1,0:T(8,128)(2,1)S(1)}, u32[]{:S(2)}, u32[]{:S(2)}) collective-permute-start(bf16[328,1024]{1,0:T(8,128)(2,1)S(1)} %constant_dynamic-slice_fusion.1), channel_id=1, source_target_pairs={{0,96},{32,64},{64,32},{96,0},{1,97},{33,65},{65,33},{97,1},{2,98}... | collective-permute-start | bytes 2015240 | tf_op jit(solution)/shard_map/ppermute | solution.py:37
  71.7 20.0 %collective-permute-start.14 = (bf16[328,1024]{1,0:T(8,128)(2,1)}, bf16[328,1024]{1,0:T(8,128)(2,1)S(1)}, u32[]{:S(2)}, u32[]{:S(2)}) collective-permute-start(bf16[328,1024]{1,0:T(8,128)(2,1)} %collective-permute-done.13), channel_id=1, source_target_pairs={{0,4},{4,0},{1,5},{5,1},{2,6},{6,2},{3,7},{7,3},{8,12},{12,8},{9,1... | collective-permute-start | bytes 2015240 | tf_op jit(solution)/shard_map/ppermute | solution.py:29
  86.6 17.3 %collective-permute-start.17 = (bf16[328,1024]{1,0:T(8,128)(2,1)S(1)}, bf16[328,1024]{1,0:T(8,128)(2,1)S(1)}, u32[]{:S(2)}, u32[]{:S(2)}) collective-permute-start(bf16[328,1024]{1,0:T(8,128)(2,1)S(1)} %constant_dynamic-slice_fusion), channel_id=1, source_target_pairs={{0,96},{32,64},{64,32},{96,0},{1,97},{33,65},{65,33},{97,1},{2,98}... | collective-permute-start | bytes 2015240 | tf_op jit(solution)/shard_map/ppermute | solution.py:37
  89.7 14.2 %collective-permute-start.16 = (bf16[328,1024]{1,0:T(8,128)(2,1)S(1)}, bf16[328,1024]{1,0:T(8,128)(2,1)S(1)}, u32[]{:S(2)}, u32[]{:S(2)}) collective-permute-start(bf16[328,1024]{1,0:T(8,128)(2,1)S(1)} %collective-permute-done.15), channel_id=1, source_target_pairs={{0,4},{4,0},{1,5},{5,1},{2,6},{6,2},{3,7},{7,3},{8,12},{12,8},{9,1... | collective-permute-start | bytes 2015240 | tf_op jit(solution)/shard_map/ppermute | solution.py:29
  115.0 11.3 %collective-permute-start.22 = (bf16[128,1024]{1,0:T(8,128)(2,1)}, bf16[128,1024]{1,0:T(8,128)(2,1)}, u32[]{:S(2)}, u32[]{:S(2)}) collective-permute-start(bf16[128,1024]{1,0:T(8,128)(2,1)} %get-tuple-element.305), channel_id=1, source_target_pairs={{0,3},{1,0},{2,1},{3,2},{4,7},{5,4},{6,5},{7,6},{8,11},{9,8},{10,9... | collective-permute-start | bytes 786440 | tf_op jit(solution)/shard_map/ppermute | solution.py:25
  135.0 13.1 %collective-permute-start.25 = (bf16[128,1024]{1,0:T(8,128)(2,1)S(1)}, bf16[128,1024]{1,0:T(8,128)(2,1)S(1)}, u32[]{:S(2)}, u32[]{:S(2)}) collective-permute-start(bf16[128,1024]{1,0:T(8,128)(2,1)S(1)} %fusion.46), channel_id=1, source_target_pairs={{0,2},{1,3},{2,0},{3,1},{4,6},{5,7},{6,4},{7,5},{8,10},{9,11},{10,... | collective-permute-start | bytes 786440 | tf_op jit(solution)/shard_map/ppermute | solution.py:25
  153.0 13.4 %collective-permute-start.28 = (bf16[128,1024]{1,0:T(8,128)(2,1)S(1)}, bf16[128,1024]{1,0:T(8,128)(2,1)S(1)}, u32[]{:S(2)}, u32[]{:S(2)}) collective-permute-start(bf16[128,1024]{1,0:T(8,128)(2,1)S(1)} %get-tuple-element.303), channel_id=1, source_target_pairs={{0,3},{1,0},{2,1},{3,2},{4,7},{5,4},{6,5},{7,6},{8,11},{9,8},{10,9... | collective-permute-start | bytes 786440 | tf_op jit(solution)/shard_map/ppermute | solution.py:25
  154.3 17.7 %collective-permute-start.27 = (bf16[128,1024]{1,0:T(8,128)(2,1)S(1)}, bf16[128,1024]{1,0:T(8,128)(2,1)S(1)}, u32[]{:S(2)}, u32[]{:S(2)}) collective-permute-start(bf16[128,1024]{1,0:T(8,128)(2,1)S(1)} %get-tuple-element.302), channel_id=1, source_target_pairs={{0,1},{1,2},{2,3},{3,0},{4,5},{5,6},{6,7},{7,4},{8,9},{9,10},{10,1... | collective-permute-start | bytes 786440 | tf_op jit(solution)/shard_map/ppermute | solution.py:25
  155.1 16.9 %collective-permute-start.26 = (bf16[128,1024]{1,0:T(8,128)(2,1)S(1)}, bf16[128,1024]{1,0:T(8,128)(2,1)S(1)}, u32[]{:S(2)}, u32[]{:S(2)}) collective-permute-start(bf16[128,1024]{1,0:T(8,128)(2,1)S(1)} %get-tuple-element.110), channel_id=1, source_target_pairs={{0,2},{1,3},{2,0},{3,1},{4,6},{5,7},{6,4},{7,5},{8,10},{9,11},{10,... | collective-permute-start | bytes 786440 | tf_op jit(solution)/shard_map/ppermute | solution.py:25
  159.4 17.2 %collective-permute-start.33 = (bf16[128,1024]{1,0:T(8,128)(2,1)S(1)}, bf16[128,1024]{1,0:T(8,128)(2,1)S(1)}, u32[]{:S(2)}, u32[]{:S(2)}) collective-permute-start(bf16[128,1024]{1,0:T(8,128)(2,1)S(1)} %select_bitcast_fusion.9), channel_id=1, source_target_pairs={{0,1},{1,2},{2,3},{3,0},{4,5},{5,6},{6,7},{7,4},{8,9},{9,10},{10,1... | collective-permute-start | bytes 786440 | tf_op jit(solution)/shard_map/ppermute | solution.py:25
  159.5 18.1 %collective-permute-start.32 = (bf16[128,1024]{1,0:T(8,128)(2,1)S(1)}, bf16[128,1024]{1,0:T(8,128)(2,1)S(1)}, u32[]{:S(2)}, u32[]{:S(2)}) collective-permute-start(bf16[128,1024]{1,0:T(8,128)(2,1)S(1)} %select_bitcast_fusion.9), channel_id=1, source_target_pairs={{0,3},{1,0},{2,1},{3,2},{4,7},{5,4},{6,5},{7,6},{8,11},{9,8},{10,9... | collective-permute-start | bytes 786440 | tf_op jit(solution)/shard_map/ppermute | solution.py:25
  166.4 13.8 %collective-permute-start.34 = (bf16[128,1024]{1,0:T(8,128)(2,1)S(1)}, bf16[128,1024]{1,0:T(8,128)(2,1)S(1)}, u32[]{:S(2)}, u32[]{:S(2)}) collective-permute-start(bf16[128,1024]{1,0:T(8,128)(2,1)S(1)} %select_bitcast_fusion.9), channel_id=1, source_target_pairs={{0,2},{1,3},{2,0},{3,1},{4,6},{5,7},{6,4},{7,5},{8,10},{9,11},{10,... | collective-permute-start | bytes 786440 | tf_op jit(solution)/shard_map/ppermute | solution.py:25
  172.7 13.2 %collective-permute-start.30 = (bf16[128,1024]{1,0:T(8,128)(2,1)S(1)}, bf16[128,1024]{1,0:T(8,128)(2,1)S(1)}, u32[]{:S(2)}, u32[]{:S(2)}) collective-permute-start(bf16[128,1024]{1,0:T(8,128)(2,1)S(1)} %multiply_convert_fusion.4), channel_id=1, source_target_pairs={{0,1},{1,2},{2,3},{3,0},{4,5},{5,6},{6,7},{7,4},{8,9},{9,10},{10,1... | collective-permute-start | bytes 786440 | tf_op jit(solution)/shard_map/ppermute | solution.py:25
  172.8 13.1 %collective-permute-start.29 = (bf16[128,1024]{1,0:T(8,128)(2,1)S(1)}, bf16[128,1024]{1,0:T(8,128)(2,1)S(1)}, u32[]{:S(2)}, u32[]{:S(2)}) collective-permute-start(bf16[128,1024]{1,0:T(8,128)(2,1)S(1)} %multiply_convert_fusion.4), channel_id=1, source_target_pairs={{0,3},{1,0},{2,1},{3,2},{4,7},{5,4},{6,5},{7,6},{8,11},{9,8},{10,9... | collective-permute-start | bytes 786440 | tf_op jit(solution)/shard_map/ppermute | solution.py:25
  180.2 15.0 %collective-permute-start.31 = (bf16[128,1024]{1,0:T(8,128)(2,1)S(1)}, bf16[128,1024]{1,0:T(8,128)(2,1)S(1)}, u32[]{:S(2)}, u32[]{:S(2)}) collective-permute-start(bf16[128,1024]{1,0:T(8,128)(2,1)S(1)} %multiply_convert_fusion.4), channel_id=1, source_target_pairs={{0,2},{1,3},{2,0},{3,1},{4,6},{5,7},{6,4},{7,5},{8,10},{9,11},{10,... | collective-permute-start | bytes 786440 | tf_op jit(solution)/shard_map/ppermute | solution.py:25
  206.7 11.0 %collective-permute-start.39 = (bf16[128,1024]{1,0:T(8,128)(2,1)S(1)}, bf16[128,1024]{1,0:T(8,128)(2,1)S(1)}, u32[]{:S(2)}, u32[]{:S(2)}) collective-permute-start(bf16[128,1024]{1,0:T(8,128)(2,1)S(1)} %get-tuple-element.230), channel_id=1, source_target_pairs={{0,1},{1,2},{2,3},{3,0},{4,5},{5,6},{6,7},{7,4},{8,9},{9,10},{10,1... | collective-permute-start | bytes 786440 | tf_op jit(solution)/shard_map/ppermute | solution.py:25
  214.1 41.3 %collective-permute-start.48 = (bf16[328,1024]{1,0:T(8,128)(2,1)}, bf16[328,1024]{1,0:T(8,128)(2,1)}, u32[]{:S(2)}, u32[]{:S(2)}) collective-permute-start(bf16[328,1024]{1,0:T(8,128)(2,1)} %convolution_convert_fusion.7), channel_id=1, source_target_pairs={{0,4},{4,0},{1,5},{5,1},{2,6},{6,2},{3,7},{7,3},{8,12},{12,8},{9,1... | collective-permute-start | bytes 2015240 | tf_op jit(solution)/shard_map/ppermute | solution.py:29
  217.2 42.7 %collective-permute-start.47 = (bf16[656,1024]{1,0:T(8,128)(2,1)}, bf16[656,1024]{1,0:T(8,128)(2,1)}, u32[]{:S(2)}, u32[]{:S(2)}) collective-permute-start(bf16[656,1024]{1,0:T(8,128)(2,1)} %convolution_convert_fusion.1), channel_id=1, source_target_pairs={{0,4},{4,0},{1,5},{5,1},{2,6},{6,2},{3,7},{7,3},{8,12},{12,8},{9,1... | collective-permute-start | bytes 4030472 | tf_op jit(solution)/shard_map/ppermute | solution.py:29
  229.0 12.5 %collective-permute-start.41 = (bf16[128,1024]{1,0:T(8,128)(2,1)S(1)}, bf16[128,1024]{1,0:T(8,128)(2,1)S(1)}, u32[]{:S(2)}, u32[]{:S(2)}) collective-permute-start(bf16[128,1024]{1,0:T(8,128)(2,1)S(1)} %get-tuple-element.134), channel_id=1, source_target_pairs={{0,2},{1,3},{2,0},{3,1},{4,6},{5,7},{6,4},{7,5},{8,10},{9,11},{10,... | collective-permute-start | bytes 786440 | tf_op jit(solution)/shard_map/ppermute | solution.py:25
  242.6 14.6 %collective-permute-start.45 = (bf16[128,1024]{1,0:T(8,128)(2,1)S(1)}, bf16[128,1024]{1,0:T(8,128)(2,1)}, u32[]{:S(2)}, u32[]{:S(2)}) collective-permute-start(bf16[128,1024]{1,0:T(8,128)(2,1)S(1)} %add_convert_fusion.9), channel_id=1, source_target_pairs={{0,1},{1,2},{2,3},{3,0},{4,5},{5,6},{6,7},{7,4},{8,9},{9,10},{10,1... | collective-permute-start | bytes 786440 | tf_op jit(solution)/shard_map/ppermute | solution.py:25
  243.3 14.6 %collective-permute-start.44 = (bf16[128,1024]{1,0:T(8,128)(2,1)S(1)}, bf16[128,1024]{1,0:T(8,128)(2,1)}, u32[]{:S(2)}, u32[]{:S(2)}) collective-permute-start(bf16[128,1024]{1,0:T(8,128)(2,1)S(1)} %add_convert_fusion.9), channel_id=1, source_target_pairs={{0,3},{1,0},{2,1},{3,2},{4,7},{5,4},{6,5},{7,6},{8,11},{9,8},{10,9... | collective-permute-start | bytes 786440 | tf_op jit(solution)/shard_map/ppermute | solution.py:25
  245.1 18.7 %collective-permute-start.46 = (bf16[128,1024]{1,0:T(8,128)(2,1)S(1)}, bf16[128,1024]{1,0:T(8,128)(2,1)}, u32[]{:S(2)}, u32[]{:S(2)}) collective-permute-start(bf16[128,1024]{1,0:T(8,128)(2,1)S(1)} %add_convert_fusion.9), channel_id=1, source_target_pairs={{0,2},{1,3},{2,0},{3,1},{4,6},{5,7},{6,4},{7,5},{8,10},{9,11},{10,... | collective-permute-start | bytes 786440 | tf_op jit(solution)/shard_map/ppermute | solution.py:25
  255.4 38.6 %collective-permute-start.66 = (bf16[1024,256]{1,0:T(8,128)(2,1)}, bf16[1024,256]{1,0:T(8,128)(2,1)}, u32[]{:S(2)}, u32[]{:S(2)}) collective-permute-start(bf16[1024,256]{1,0:T(8,128)(2,1)} %convolution_convert_fusion.8), channel_id=1, source_target_pairs={{0,4},{4,0},{1,5},{5,1},{2,6},{6,2},{3,7},{7,3},{8,12},{12,8},{9,1... | collective-permute-start | bytes 1572872 | tf_op jit(solution)/shard_map/ppermute | solution.py:29
  257.2 20.1 %collective-permute-start.65 = (bf16[1024,256]{1,0:T(8,128)(2,1)}, bf16[1024,256]{1,0:T(8,128)(2,1)}, u32[]{:S(2)}, u32[]{:S(2)}) collective-permute-start(bf16[1024,256]{1,0:T(8,128)(2,1)} %convolution_convert_fusion.9), channel_id=1, source_target_pairs={{0,4},{4,0},{1,5},{5,1},{2,6},{6,2},{3,7},{7,3},{8,12},{12,8},{9,1... | collective-permute-start | bytes 1572872 | tf_op jit(solution)/shard_map/ppermute | solution.py:29
  268.7 11.0 %collective-permute-start.51 = (bf16[128,1024]{1,0:T(8,128)(2,1)S(1)}, bf16[128,1024]{1,0:T(8,128)(2,1)S(1)}, u32[]{:S(2)}, u32[]{:S(2)}) collective-permute-start(bf16[128,1024]{1,0:T(8,128)(2,1)S(1)} %get-tuple-element.297), channel_id=1, source_target_pairs={{0,3},{1,0},{2,1},{3,2},{4,7},{5,4},{6,5},{7,6},{8,11},{9,8},{10,9... | collective-permute-start | bytes 786440 | tf_op jit(solution)/shard_map/ppermute | solution.py:25
  273.7 11.1 %collective-permute-start.49 = (bf16[128,1024]{1,0:T(8,128)(2,1)S(1)}, bf16[128,1024]{1,0:T(8,128)(2,1)S(1)}, u32[]{:S(2)}, u32[]{:S(2)}) collective-permute-start(bf16[128,1024]{1,0:T(8,128)(2,1)S(1)} %convolution_convert_fusion.14), channel_id=1, source_target_pairs={{0,2},{1,3},{2,0},{3,1},{4,6},{5,7},{6,4},{7,5},{8,10},{9,11},{10,... | collective-permute-start | bytes 786440 | tf_op jit(solution)/shard_map/ppermute | solution.py:25
  289.9 18.7 %collective-permute-start.52 = (bf16[656,1024]{1,0:T(8,128)(2,1)}, bf16[656,1024]{1,0:T(8,128)(2,1)}, u32[]{:S(2)}, u32[]{:S(2)}) collective-permute-start(bf16[656,1024]{1,0:T(8,128)(2,1)} %convolution_convert_fusion), channel_id=1, source_target_pairs={{0,4},{4,0},{1,5},{5,1},{2,6},{6,2},{3,7},{7,3},{8,12},{12,8},{9,1... | collective-permute-start | bytes 4030472 | tf_op jit(solution)/shard_map/ppermute | solution.py:29
  293.4 13.4 %collective-permute-start.53 = (bf16[328,1024]{1,0:T(8,128)(2,1)}, bf16[328,1024]{1,0:T(8,128)(2,1)}, u32[]{:S(2)}, u32[]{:S(2)}) collective-permute-start(bf16[328,1024]{1,0:T(8,128)(2,1)} %convolution_convert_fusion.6), channel_id=1, source_target_pairs={{0,4},{4,0},{1,5},{5,1},{2,6},{6,2},{3,7},{7,3},{8,12},{12,8},{9,1... | collective-permute-start | bytes 2015240 | tf_op jit(solution)/shard_map/ppermute | solution.py:29
  296.0 123.8 %reduce-scatter.3.cloned.1.call-start = ((), (), s32[]{:S(2)}) async-start(), calls=%async_computation.5 | async-start | bytes 2359296 | tf_op jit(solution)/shard_map/reduce_scatter | solution.py:425
  298.5 14.0 %collective-permute-start.59 = (bf16[128,1024]{1,0:T(8,128)(2,1)}, bf16[128,1024]{1,0:T(8,128)(2,1)S(1)}, u32[]{:S(2)}, u32[]{:S(2)}) collective-permute-start(bf16[128,1024]{1,0:T(8,128)(2,1)} %get-tuple-element.220), channel_id=1, source_target_pairs={{0,2},{1,3},{2,0},{3,1},{4,6},{5,7},{6,4},{7,5},{8,10},{9,11},{10,... | collective-permute-start | bytes 786440 | tf_op jit(solution)/shard_map/ppermute | solution.py:25
  330.3 40.8 %collective-permute-start.62 = (bf16[128,1024]{1,0:T(8,128)(2,1)}, bf16[128,1024]{1,0:T(8,128)(2,1)}, u32[]{:S(2)}, u32[]{:S(2)}) collective-permute-start(bf16[128,1024]{1,0:T(8,128)(2,1)} %get-tuple-element.293), channel_id=1, source_target_pairs={{0,3},{1,0},{2,1},{3,2},{4,7},{5,4},{6,5},{7,6},{8,11},{9,8},{10,9... | collective-permute-start | bytes 786440 | tf_op jit(solution)/shard_map/ppermute | solution.py:25
  338.1 34.2 %collective-permute-start.61 = (bf16[128,1024]{1,0:T(8,128)(2,1)}, bf16[128,1024]{1,0:T(8,128)(2,1)}, u32[]{:S(2)}, u32[]{:S(2)}) collective-permute-start(bf16[128,1024]{1,0:T(8,128)(2,1)} %get-tuple-element.292), channel_id=1, source_target_pairs={{0,1},{1,2},{2,3},{3,0},{4,5},{5,6},{6,7},{7,4},{8,9},{9,10},{10,1... | collective-permute-start | bytes 786440 | tf_op jit(solution)/shard_map/ppermute | solution.py:25
  338.1 34.2 %collective-permute-start.60 = (bf16[128,1024]{1,0:T(8,128)(2,1)}, bf16[128,1024]{1,0:T(8,128)(2,1)}, u32[]{:S(2)}, u32[]{:S(2)}) collective-permute-start(bf16[128,1024]{1,0:T(8,128)(2,1)} %get-tuple-element.161), channel_id=1, source_target_pairs={{0,2},{1,3},{2,0},{3,1},{4,6},{5,7},{6,4},{7,5},{8,10},{9,11},{10,... | collective-permute-start | bytes 786440 | tf_op jit(solution)/shard_map/ppermute | solution.py:25
  362.9 43.4 %all-to-all-start = ((bf16[8,544,256]{2,1,0:T(8,128)(2,1)}), bf16[8,544,256]{2,1,0:T(8,128)(2,1)}, u32[]{:S(2)}, u32[]{:S(2)}) async-start(bf16[8,544,256]{2,1,0:T(8,128)(2,1)} %pad_maximum_fusion.1), calls=%async_computation.1 | async-start | bytes 4456448 | tf_op jit(solution)/shard_map/all_to_all | solution.py:429
  368.5 14.4 %collective-permute-start.56 = (bf16[128,1024]{1,0:T(8,128)(2,1)S(1)}, bf16[128,1024]{1,0:T(8,128)(2,1)S(1)}, u32[]{:S(2)}, u32[]{:S(2)}) collective-permute-start(bf16[128,1024]{1,0:T(8,128)(2,1)S(1)} %get-tuple-element.295), channel_id=1, source_target_pairs={{0,3},{1,0},{2,1},{3,2},{4,7},{5,4},{6,5},{7,6},{8,11},{9,8},{10,9... | collective-permute-start | bytes 786440 | tf_op jit(solution)/shard_map/ppermute | solution.py:25
  368.6 14.3 %collective-permute-start.55 = (bf16[128,1024]{1,0:T(8,128)(2,1)S(1)}, bf16[128,1024]{1,0:T(8,128)(2,1)S(1)}, u32[]{:S(2)}, u32[]{:S(2)}) collective-permute-start(bf16[128,1024]{1,0:T(8,128)(2,1)S(1)} %get-tuple-element.294), channel_id=1, source_target_pairs={{0,1},{1,2},{2,3},{3,0},{4,5},{5,6},{6,7},{7,4},{8,9},{9,10},{10,1... | collective-permute-start | bytes 786440 | tf_op jit(solution)/shard_map/ppermute | solution.py:25
  371.1 11.9 %collective-permute-start.54 = (bf16[128,1024]{1,0:T(8,128)(2,1)S(1)}, bf16[128,1024]{1,0:T(8,128)(2,1)S(1)}, u32[]{:S(2)}, u32[]{:S(2)}) collective-permute-start(bf16[128,1024]{1,0:T(8,128)(2,1)S(1)} %convolution_convert_fusion.12), channel_id=1, source_target_pairs={{0,2},{1,3},{2,0},{3,1},{4,6},{5,7},{6,4},{7,5},{8,10},{9,11},{10,... | collective-permute-start | bytes 786440 | tf_op jit(solution)/shard_map/ppermute | solution.py:25
  462.5 21.6 %all-to-all-start.2 = ((bf16[8,272,256]{2,1,0:T(8,128)(2,1)}), bf16[8,272,256]{2,1,0:T(8,128)(2,1)}, u32[]{:S(2)}, u32[]{:S(2)}) async-start(bf16[8,272,256]{2,1,0:T(8,128)(2,1)} %broadcast_in_dim.114), calls=%async_computation.4 | async-start | bytes 2228224 | tf_op jit(solution)/shard_map/all_to_all | solution.py:436
  484.1 17.6 %collective-permute-start.71 = (bf16[2176,256]{1,0:T(8,128)(2,1)}, bf16[2176,256]{1,0:T(8,128)(2,1)S(1)}, u32[]{:S(2)}, u32[]{:S(2)}) collective-permute-start(bf16[2176,256]{1,0:T(8,128)(2,1)} %bitcast.43), channel_id=1, source_target_pairs={{0,4},{4,0},{1,5},{5,1},{2,6},{6,2},{3,7},{7,3},{8,12},{12,8},{9,1... | collective-permute-start | bytes 3342344 | tf_op jit(solution)/shard_map/ppermute | solution.py:29
  485.4 14.6 %collective-permute-start.68 = (bf16[128,1024]{1,0:T(8,128)(2,1)S(1)}, bf16[128,1024]{1,0:T(8,128)(2,1)S(1)}, u32[]{:S(2)}, u32[]{:S(2)}) collective-permute-start(bf16[128,1024]{1,0:T(8,128)(2,1)S(1)} %copy-done.93), channel_id=1, source_target_pairs={{0,64},{64,0},{1,65},{65,1},{2,66},{66,2},{3,67},{67,3},{4,68},{68... | collective-permute-start | bytes 786440 | tf_op jit(solution)/shard_map/ppermute | solution.py:33
  (139 other events, 1516.8 us)
Sparse Core Ops, SparseCore 0:
  296.1 42.9 reduce-scatter.4
  351.2 68.5 reduce-scatter.2

commit v2 on v1

--- a/solution.py
+++ b/solution.py
@@ -529,9 +529,10 @@
     )
     model_width = w_qkv.shape[1]
     ffn1 = reduce_part(ffn_pack1)
-    ffn_pack0 = ffn_grads0(mid0)[1](())
-    in0, attn_grads0, unused, gain_before, unused = backward_attn(
-        mid0, kept0, gains0[0], layer0, allowed0, tables0, ffn_pack0, lambda gate: ()
+    ffn_sent0, ffn_pack0 = ffn_grads0(mid0)
+    in0, attn_grads0, unused, gain_before, (ffn_pack0, unused) = backward_attn(
+        mid0, kept0, gains0[0], layer0, allowed0, tables0, ffn_sent0,
+        lambda gate: (ffn_pack0(gate), ffn1),
     )
     in0 = in0.astype(bf16)
     ffn0 = reduce_part(ffn_pack0)
@@ -550,7 +551,19 @@
     part = (own_part.astype(f32) + swap_section(sent_part).astype(f32)).astype(bf16)
     ffn_rows = ffn0.shape[0]
     ffn_half = spread_part(part[:ffn_rows])
-    attn_part = after_all(part[ffn_rows:].reshape(-1, attn_width), ffn_half)
+    got_out = swap_section(jnp.where(is_first, out1, out0))
+    got_in = swap_section(jnp.where(is_first, in1, in0))
+    attn_part = part[ffn_rows:].reshape(-1, attn_width)
+    gain_start = 2 * model_width % attn_rows
+    gain_span = slice(gain_start, gain_start + 8)
+    gain_rows = attn_part[gain_span]
+    holds_gains = lax.axis_index(("zlo", "x")) == 2 * model_width // attn_rows
+    gain_rows = jnp.where(
+        holds_gains, sum_tensor(gain_rows.astype(f32)).astype(bf16), gain_rows
+    )
+    attn_part = joined([attn_part[:gain_start], gain_rows, attn_part[gain_start + 8 :]])
+    attn_part, got_out, got_in = after_all((attn_part, got_out, got_in), ffn_half)
+    attn_part = after_all(attn_part, got_out, got_in)
     attn_half = spread_part(attn_part)
     is_core0 = lax.axis_index("core") == 0
 
@@ -566,8 +579,8 @@
     )
     attn_half, grad_up, grad_down = lax.optimization_barrier((attn_half, grad_up, grad_down))
     attn_halves = (attn_half, swap_core(attn_half))
-    gain_rows = sum(of_core(core, attn_halves, 2 * model_width, 8) for core in range(2))
-    gain_total = sum_tensor(gain_rows).reshape(2, -1)
+    gain_total = sum(of_core(core, attn_halves, 2 * model_width, 8) for core in range(2))
+    gain_total = gain_total.reshape(2, -1)
     grad_qkv = jnp.stack(
         [
             of_core(0, attn_halves, 0, model_width),
@@ -577,10 +590,6 @@
     )
     grad_out = of_core(1, attn_halves, model_width, model_width).T
 
-    sent_out, sent_in = after_all(
-        (jnp.where(is_first, out1, out0), jnp.where(is_first, in1, in0)), ffn_half
-    )
-    got_out, got_in = swap_section(sent_out), swap_section(sent_in)
     section_out = jnp.stack(
         [jnp.where(is_first, out0, got_out), jnp.where(is_first, got_out, out1)]
     )

time: 529 us -> 502 us (0.949)
  the two profiles are of different devices: /device:TPU:8 before, /device:TPU:1 now
where the time goes in v2:
time: 502 us; the launch traced here: 492 us
  waiting for transfers between devices  150 us (30%)
  starting transfers between devices  131 us (26%)
  other arithmetic  67.6 us (13%)
  matrix products  41.4 us (8%)
  local copies, waits for them, and re-layouts  35.7 us (7%)
  blocking collectives  26.8 us (5%)
  Pallas kernels  23.2 us (5%)
  between operations  16.3 us (3%)
    ppermute x51, waiting for transfers between devices, around(): lax.ppermute(block, axis, [(i, (i + distance) % count) for i in range(cou...  79.9 us
    ppermute x51, starting transfers between devices, around(): lax.ppermute(block, axis, [(i, (i + distance) % count) for i in range(cou...  61.6 us
    ppermute x15, starting transfers between devices, swap_core(): return lax.ppermute(block, 'core', [(0, 1), (1, 0)])  46 us
    reduce_scatter x2, waiting for transfers between devices, reduce_part(): lax.psum_scatter(grads, ('zlo', 'x'), scatter_dimension=0, tiled=True)  32 us
    all_to_all x1, blocking collectives, spread_part(): return lax.all_to_all(copies, ('zlo', 'x'), 0, 0, tiled=True)  26.8 us
    pallas_call x4, Pallas kernels, whole_call(): pl.pallas_call(kernel, out_shape=[jax.ShapeDtypeStruct(*shape) for shape...  23.2 us
    dot_general x16, matrix products, contract_rows(): lax.dot_general(left_rows, right_rows, (((0,), (0,)), ((), ())), preferre...  19.9 us
    ppermute x3, waiting for transfers between devices, swap_section(): return lax.ppermute(block, 'section', [(0, 1), (1, 0)])  17.7 us
  transfers between devices with their start and end apart: 79, of which 25 were waited for; matrix products, arithmetic and copies ran while one was open for 24% of the time, Pallas kernels for 4%

profile of v2, /device:TPU:1, one launch (start us, length us, event | category | flops | bytes accessed | tf_op | source)
XLA Modules:
  0.0 492.1 jit_solution(11084584537341008032)
XLA Ops:
  14.7 3.8 collective-permute-start.4
  19.5 3.5 slice_bitcast_fusion.1
  25.0 2.7 collective-permute-start.3
  34.4 9.5 %collective-permute-done.3 = bf16[1536,256]{1,0:T(8,128)(2,1)} collective-permute-done((bf16[1536,256]{1,0:T(8,128)(2,1)}, bf16[1536,256]{1,0:T(8,128)(2,1)}, u32[]{:S(2)}, u32[]{:S(2)}) %collective-permute-start.3) | collective-permute-done | bytes 786464 | tf_op jit(solution)/shard_map/ppermute | solution.py:37
  44.9 5.1 %collective-permute-start.6 = (bf16[1536,256]{1,0:T(8,128)(2,1)}, bf16[1536,256]{1,0:T(8,128)(2,1)S(1)}, u32[]{:S(2)}, u32[]{:S(2)}) collective-permute-start(bf16[1536,256]{1,0:T(8,128)(2,1)} %collective-permute-done.3), channel_id=1, source_target_pairs={{0,4},{4,0},{1,5},{5,1},{2,6},{6,2},{3,7},{7,3},{8,12},{12,8},{9,1... | collective-permute-start | bytes 2359304 | tf_op jit(solution)/shard_map/ppermute | solution.py:29
  59.2 4.9 shard_map.144
  67.0 2.9 collective-permute-start.15
  70.0 13.9 %collective-permute-start.14 = (bf16[328,1024]{1,0:T(8,128)(2,1)}, bf16[328,1024]{1,0:T(8,128)(2,1)S(1)}, u32[]{:S(2)}, u32[]{:S(2)}) collective-permute-start(bf16[328,1024]{1,0:T(8,128)(2,1)} %collective-permute-done.13), channel_id=1, source_target_pairs={{0,4},{4,0},{1,5},{5,1},{2,6},{6,2},{3,7},{7,3},{8,12},{12,8},{9,1... | collective-permute-start | bytes 2015240 | tf_op jit(solution)/shard_map/ppermute | solution.py:29
  89.1 4.7 collective-permute-done.12
  96.5 5.9 %collective-permute-done.18 = bf16[128,1024]{1,0:T(8,128)(2,1)S(1)} collective-permute-done((bf16[128,1024]{1,0:T(8,128)(2,1)S(1)}, bf16[128,1024]{1,0:T(8,128)(2,1)S(1)}, u32[]{:S(2)}, u32[]{:S(2)}) %collective-permute-start.18) | collective-permute-done | bytes 262176 | tf_op jit(solution)/shard_map/ppermute | solution.py:25
  110.6 3.0 multiply_convert_fusion.3
  128.6 2.8 collective-permute-done.20
  133.5 2.7 collective-permute-start.23
  137.7 2.8 collective-permute-done.24
  140.6 6.2 %collective-permute-done.25.far = bf16[128,1024]{1,0:T(8,128)(2,1)S(1)} collective-permute-done((bf16[128,1024]{1,0:T(8,128)(2,1)S(1)}, bf16[128,1024]{1,0:T(8,128)(2,1)S(1)}, u32[]{:S(2)}, u32[]{:S(2)}) %collective-permute-start.25) | collective-permute-done | bytes 262176 | tf_op jit(solution)/shard_map/ppermute | solution.py:25
  146.7 4.8 shard_map.145
  158.6 4.8 collective-permute-done.27
  164.2 2.7 collective-permute-start.29
  166.9 7.8 %collective-permute-done.32 = bf16[128,1024]{1,0:T(8,128)(2,1)S(1)} collective-permute-done((bf16[128,1024]{1,0:T(8,128)(2,1)S(1)}, bf16[128,1024]{1,0:T(8,128)(2,1)S(1)}, u32[]{:S(2)}, u32[]{:S(2)}) %collective-permute-start.32) | collective-permute-done | bytes 262176 | tf_op jit(solution)/shard_map/ppermute | solution.py:25
  176.4 9.5 %collective-permute-done.30 = bf16[128,1024]{1,0:T(8,128)(2,1)S(1)} collective-permute-done((bf16[128,1024]{1,0:T(8,128)(2,1)S(1)}, bf16[128,1024]{1,0:T(8,128)(2,1)S(1)}, u32[]{:S(2)}, u32[]{:S(2)}) %collective-permute-start.30) | collective-permute-done | bytes 262176 | tf_op jit(solution)/shard_map/ppermute | solution.py:25
  187.5 2.8 multiply_convert_fusion.2
  198.9 5.2 %collective-permute-done.35 = bf16[128,1024]{1,0:T(8,128)(2,1)S(1)} collective-permute-done((bf16[128,1024]{1,0:T(8,128)(2,1)S(1)}, bf16[128,1024]{1,0:T(8,128)(2,1)S(1)}, u32[]{:S(2)}, u32[]{:S(2)}) %collective-permute-start.35) | collective-permute-done | bytes 262176 | tf_op jit(solution)/shard_map/ppermute | solution.py:25
  205.1 2.7 collective-permute-start.38
  209.9 5.4 %collective-permute-start.48 = (bf16[328,1024]{1,0:T(8,128)(2,1)}, bf16[328,1024]{1,0:T(8,128)(2,1)}, u32[]{:S(2)}, u32[]{:S(2)}) collective-permute-start(bf16[328,1024]{1,0:T(8,128)(2,1)} %convolution_convert_fusion.7), channel_id=1, source_target_pairs={{0,4},{4,0},{1,5},{5,1},{2,6},{6,2},{3,7},{7,3},{8,12},{12,8},{9,1... | collective-permute-start | bytes 2015240 | tf_op jit(solution)/shard_map/ppermute | solution.py:29
  218.3 6.7 %shard_map.146 = (bf16[512,768]{1,0:T(8,128)(2,1)S(1)}, bf16[384,1024]{1,0:T(8,128)(2,1)S(1)}, bf16[128,1024]{1,0:T(8,128)(2,1)S(1)}) custom-call(bf16[384,1024]{1,0:T(8,128)(2,1)S(1)} %pad_maximum_fusion.11.near, bf16[128,1024]{1,0:T(8,128)(2,1)S(1)} %collective-permute-done.40.far, bf16[1024,768]{1,0:T(8,128)(2,1)S(1)} %pad_maximum_fusion.4.w_qkv, ...), custom_call_target="tpu_custom_call" | custom-call | flops 4294967296 | bytes 8388608 | tf_op jit(solution)/shard_map/pallas_call | solution.py:239
  226.6 3.3 collective-permute-start.41
  232.8 7.2 %collective-permute-done.41 = bf16[128,1024]{1,0:T(8,128)(2,1)S(1)} collective-permute-done((bf16[128,1024]{1,0:T(8,128)(2,1)S(1)}, bf16[128,1024]{1,0:T(8,128)(2,1)S(1)}, u32[]{:S(2)}, u32[]{:S(2)}) %collective-permute-start.41) | collective-permute-done | bytes 262176 | tf_op jit(solution)/shard_map/ppermute | solution.py:25
  241.1 2.7 collective-permute-start.44
  246.2 4.0 collective-permute-start.59
  275.6 3.1 collective-permute-start.49
  281.2 6.4 %collective-permute-done.49 = bf16[128,1024]{1,0:T(8,128)(2,1)} collective-permute-done((bf16[128,1024]{1,0:T(8,128)(2,1)}, bf16[128,1024]{1,0:T(8,128)(2,1)}, u32[]{:S(2)}, u32[]{:S(2)}) %collective-permute-start.49) | collective-permute-done | bytes 262176 | tf_op jit(solution)/shard_map/ppermute | solution.py:25
  291.8 2.7 collective-permute-start.52
  301.8 3.4 collective-permute-done.53
  305.3 6.8 %shard_map.147 = (bf16[512,768]{1,0:T(8,128)(2,1)S(1)}, bf16[384,1024]{1,0:T(8,128)(2,1)S(1)}, bf16[128,1024]{1,0:T(8,128)(2,1)S(1)}) custom-call(bf16[384,1024]{1,0:T(8,128)(2,1)S(1)} %pad_maximum_fusion.13.near, bf16[128,1024]{1,0:T(8,128)(2,1)S(1)} %collective-permute-done.54.far, bf16[1024,768]{1,0:T(8,128)(2,1)S(1)} %pad_maximum_fusion.3.w_qkv, ...), custom_call_target="tpu_custom_call" | custom-call | flops 4294967296 | bytes 8388608 | tf_op jit(solution)/shard_map/pallas_call | solution.py:239
  326.2 2.7 collective-permute-start.66
  335.4 4.5 all-to-all-start
  342.0 2.7 collective-permute-start.63
  346.9 6.4 %collective-permute-done.63 = bf16[128,1024]{1,0:T(8,128)(2,1)S(1)} collective-permute-done((bf16[128,1024]{1,0:T(8,128)(2,1)S(1)}, bf16[128,1024]{1,0:T(8,128)(2,1)S(1)}, u32[]{:S(2)}, u32[]{:S(2)}) %collective-permute-start.63) | collective-permute-done | bytes 262176 | tf_op jit(solution)/shard_map/ppermute | solution.py:25
  356.2 32.0 %reduce-scatter.3.cloned.1.call-done = bf16[128,1024]{1,0:T(8,128)(2,1)} async-done(((bf16[1024,1024]{1,0:T(8,128)(2,1)}), bf16[128,1024]{1,0:T(8,128)(2,1)}) %reduce-scatter.3.cloned.1.call-update) | async-done | bytes 262160 | tf_op jit(solution)/shard_map/reduce_scatter | solution.py:425
  393.2 6.7 %collective-permute-done.67 = bf16[196,1024]{1,0:T(8,128)(2,1)S(1)} collective-permute-done((bf16[196,1024]{1,0:T(8,128)(2,1)S(1)}, bf16[196,1024]{1,0:T(8,128)(2,1)S(1)}, u32[]{:S(2)}, u32[]{:S(2)}) %collective-permute-start.67) | collective-permute-done | bytes 401440 | tf_op jit(solution)/shard_map/ppermute | solution.py:33
  400.4 26.8 %all_to_all.24 = bf16[8,128,1024]{2,1,0:T(8,128)(2,1)} all-to-all(bf16[8,128,1024]{2,1,0:T(8,128)(2,1)S(1)} %broadcast_in_dim.111), channel_id=1, replica_groups=mesh['section'=2,'zlo'=2,'x'=4,'core'=2,'tensor'=4] {'zlo','x'}, dimensions={0} | all-to-all | bytes 4194304 | tf_op jit(solution)/shard_map/all_to_all | solution.py:436
  427.1 6.2 %collective-permute-start.73 = (bf16[1024,1024]{1,0:T(8,128)(2,1)}, bf16[1024,1024]{1,0:T(8,128)(2,1)}, u32[]{:S(2)}, u32[]{:S(2)}) collective-permute-start(bf16[1024,1024]{1,0:T(8,128)(2,1)} %bitcast.36), channel_id=1, source_target_pairs={{0,4},{4,0},{1,5},{5,1},{2,6},{6,2},{3,7},{7,3},{8,12},{12,8},{9,1... | collective-permute-start | bytes 6291464 | tf_op jit(solution)/shard_map/ppermute | solution.py:29
  433.3 2.9 collective-permute-start.70
  441.4 5.4 %collective-permute-done.71 = bf16[128,1024]{1,0:T(8,128)(2,1)S(1)} collective-permute-done((bf16[128,1024]{1,0:T(8,128)(2,1)}, bf16[128,1024]{1,0:T(8,128)(2,1)S(1)}, u32[]{:S(2)}, u32[]{:S(2)}) %collective-permute-start.71) | collective-permute-done | bytes 262176 | tf_op jit(solution)/shard_map/ppermute | solution.py:33
  446.8 5.6 %collective-permute-done.72 = bf16[128,1024]{1,0:T(8,128)(2,1)S(1)} collective-permute-done((bf16[128,1024]{1,0:T(8,128)(2,1)}, bf16[128,1024]{1,0:T(8,128)(2,1)S(1)}, u32[]{:S(2)}, u32[]{:S(2)}) %collective-permute-start.72) | collective-permute-done | bytes 262176 | tf_op jit(solution)/shard_map/ppermute | solution.py:33
  453.5 4.3 all-to-all-start.2
  462.9 2.8 maximum_convert_fusion
  465.7 8.6 %all-to-all-done.2 = bf16[8,272,256]{2,1,0:T(8,128)(2,1)} async-done(((bf16[8,272,256]{2,1,0:T(8,128)(2,1)}), bf16[8,272,256]{2,1,0:T(8,128)(2,1)}, u32[]{:S(2)}, u32[]{:S(2)}) %all-to-all-start.2) | async-done | bytes 1114144 | tf_op jit(solution)/shard_map/all_to_all | solution.py:436
  (560 shorter events, 192.2 us)
Async XLA Ops:
  7.2 324.1 %reduce-scatter.5.cloned.1.call-start = ((), (), s32[]{:S(2)}) async-start(), calls=%async_computation.6 | async-start | bytes 2359296 | tf_op jit(solution)/shard_map/reduce_scatter | solution.py:425
  8.4 23.7 %collective-permute-start.1 = (bf16[128,1024]{1,0:T(8,128)(2,1)S(1)}, bf16[128,1024]{1,0:T(8,128)(2,1)S(1)}, u32[]{:S(2)}, u32[]{:S(2)}) collective-permute-start(bf16[128,1024]{1,0:T(8,128)(2,1)S(1)} %get-tuple-element.229), channel_id=1, source_target_pairs={{0,1},{1,2},{2,3},{3,0},{4,5},{5,6},{6,7},{7,4},{8,9},{9,10},{10,1... | collective-permute-start | bytes 786440 | tf_op jit(solution)/shard_map/ppermute | solution.py:25
  10.6 21.6 %collective-permute-start = (bf16[128,1024]{1,0:T(8,128)(2,1)S(1)}, bf16[128,1024]{1,0:T(8,128)(2,1)S(1)}, u32[]{:S(2)}, u32[]{:S(2)}) collective-permute-start(bf16[128,1024]{1,0:T(8,128)(2,1)S(1)} %get-tuple-element.229), channel_id=1, source_target_pairs={{0,3},{1,0},{2,1},{3,2},{4,7},{5,4},{6,5},{7,6},{8,11},{9,8},{10,9... | collective-permute-start | bytes 786440 | tf_op jit(solution)/shard_map/ppermute | solution.py:25
  12.1 22.2 %collective-permute-start.2 = (bf16[128,1024]{1,0:T(8,128)(2,1)S(1)}, bf16[128,1024]{1,0:T(8,128)(2,1)S(1)}, u32[]{:S(2)}, u32[]{:S(2)}) collective-permute-start(bf16[128,1024]{1,0:T(8,128)(2,1)S(1)} %get-tuple-element.229), channel_id=1, source_target_pairs={{0,2},{1,3},{2,0},{3,1},{4,6},{5,7},{6,4},{7,5},{8,10},{9,11},{10,... | collective-permute-start | bytes 786440 | tf_op jit(solution)/shard_map/ppermute | solution.py:25
  14.7 13.1 %collective-permute-start.4 = (bf16[128,1024]{1,0:T(8,128)(2,1)S(1)}, bf16[128,1024]{1,0:T(8,128)(2,1)S(1)}, u32[]{:S(2)}, u32[]{:S(2)}) collective-permute-start(bf16[128,1024]{1,0:T(8,128)(2,1)S(1)} %constant_dynamic-slice_fusion.3), channel_id=1, source_target_pairs={{0,96},{32,64},{64,32},{96,0},{1,97},{33,65},{65,33},{97,1},{2,98}... | collective-permute-start | bytes 786440 | tf_op jit(solution)/shard_map/ppermute | solution.py:37
  25.0 18.8 %collective-permute-start.3 = (bf16[1536,256]{1,0:T(8,128)(2,1)}, bf16[1536,256]{1,0:T(8,128)(2,1)}, u32[]{:S(2)}, u32[]{:S(2)}) collective-permute-start(bf16[1536,256]{1,0:T(8,128)(2,1)} %constant_dynamic-slice_fusion.4), channel_id=1, source_target_pairs={{0,96},{32,64},{64,32},{96,0},{1,97},{33,65},{65,33},{97,1},{2,98}... | collective-permute-start | bytes 2359304 | tf_op jit(solution)/shard_map/ppermute | solution.py:37
  32.1 34.8 %collective-permute-start.13 = (bf16[328,1024]{1,0:T(8,128)(2,1)}, bf16[328,1024]{1,0:T(8,128)(2,1)}, u32[]{:S(2)}, u32[]{:S(2)}) collective-permute-start(bf16[328,1024]{1,0:T(8,128)(2,1)} %constant_dynamic-slice_fusion.2), channel_id=1, source_target_pairs={{0,96},{32,64},{64,32},{96,0},{1,97},{33,65},{65,33},{97,1},{2,98}... | collective-permute-start | bytes 2015240 | tf_op jit(solution)/shard_map/ppermute | solution.py:37
  64.2 19.7 %collective-permute-start.10 = (bf16[128,1024]{1,0:T(8,128)(2,1)S(1)}, bf16[128,1024]{1,0:T(8,128)(2,1)S(1)}, u32[]{:S(2)}, u32[]{:S(2)}) collective-permute-start(bf16[128,1024]{1,0:T(8,128)(2,1)S(1)} %get-tuple-element.313), channel_id=1, source_target_pairs={{0,3},{1,0},{2,1},{3,2},{4,7},{5,4},{6,5},{7,6},{8,11},{9,8},{10,9... | collective-permute-start | bytes 786440 | tf_op jit(solution)/shard_map/ppermute | solution.py:25
  65.0 18.9 %collective-permute-start.9 = (bf16[128,1024]{1,0:T(8,128)(2,1)S(1)}, bf16[128,1024]{1,0:T(8,128)(2,1)S(1)}, u32[]{:S(2)}, u32[]{:S(2)}) collective-permute-start(bf16[128,1024]{1,0:T(8,128)(2,1)S(1)} %get-tuple-element.312), channel_id=1, source_target_pairs={{0,1},{1,2},{2,3},{3,0},{4,5},{5,6},{6,7},{7,4},{8,9},{9,10},{10,1... | collective-permute-start | bytes 786440 | tf_op jit(solution)/shard_map/ppermute | solution.py:25
  65.7 18.2 %collective-permute-start.8 = (bf16[128,1024]{1,0:T(8,128)(2,1)S(1)}, bf16[128,1024]{1,0:T(8,128)(2,1)S(1)}, u32[]{:S(2)}, u32[]{:S(2)}) collective-permute-start(bf16[128,1024]{1,0:T(8,128)(2,1)S(1)} %get-tuple-element.104), channel_id=1, source_target_pairs={{0,2},{1,3},{2,0},{3,1},{4,6},{5,7},{6,4},{7,5},{8,10},{9,11},{10,... | collective-permute-start | bytes 786440 | tf_op jit(solution)/shard_map/ppermute | solution.py:25
  67.0 20.3 %collective-permute-start.15 = (bf16[328,1024]{1,0:T(8,128)(2,1)S(1)}, bf16[328,1024]{1,0:T(8,128)(2,1)S(1)}, u32[]{:S(2)}, u32[]{:S(2)}) collective-permute-start(bf16[328,1024]{1,0:T(8,128)(2,1)S(1)} %constant_dynamic-slice_fusion.1), channel_id=1, source_target_pairs={{0,96},{32,64},{64,32},{96,0},{1,97},{33,65},{65,33},{97,1},{2,98}... | collective-permute-start | bytes 2015240 | tf_op jit(solution)/shard_map/ppermute | solution.py:37
  70.0 25.3 %collective-permute-start.14 = (bf16[328,1024]{1,0:T(8,128)(2,1)}, bf16[328,1024]{1,0:T(8,128)(2,1)S(1)}, u32[]{:S(2)}, u32[]{:S(2)}) collective-permute-start(bf16[328,1024]{1,0:T(8,128)(2,1)} %collective-permute-done.13), channel_id=1, source_target_pairs={{0,4},{4,0},{1,5},{5,1},{2,6},{6,2},{3,7},{7,3},{8,12},{12,8},{9,1... | collective-permute-start | bytes 2015240 | tf_op jit(solution)/shard_map/ppermute | solution.py:29
  87.4 17.3 %collective-permute-start.17 = (bf16[328,1024]{1,0:T(8,128)(2,1)S(1)}, bf16[328,1024]{1,0:T(8,128)(2,1)S(1)}, u32[]{:S(2)}, u32[]{:S(2)}) collective-permute-start(bf16[328,1024]{1,0:T(8,128)(2,1)S(1)} %constant_dynamic-slice_fusion), channel_id=1, source_target_pairs={{0,96},{32,64},{64,32},{96,0},{1,97},{33,65},{65,33},{97,1},{2,98}... | collective-permute-start | bytes 2015240 | tf_op jit(solution)/shard_map/ppermute | solution.py:37
  87.6 18.6 %collective-permute-start.16 = (bf16[328,1024]{1,0:T(8,128)(2,1)S(1)}, bf16[328,1024]{1,0:T(8,128)(2,1)S(1)}, u32[]{:S(2)}, u32[]{:S(2)}) collective-permute-start(bf16[328,1024]{1,0:T(8,128)(2,1)S(1)} %collective-permute-done.15), channel_id=1, source_target_pairs={{0,4},{4,0},{1,5},{5,1},{2,6},{6,2},{3,7},{7,3},{8,12},{12,8},{9,1... | collective-permute-start | bytes 2015240 | tf_op jit(solution)/shard_map/ppermute | solution.py:29
  117.2 11.4 %collective-permute-start.22 = (bf16[128,1024]{1,0:T(8,128)(2,1)}, bf16[128,1024]{1,0:T(8,128)(2,1)}, u32[]{:S(2)}, u32[]{:S(2)}) collective-permute-start(bf16[128,1024]{1,0:T(8,128)(2,1)} %get-tuple-element.311), channel_id=1, source_target_pairs={{0,3},{1,0},{2,1},{3,2},{4,7},{5,4},{6,5},{7,6},{8,11},{9,8},{10,9... | collective-permute-start | bytes 786440 | tf_op jit(solution)/shard_map/ppermute | solution.py:25
  117.5 11.1 %collective-permute-start.21 = (bf16[128,1024]{1,0:T(8,128)(2,1)}, bf16[128,1024]{1,0:T(8,128)(2,1)}, u32[]{:S(2)}, u32[]{:S(2)}) collective-permute-start(bf16[128,1024]{1,0:T(8,128)(2,1)} %get-tuple-element.310), channel_id=1, source_target_pairs={{0,1},{1,2},{2,3},{3,0},{4,5},{5,6},{6,7},{7,4},{8,9},{9,10},{10,1... | collective-permute-start | bytes 786440 | tf_op jit(solution)/shard_map/ppermute | solution.py:25
  154.7 20.0 %collective-permute-start.32 = (bf16[128,1024]{1,0:T(8,128)(2,1)S(1)}, bf16[128,1024]{1,0:T(8,128)(2,1)S(1)}, u32[]{:S(2)}, u32[]{:S(2)}) collective-permute-start(bf16[128,1024]{1,0:T(8,128)(2,1)S(1)} %select_bitcast_fusion.9), channel_id=1, source_target_pairs={{0,1},{1,2},{2,3},{3,0},{4,5},{5,6},{6,7},{7,4},{8,9},{9,10},{10,1... | collective-permute-start | bytes 786440 | tf_op jit(solution)/shard_map/ppermute | solution.py:25
  156.8 17.9 %collective-permute-start.31 = (bf16[128,1024]{1,0:T(8,128)(2,1)S(1)}, bf16[128,1024]{1,0:T(8,128)(2,1)S(1)}, u32[]{:S(2)}, u32[]{:S(2)}) collective-permute-start(bf16[128,1024]{1,0:T(8,128)(2,1)S(1)} %select_bitcast_fusion.9), channel_id=1, source_target_pairs={{0,3},{1,0},{2,1},{3,2},{4,7},{5,4},{6,5},{7,6},{8,11},{9,8},{10,9... | collective-permute-start | bytes 786440 | tf_op jit(solution)/shard_map/ppermute | solution.py:25
  157.4 17.3 %collective-permute-start.33 = (bf16[128,1024]{1,0:T(8,128)(2,1)S(1)}, bf16[128,1024]{1,0:T(8,128)(2,1)S(1)}, u32[]{:S(2)}, u32[]{:S(2)}) collective-permute-start(bf16[128,1024]{1,0:T(8,128)(2,1)S(1)} %select_bitcast_fusion.9), channel_id=1, source_target_pairs={{0,2},{1,3},{2,0},{3,1},{4,6},{5,7},{6,4},{7,5},{8,10},{9,11},{10,... | collective-permute-start | bytes 786440 | tf_op jit(solution)/shard_map/ppermute | solution.py:25
  164.1 21.8 %collective-permute-start.30 = (bf16[128,1024]{1,0:T(8,128)(2,1)S(1)}, bf16[128,1024]{1,0:T(8,128)(2,1)S(1)}, u32[]{:S(2)}, u32[]{:S(2)}) collective-permute-start(bf16[128,1024]{1,0:T(8,128)(2,1)S(1)} %multiply_convert_fusion.4), channel_id=1, source_target_pairs={{0,1},{1,2},{2,3},{3,0},{4,5},{5,6},{6,7},{7,4},{8,9},{9,10},{10,1... | collective-permute-start | bytes 786440 | tf_op jit(solution)/shard_map/ppermute | solution.py:25
  164.2 21.7 %collective-permute-start.29 = (bf16[128,1024]{1,0:T(8,128)(2,1)S(1)}, bf16[128,1024]{1,0:T(8,128)(2,1)S(1)}, u32[]{:S(2)}, u32[]{:S(2)}) collective-permute-start(bf16[128,1024]{1,0:T(8,128)(2,1)S(1)} %multiply_convert_fusion.4), channel_id=1, source_target_pairs={{0,3},{1,0},{2,1},{3,2},{4,7},{5,4},{6,5},{7,6},{8,11},{9,8},{10,9... | collective-permute-start | bytes 786440 | tf_op jit(solution)/shard_map/ppermute | solution.py:25
  174.7 19.2 %collective-permute-start.34 = (bf16[128,1024]{1,0:T(8,128)(2,1)S(1)}, bf16[128,1024]{1,0:T(8,128)(2,1)S(1)}, u32[]{:S(2)}, u32[]{:S(2)}) collective-permute-start(bf16[128,1024]{1,0:T(8,128)(2,1)S(1)} %multiply_convert_fusion.4), channel_id=1, source_target_pairs={{0,2},{1,3},{2,0},{3,1},{4,6},{5,7},{6,4},{7,5},{8,10},{9,11},{10,... | collective-permute-start | bytes 786440 | tf_op jit(solution)/shard_map/ppermute | solution.py:25
  205.0 13.3 %collective-permute-start.39 = (bf16[128,1024]{1,0:T(8,128)(2,1)S(1)}, bf16[128,1024]{1,0:T(8,128)(2,1)S(1)}, u32[]{:S(2)}, u32[]{:S(2)}) collective-permute-start(bf16[128,1024]{1,0:T(8,128)(2,1)S(1)} %get-tuple-element.236), channel_id=1, source_target_pairs={{0,1},{1,2},{2,3},{3,0},{4,5},{5,6},{6,7},{7,4},{8,9},{9,10},{10,1... | collective-permute-start | bytes 786440 | tf_op jit(solution)/shard_map/ppermute | solution.py:25
  205.1 13.2 %collective-permute-start.38 = (bf16[128,1024]{1,0:T(8,128)(2,1)S(1)}, bf16[128,1024]{1,0:T(8,128)(2,1)S(1)}, u32[]{:S(2)}, u32[]{:S(2)}) collective-permute-start(bf16[128,1024]{1,0:T(8,128)(2,1)S(1)} %get-tuple-element.236), channel_id=1, source_target_pairs={{0,3},{1,0},{2,1},{3,2},{4,7},{5,4},{6,5},{7,6},{8,11},{9,8},{10,9... | collective-permute-start | bytes 786440 | tf_op jit(solution)/shard_map/ppermute | solution.py:25
  209.9 43.2 %collective-permute-start.48 = (bf16[328,1024]{1,0:T(8,128)(2,1)}, bf16[328,1024]{1,0:T(8,128)(2,1)}, u32[]{:S(2)}, u32[]{:S(2)}) collective-permute-start(bf16[328,1024]{1,0:T(8,128)(2,1)} %convolution_convert_fusion.7), channel_id=1, source_target_pairs={{0,4},{4,0},{1,5},{5,1},{2,6},{6,2},{3,7},{7,3},{8,12},{12,8},{9,1... | collective-permute-start | bytes 2015240 | tf_op jit(solution)/shard_map/ppermute | solution.py:29
  217.4 42.7 %collective-permute-start.47 = (bf16[656,1024]{1,0:T(8,128)(2,1)}, bf16[656,1024]{1,0:T(8,128)(2,1)}, u32[]{:S(2)}, u32[]{:S(2)}) collective-permute-start(bf16[656,1024]{1,0:T(8,128)(2,1)} %convolution_convert_fusion.1), channel_id=1, source_target_pairs={{0,4},{4,0},{1,5},{5,1},{2,6},{6,2},{3,7},{7,3},{8,12},{12,8},{9,1... | collective-permute-start | bytes 4030472 | tf_op jit(solution)/shard_map/ppermute | solution.py:29
  226.6 13.5 %collective-permute-start.41 = (bf16[128,1024]{1,0:T(8,128)(2,1)S(1)}, bf16[128,1024]{1,0:T(8,128)(2,1)S(1)}, u32[]{:S(2)}, u32[]{:S(2)}) collective-permute-start(bf16[128,1024]{1,0:T(8,128)(2,1)S(1)} %get-tuple-element.137), channel_id=1, source_target_pairs={{0,2},{1,3},{2,0},{3,1},{4,6},{5,7},{6,4},{7,5},{8,10},{9,11},{10,... | collective-permute-start | bytes 786440 | tf_op jit(solution)/shard_map/ppermute | solution.py:25
  241.0 14.2 %collective-permute-start.45 = (bf16[128,1024]{1,0:T(8,128)(2,1)S(1)}, bf16[128,1024]{1,0:T(8,128)(2,1)}, u32[]{:S(2)}, u32[]{:S(2)}) collective-permute-start(bf16[128,1024]{1,0:T(8,128)(2,1)S(1)} %add_convert_fusion.9), channel_id=1, source_target_pairs={{0,1},{1,2},{2,3},{3,0},{4,5},{5,6},{6,7},{7,4},{8,9},{9,10},{10,1... | collective-permute-start | bytes 786440 | tf_op jit(solution)/shard_map/ppermute | solution.py:25
  241.1 14.4 %collective-permute-start.44 = (bf16[128,1024]{1,0:T(8,128)(2,1)S(1)}, bf16[128,1024]{1,0:T(8,128)(2,1)}, u32[]{:S(2)}, u32[]{:S(2)}) collective-permute-start(bf16[128,1024]{1,0:T(8,128)(2,1)S(1)} %add_convert_fusion.9), channel_id=1, source_target_pairs={{0,3},{1,0},{2,1},{3,2},{4,7},{5,4},{6,5},{7,6},{8,11},{9,8},{10,9... | collective-permute-start | bytes 786440 | tf_op jit(solution)/shard_map/ppermute | solution.py:25
  246.2 11.4 %collective-permute-start.59 = (bf16[1024,256]{1,0:T(8,128)(2,1)}, bf16[1024,256]{1,0:T(8,128)(2,1)}, u32[]{:S(2)}, u32[]{:S(2)}) collective-permute-start(bf16[1024,256]{1,0:T(8,128)(2,1)} %convolution_convert_fusion.9), channel_id=1, source_target_pairs={{0,4},{4,0},{1,5},{5,1},{2,6},{6,2},{3,7},{7,3},{8,12},{12,8},{9,1... | collective-permute-start | bytes 1572872 | tf_op jit(solution)/shard_map/ppermute | solution.py:29
  253.1 11.0 %collective-permute-start.46 = (bf16[128,1024]{1,0:T(8,128)(2,1)S(1)}, bf16[128,1024]{1,0:T(8,128)(2,1)}, u32[]{:S(2)}, u32[]{:S(2)}) collective-permute-start(bf16[128,1024]{1,0:T(8,128)(2,1)S(1)} %add_convert_fusion.9), channel_id=1, source_target_pairs={{0,2},{1,3},{2,0},{3,1},{4,6},{5,7},{6,4},{7,5},{8,10},{9,11},{10,... | collective-permute-start | bytes 786440 | tf_op jit(solution)/shard_map/ppermute | solution.py:25
  255.2 23.5 %collective-permute-start.60 = (bf16[1024,256]{1,0:T(8,128)(2,1)}, bf16[1024,256]{1,0:T(8,128)(2,1)S(1)}, u32[]{:S(2)}, u32[]{:S(2)}) collective-permute-start(bf16[1024,256]{1,0:T(8,128)(2,1)} %convolution_convert_fusion.8), channel_id=1, source_target_pairs={{0,4},{4,0},{1,5},{5,1},{2,6},{6,2},{3,7},{7,3},{8,12},{12,8},{9,1... | collective-permute-start | bytes 1572872 | tf_op jit(solution)/shard_map/ppermute | solution.py:29
  275.6 12.1 %collective-permute-start.49 = (bf16[128,1024]{1,0:T(8,128)(2,1)}, bf16[128,1024]{1,0:T(8,128)(2,1)}, u32[]{:S(2)}, u32[]{:S(2)}) collective-permute-start(bf16[128,1024]{1,0:T(8,128)(2,1)} %convolution_convert_fusion.14), channel_id=1, source_target_pairs={{0,2},{1,3},{2,0},{3,1},{4,6},{5,7},{6,4},{7,5},{8,10},{9,11},{10,... | collective-permute-start | bytes 786440 | tf_op jit(solution)/shard_map/ppermute | solution.py:25
  279.7 108.4 %reduce-scatter.3.cloned.1.call-start = ((), (), s32[]{:S(2)}) async-start(), calls=%async_computation.5 | async-start | bytes 2359296 | tf_op jit(solution)/shard_map/reduce_scatter | solution.py:425
  291.8 13.4 %collective-permute-start.53 = (bf16[128,1024]{1,0:T(8,128)(2,1)S(1)}, bf16[128,1024]{1,0:T(8,128)(2,1)S(1)}, u32[]{:S(2)}, u32[]{:S(2)}) collective-permute-start(bf16[128,1024]{1,0:T(8,128)(2,1)S(1)} %get-tuple-element.230), channel_id=1, source_target_pairs={{0,1},{1,2},{2,3},{3,0},{4,5},{5,6},{6,7},{7,4},{8,9},{9,10},{10,1... | collective-permute-start | bytes 786440 | tf_op jit(solution)/shard_map/ppermute | solution.py:25
  291.8 13.4 %collective-permute-start.52 = (bf16[128,1024]{1,0:T(8,128)(2,1)S(1)}, bf16[128,1024]{1,0:T(8,128)(2,1)S(1)}, u32[]{:S(2)}, u32[]{:S(2)}) collective-permute-start(bf16[128,1024]{1,0:T(8,128)(2,1)S(1)} %get-tuple-element.230), channel_id=1, source_target_pairs={{0,3},{1,0},{2,1},{3,2},{4,7},{5,4},{6,5},{7,6},{8,11},{9,8},{10,9... | collective-permute-start | bytes 786440 | tf_op jit(solution)/shard_map/ppermute | solution.py:25
  294.4 10.8 %collective-permute-start.54 = (bf16[128,1024]{1,0:T(8,128)(2,1)S(1)}, bf16[128,1024]{1,0:T(8,128)(2,1)S(1)}, u32[]{:S(2)}, u32[]{:S(2)}) collective-permute-start(bf16[128,1024]{1,0:T(8,128)(2,1)S(1)} %get-tuple-element.230), channel_id=1, source_target_pairs={{0,2},{1,3},{2,0},{3,1},{4,6},{5,7},{6,4},{7,5},{8,10},{9,11},{10,... | collective-permute-start | bytes 786440 | tf_op jit(solution)/shard_map/ppermute | solution.py:25
  299.3 18.5 %collective-permute-start.56 = (bf16[328,1024]{1,0:T(8,128)(2,1)S(1)}, bf16[328,1024]{1,0:T(8,128)(2,1)S(1)}, u32[]{:S(2)}, u32[]{:S(2)}) collective-permute-start(bf16[328,1024]{1,0:T(8,128)(2,1)S(1)} %convolution_convert_fusion.6), channel_id=1, source_target_pairs={{0,4},{4,0},{1,5},{5,1},{2,6},{6,2},{3,7},{7,3},{8,12},{12,8},{9,1... | collective-permute-start | bytes 2015240 | tf_op jit(solution)/shard_map/ppermute | solution.py:29
  301.2 19.3 %collective-permute-start.55 = (bf16[656,1024]{1,0:T(8,128)(2,1)S(1)}, bf16[656,1024]{1,0:T(8,128)(2,1)S(1)}, u32[]{:S(2)}, u32[]{:S(2)}) collective-permute-start(bf16[656,1024]{1,0:T(8,128)(2,1)S(1)} %convolution_convert_fusion), channel_id=1, source_target_pairs={{0,4},{4,0},{1,5},{5,1},{2,6},{6,2},{3,7},{7,3},{8,12},{12,8},{9,1... | collective-permute-start | bytes 4030472 | tf_op jit(solution)/shard_map/ppermute | solution.py:29
  326.2 18.5 %collective-permute-start.66 = (bf16[128,1024]{1,0:T(8,128)(2,1)}, bf16[128,1024]{1,0:T(8,128)(2,1)S(1)}, u32[]{:S(2)}, u32[]{:S(2)}) collective-permute-start(bf16[128,1024]{1,0:T(8,128)(2,1)} %get-tuple-element.295), channel_id=1, source_target_pairs={{0,3},{1,0},{2,1},{3,2},{4,7},{5,4},{6,5},{7,6},{8,11},{9,8},{10,9... | collective-permute-start | bytes 786440 | tf_op jit(solution)/shard_map/ppermute | solution.py:25
  328.9 15.8 %collective-permute-start.65 = (bf16[128,1024]{1,0:T(8,128)(2,1)}, bf16[128,1024]{1,0:T(8,128)(2,1)}, u32[]{:S(2)}, u32[]{:S(2)}) collective-permute-start(bf16[128,1024]{1,0:T(8,128)(2,1)} %get-tuple-element.294), channel_id=1, source_target_pairs={{0,1},{1,2},{2,3},{3,0},{4,5},{5,6},{6,7},{7,4},{8,9},{9,10},{10,1... | collective-permute-start | bytes 786440 | tf_op jit(solution)/shard_map/ppermute | solution.py:25
  330.1 14.6 %collective-permute-start.64 = (bf16[128,1024]{1,0:T(8,128)(2,1)}, bf16[128,1024]{1,0:T(8,128)(2,1)}, u32[]{:S(2)}, u32[]{:S(2)}) collective-permute-start(bf16[128,1024]{1,0:T(8,128)(2,1)} %convolution_convert_fusion.12), channel_id=1, source_target_pairs={{0,2},{1,3},{2,0},{3,1},{4,6},{5,7},{6,4},{7,5},{8,10},{9,11},{10,... | collective-permute-start | bytes 786440 | tf_op jit(solution)/shard_map/ppermute | solution.py:25
  335.4 53.7 %all-to-all-start = ((bf16[8,544,256]{2,1,0:T(8,128)(2,1)}), bf16[8,544,256]{2,1,0:T(8,128)(2,1)}, u32[]{:S(2)}, u32[]{:S(2)}) async-start(bf16[8,544,256]{2,1,0:T(8,128)(2,1)} %pad_maximum_fusion.1), calls=%async_computation.2 | async-start | bytes 4456448 | tf_op jit(solution)/shard_map/all_to_all | solution.py:429
  339.9 14.7 %collective-permute-start.61 = (bf16[128,1024]{1,0:T(8,128)(2,1)S(1)}, bf16[128,1024]{1,0:T(8,128)(2,1)S(1)}, u32[]{:S(2)}, u32[]{:S(2)}) collective-permute-start(bf16[128,1024]{1,0:T(8,128)(2,1)S(1)} %copy-done.11), channel_id=1, source_target_pairs={{0,2},{1,3},{2,0},{3,1},{4,6},{5,7},{6,4},{7,5},{8,10},{9,11},{10,... | collective-permute-start | bytes 786440 | tf_op jit(solution)/shard_map/ppermute | solution.py:25
  342.0 11.2 %collective-permute-start.63 = (bf16[128,1024]{1,0:T(8,128)(2,1)S(1)}, bf16[128,1024]{1,0:T(8,128)(2,1)S(1)}, u32[]{:S(2)}, u32[]{:S(2)}) collective-permute-start(bf16[128,1024]{1,0:T(8,128)(2,1)S(1)} %get-tuple-element.297), channel_id=1, source_target_pairs={{0,3},{1,0},{2,1},{3,2},{4,7},{5,4},{6,5},{7,6},{8,11},{9,8},{10,9... | collective-permute-start | bytes 786440 | tf_op jit(solution)/shard_map/ppermute | solution.py:25
  427.1 30.7 %collective-permute-start.73 = (bf16[1024,1024]{1,0:T(8,128)(2,1)}, bf16[1024,1024]{1,0:T(8,128)(2,1)}, u32[]{:S(2)}, u32[]{:S(2)}) collective-permute-start(bf16[1024,1024]{1,0:T(8,128)(2,1)} %bitcast.36), channel_id=1, source_target_pairs={{0,4},{4,0},{1,5},{5,1},{2,6},{6,2},{3,7},{7,3},{8,12},{12,8},{9,1... | collective-permute-start | bytes 6291464 | tf_op jit(solution)/shard_map/ppermute | solution.py:29
  440.2 12.3 %collective-permute-start.72 = (bf16[128,1024]{1,0:T(8,128)(2,1)}, bf16[128,1024]{1,0:T(8,128)(2,1)S(1)}, u32[]{:S(2)}, u32[]{:S(2)}) collective-permute-start(bf16[128,1024]{1,0:T(8,128)(2,1)} %get-tuple-element.222), channel_id=1, source_target_pairs={{0,64},{64,0},{1,65},{65,1},{2,66},{66,2},{3,67},{67,3},{4,68},{68... | collective-permute-start | bytes 786440 | tf_op jit(solution)/shard_map/ppermute | solution.py:33
  453.5 20.8 %all-to-all-start.2 = ((bf16[8,272,256]{2,1,0:T(8,128)(2,1)}), bf16[8,272,256]{2,1,0:T(8,128)(2,1)}, u32[]{:S(2)}, u32[]{:S(2)}) async-start(bf16[8,272,256]{2,1,0:T(8,128)(2,1)} %broadcast_in_dim.114), calls=%async_computation.4 | async-start | bytes 2228224 | tf_op jit(solution)/shard_map/all_to_all | solution.py:436
  (131 other events, 1257.1 us)
Sparse Core Ops, SparseCore 0:
  279.8 35.3 reduce-scatter.4
  323.3 64.7 reduce-scatter.2

commit v3 on v2

--- a/solution.py
+++ b/solution.py
@@ -535,7 +535,7 @@
         lambda gate: (ffn_pack0(gate), ffn1),
     )
     in0 = in0.astype(bf16)
-    ffn0 = reduce_part(ffn_pack0)
+    ffn0 = reduce_part_now(ffn_pack0)
     attn_pack1 = attn_grads1(in1, [gain_first1, gain_mid1])
     attn_pack0 = attn_grads0((), [gain_before(), gain_mid0])
     out1_terms = out1_of(ffn_pack0)
@@ -544,26 +544,25 @@
     packs = [pack.reshape(8, -1, attn_width) for pack in (attn_pack0, attn_pack1)]
     attn_rows = packs[0].shape[1]
     attn_both = reduce_part_now(joined(packs, 1).reshape(-1, attn_width))
-    part0 = joined([ffn0, attn_both[:attn_rows].reshape(-1, model_width)])
-    part1 = joined([ffn1, attn_both[attn_rows:].reshape(-1, model_width)])
+    gain_start = 2 * model_width % attn_rows
+    holds_gains = lax.axis_index(("zlo", "x")) == 2 * model_width // attn_rows
+    attn_both = attn_both.reshape(2, attn_rows, attn_width)
+    gain_rows = attn_both[:, gain_start : gain_start + 8]
+    gain_sums = sum_tensor(gain_rows.astype(f32)).astype(bf16)
+    gain_rows = jnp.where(holds_gains, gain_sums, gain_rows)
+    attn_both = joined(
+        [attn_both[:, :gain_start], gain_rows, attn_both[:, gain_start + 8 :]], 1
+    )
+    got_out = swap_section(jnp.where(is_first, out1, out0))
+    got_in = swap_section(jnp.where(is_first, in1, in0))
+    part0 = joined([ffn0, attn_both[0].reshape(-1, model_width)])
+    part1 = joined([ffn1, attn_both[1].reshape(-1, model_width)])
     own_part, sent_part = pick_sections(is_first, part0, part1)
-    sent_part = after_all(sent_part, in0, out1)
+    sent_part = after_all(sent_part, got_in, got_out)
     part = (own_part.astype(f32) + swap_section(sent_part).astype(f32)).astype(bf16)
     ffn_rows = ffn0.shape[0]
     ffn_half = spread_part(part[:ffn_rows])
-    got_out = swap_section(jnp.where(is_first, out1, out0))
-    got_in = swap_section(jnp.where(is_first, in1, in0))
-    attn_part = part[ffn_rows:].reshape(-1, attn_width)
-    gain_start = 2 * model_width % attn_rows
-    gain_span = slice(gain_start, gain_start + 8)
-    gain_rows = attn_part[gain_span]
-    holds_gains = lax.axis_index(("zlo", "x")) == 2 * model_width // attn_rows
-    gain_rows = jnp.where(
-        holds_gains, sum_tensor(gain_rows.astype(f32)).astype(bf16), gain_rows
-    )
-    attn_part = joined([attn_part[:gain_start], gain_rows, attn_part[gain_start + 8 :]])
-    attn_part, got_out, got_in = after_all((attn_part, got_out, got_in), ffn_half)
-    attn_part = after_all(attn_part, got_out, got_in)
+    attn_part = after_all(part[ffn_rows:].reshape(-1, attn_width), ffn_half)
     attn_half = spread_part(attn_part)
     is_core0 = lax.axis_index("core") == 0
 

time: 502 us -> 495 us (0.986)
  waiting for transfers between devices: 150 us -> 143 us
    reduce_scatter x2 -> x1, waiting for transfers between devices: 32 us -> 0.01 us  [reduce_part(): lax.psum_scatter(grads, ('zlo', 'x'), scatter_dimension=0, tiled=True)]
    all_to_all x1 -> x2, waiting for transfers between devices: 0.01 us -> 22.1 us  [reduce_part_now(): pieces = lax.all_to_all(grads, ('zlo', 'x'), 0, 0, tiled=True)]
    ppermute x15, starting transfers between devices: 46 us -> 34.3 us  [swap_core(): return lax.ppermute(block, 'core', [(0, 1), (1, 0)])]
    all_to_all x1 -> x2, starting transfers between devices: 4.49 us -> 11.3 us  [reduce_part_now(): pieces = lax.all_to_all(grads, ('zlo', 'x'), 0, 0, tiled=True)]
    unnamed x217 -> x218, local copies, waits for them, and re-layouts: 12.8 us -> 9.41 us
  transfers between devices with their start and end apart: 79 -> 79, of which waited for: 25 -> 32; matrix products, arithmetic and copies ran while one was open for 24% -> 26% of each run, Pallas kernels for 4% -> 4%
where the time goes in v3:
time: 495 us; the launch traced here: 486 us
  waiting for transfers between devices  143 us (29%)
  starting transfers between devices  129 us (26%)
  other arithmetic  72 us (15%)
  matrix products  42.1 us (9%)
  local copies, waits for them, and re-layouts  32.9 us (7%)
  blocking collectives  27.1 us (5%)
  Pallas kernels  23.1 us (5%)
  between operations  16.6 us (3%)
    ppermute x51, waiting for transfers between devices, around(): lax.ppermute(block, axis, [(i, (i + distance) % count) for i in range(cou...  84.6 us
    ppermute x51, starting transfers between devices, around(): lax.ppermute(block, axis, [(i, (i + distance) % count) for i in range(cou...  61.5 us
    ppermute x15, starting transfers between devices, swap_core(): return lax.ppermute(block, 'core', [(0, 1), (1, 0)])  34.3 us
    all_to_all x1, blocking collectives, spread_part(): return lax.all_to_all(copies, ('zlo', 'x'), 0, 0, tiled=True)  27.1 us
    pallas_call x4, Pallas kernels, whole_call(): pl.pallas_call(kernel, out_shape=[jax.ShapeDtypeStruct(*shape) for shape...  23.1 us
    all_to_all x2, waiting for transfers between devices, reduce_part_now(): pieces = lax.all_to_all(grads, ('zlo', 'x'), 0, 0, tiled=True)  22.1 us
    dot_general x16, matrix products, contract_rows(): lax.dot_general(left_rows, right_rows, (((0,), (0,)), ((), ())), preferre...  19.9 us
    concatenate x16, other arithmetic, joined(): return jnp.concatenate(parts, axis=axis)  14.7 us
  transfers between devices with their start and end apart: 79, of which 32 were waited for; matrix products, arithmetic and copies ran while one was open for 26% of the time, Pallas kernels for 4%

profile of v3, /device:TPU:1, one launch (start us, length us, event | category | flops | bytes accessed | tf_op | source)
XLA Modules:
  0.0 485.6 jit_solution(11236862787736987420)
XLA Ops:
  14.7 3.8 collective-permute-start.4
  19.5 3.6 slice_bitcast_fusion.1
  33.7 9.0 %collective-permute-done.3 = bf16[1536,256]{1,0:T(8,128)(2,1)S(1)} collective-permute-done((bf16[1536,256]{1,0:T(8,128)(2,1)}, bf16[1536,256]{1,0:T(8,128)(2,1)S(1)}, u32[]{:S(2)}, u32[]{:S(2)}) %collective-permute-start.3) | collective-permute-done | bytes 786464 | tf_op jit(solution)/shard_map/ppermute | solution.py:37
  43.7 5.2 %collective-permute-start.6 = (bf16[1536,256]{1,0:T(8,128)(2,1)S(1)}, bf16[1536,256]{1,0:T(8,128)(2,1)}, u32[]{:S(2)}, u32[]{:S(2)}) collective-permute-start(bf16[1536,256]{1,0:T(8,128)(2,1)S(1)} %collective-permute-done.3), channel_id=1, source_target_pairs={{0,4},{4,0},{1,5},{5,1},{2,6},{6,2},{3,7},{7,3},{8,12},{12,8},{9,1... | collective-permute-start | bytes 2359304 | tf_op jit(solution)/shard_map/ppermute | solution.py:29
  58.0 4.8 shard_map.144
  66.0 2.7 collective-permute-start.15
  73.2 4.5 collective-permute-done.8
  78.5 2.7 collective-permute-start.11
  83.0 2.8 collective-permute-start.17
  91.7 4.9 %collective-permute-done.18 = bf16[128,1024]{1,0:T(8,128)(2,1)S(1)} collective-permute-done((bf16[128,1024]{1,0:T(8,128)(2,1)S(1)}, bf16[128,1024]{1,0:T(8,128)(2,1)S(1)}, u32[]{:S(2)}, u32[]{:S(2)}) %collective-permute-start.18) | collective-permute-done | bytes 262176 | tf_op jit(solution)/shard_map/ppermute | solution.py:25
  99.1 2.7 collective-permute-start.19
  106.2 3.0 multiply_convert_fusion.3
  120.0 8.2 %collective-permute-done.21 = bf16[128,1024]{1,0:T(8,128)(2,1)S(1)} collective-permute-done((bf16[128,1024]{1,0:T(8,128)(2,1)S(1)}, bf16[128,1024]{1,0:T(8,128)(2,1)S(1)}, u32[]{:S(2)}, u32[]{:S(2)}) %collective-permute-start.21) | collective-permute-done | bytes 262176 | tf_op jit(solution)/shard_map/ppermute | solution.py:25
  130.2 2.7 collective-permute-start.23
  142.4 5.1 %collective-permute-done.25.far = bf16[128,1024]{1,0:T(8,128)(2,1)S(1)} collective-permute-done((bf16[128,1024]{1,0:T(8,128)(2,1)}, bf16[128,1024]{1,0:T(8,128)(2,1)S(1)}, u32[]{:S(2)}, u32[]{:S(2)}) %collective-permute-start.25) | collective-permute-done | bytes 262176 | tf_op jit(solution)/shard_map/ppermute | solution.py:25
  147.5 4.9 %shard_map.145 = (bf16[512,256]{1,0:T(8,128)(2,1)S(1)}, bf16[512,256]{1,0:T(8,128)(2,1)S(1)}, bf16[512,256]{1,0:T(8,128)(2,1)S(1)}, f32[8,512]{1,0:T(8,128)S(1)}...) custom-call(bf16[384,1024]{1,0:T(8,128)(2,1)S(1)} %pad_maximum_fusion.8.near, ...), custom_call_target="tpu_custom_call" | custom-call | flops 3221225472 | bytes 8388608 | tf_op jit(solution)/shard_map/pallas_call | solution.py:239
  158.5 3.7 collective-permute-done.27
  166.8 6.6 %collective-permute-done.33 = bf16[128,1024]{1,0:T(8,128)(2,1)S(1)} collective-permute-done((bf16[128,1024]{1,0:T(8,128)(2,1)S(1)}, bf16[128,1024]{1,0:T(8,128)(2,1)S(1)}, u32[]{:S(2)}, u32[]{:S(2)}) %collective-permute-start.33) | collective-permute-done | bytes 262176 | tf_op jit(solution)/shard_map/ppermute | solution.py:25
  177.2 7.4 %collective-permute-done.30 = bf16[128,1024]{1,0:T(8,128)(2,1)S(1)} collective-permute-done((bf16[128,1024]{1,0:T(8,128)(2,1)S(1)}, bf16[128,1024]{1,0:T(8,128)(2,1)S(1)}, u32[]{:S(2)}, u32[]{:S(2)}) %collective-permute-start.30) | collective-permute-done | bytes 262176 | tf_op jit(solution)/shard_map/ppermute | solution.py:25
  186.2 3.0 add_convert_fusion.5
  198.5 6.5 %collective-permute-done.35 = bf16[128,1024]{1,0:T(8,128)(2,1)S(1)} collective-permute-done((bf16[128,1024]{1,0:T(8,128)(2,1)S(1)}, bf16[128,1024]{1,0:T(8,128)(2,1)S(1)}, u32[]{:S(2)}, u32[]{:S(2)}) %collective-permute-start.35) | collective-permute-done | bytes 262176 | tf_op jit(solution)/shard_map/ppermute | solution.py:25
  210.4 4.4 collective-permute-start.48
  217.8 6.7 %shard_map.146 = (bf16[512,768]{1,0:T(8,128)(2,1)S(1)}, bf16[384,1024]{1,0:T(8,128)(2,1)S(1)}, bf16[128,1024]{1,0:T(8,128)(2,1)S(1)}) custom-call(bf16[384,1024]{1,0:T(8,128)(2,1)S(1)} %pad_maximum_fusion.11.near, bf16[128,1024]{1,0:T(8,128)(2,1)S(1)} %collective-permute-done.40.far, bf16[1024,768]{1,0:T(8,128)(2,1)S(1)} %pad_maximum_fusion.4.w_qkv, ...), custom_call_target="tpu_custom_call" | custom-call | flops 4294967296 | bytes 8388608 | tf_op jit(solution)/shard_map/pallas_call | solution.py:239
  226.1 3.3 collective-permute-start.41
  232.3 5.6 %collective-permute-done.41 = bf16[128,1024]{1,0:T(8,128)(2,1)S(1)} collective-permute-done((bf16[128,1024]{1,0:T(8,128)(2,1)S(1)}, bf16[128,1024]{1,0:T(8,128)(2,1)S(1)}, u32[]{:S(2)}, u32[]{:S(2)}) %collective-permute-start.41) | collective-permute-done | bytes 262176 | tf_op jit(solution)/shard_map/ppermute | solution.py:25
  244.0 6.5 %collective-permute-start.67 = (bf16[1024,256]{1,0:T(8,128)(2,1)}, bf16[1024,256]{1,0:T(8,128)(2,1)}, u32[]{:S(2)}, u32[]{:S(2)}) collective-permute-start(bf16[1024,256]{1,0:T(8,128)(2,1)} %convolution_convert_fusion.9), channel_id=1, source_target_pairs={{0,4},{4,0},{1,5},{5,1},{2,6},{6,2},{3,7},{7,3},{8,12},{12,8},{9,1... | collective-permute-start | bytes 1572872 | tf_op jit(solution)/shard_map/ppermute | solution.py:29
  264.3 3.8 multiply_convert_fusion
  274.8 3.1 collective-permute-start.49
  280.5 6.4 %collective-permute-done.49 = bf16[128,1024]{1,0:T(8,128)(2,1)} collective-permute-done((bf16[128,1024]{1,0:T(8,128)(2,1)}, bf16[128,1024]{1,0:T(8,128)(2,1)}, u32[]{:S(2)}, u32[]{:S(2)}) %collective-permute-start.49) | collective-permute-done | bytes 262176 | tf_op jit(solution)/shard_map/ppermute | solution.py:25
  291.0 2.7 collective-permute-start.52
  300.9 3.5 collective-permute-done.53
  304.5 6.7 %shard_map.147 = (bf16[512,768]{1,0:T(8,128)(2,1)S(1)}, bf16[384,1024]{1,0:T(8,128)(2,1)S(1)}, bf16[128,1024]{1,0:T(8,128)(2,1)S(1)}) custom-call(bf16[384,1024]{1,0:T(8,128)(2,1)S(1)} %pad_maximum_fusion.13.near, bf16[128,1024]{1,0:T(8,128)(2,1)S(1)} %collective-permute-done.54.far, bf16[1024,768]{1,0:T(8,128)(2,1)S(1)} %pad_maximum_fusion.3.w_qkv, ...), custom_call_target="tpu_custom_call" | custom-call | flops 4294967296 | bytes 8388608 | tf_op jit(solution)/shard_map/pallas_call | solution.py:239
  322.3 4.5 all-to-all-start
  329.3 2.7 collective-permute-start.59
  336.2 17.7 %all-to-all-done = bf16[8,128,1024]{2,1,0:T(8,128)(2,1)} async-done(((bf16[8,128,1024]{2,1,0:T(8,128)(2,1)}), bf16[8,128,1024]{2,1,0:T(8,128)(2,1)}, u32[]{:S(2)}, u32[]{:S(2)}) %all-to-all-start) | async-done | bytes 2097184 | tf_op jit(solution)/shard_map/all_to_all | solution.py:429
  353.9 6.8 %all-to-all-start.1 = ((bf16[8,544,256]{2,1,0:T(8,128)(2,1)}), bf16[8,544,256]{2,1,0:T(8,128)(2,1)}, u32[]{:S(2)}, u32[]{:S(2)}) async-start(bf16[8,544,256]{2,1,0:T(8,128)(2,1)} %pad_maximum_fusion.1), calls=%async_computation.2 | async-start | bytes 4456448 | tf_op jit(solution)/shard_map/all_to_all | solution.py:429
  362.4 3.2 collective-permute-start.61
  366.3 2.7 collective-permute-start.63
  375.5 6.9 %collective-permute-done.63 = bf16[128,1024]{1,0:T(8,128)(2,1)S(1)} collective-permute-done((bf16[128,1024]{1,0:T(8,128)(2,1)}, bf16[128,1024]{1,0:T(8,128)(2,1)S(1)}, u32[]{:S(2)}, u32[]{:S(2)}) %collective-permute-start.63) | collective-permute-done | bytes 262176 | tf_op jit(solution)/shard_map/ppermute | solution.py:25
  384.9 4.4 all-to-all-done.1
  391.3 2.7 collective-permute-start.71
  398.7 5.3 %collective-permute-done.64 = bf16[128,1024]{1,0:T(8,128)(2,1)S(1)} collective-permute-done((bf16[128,1024]{1,0:T(8,128)(2,1)S(1)}, bf16[128,1024]{1,0:T(8,128)(2,1)S(1)}, u32[]{:S(2)}, u32[]{:S(2)}) %collective-permute-start.64) | collective-permute-done | bytes 262176 | tf_op jit(solution)/shard_map/ppermute | solution.py:33
  406.0 8.1 %collective-permute-done.72 = bf16[196,1024]{1,0:T(8,128)(2,1)S(1)} collective-permute-done((bf16[196,1024]{1,0:T(8,128)(2,1)S(1)}, bf16[196,1024]{1,0:T(8,128)(2,1)S(1)}, u32[]{:S(2)}, u32[]{:S(2)}) %collective-permute-start.72) | collective-permute-done | bytes 401440 | tf_op jit(solution)/shard_map/ppermute | solution.py:33
  414.6 27.1 %all_to_all.33 = bf16[8,128,1024]{2,1,0:T(8,128)(2,1)S(1)} all-to-all(bf16[8,128,1024]{2,1,0:T(8,128)(2,1)S(1)} %broadcast_in_dim.113), channel_id=1, replica_groups=mesh['section'=2,'zlo'=2,'x'=4,'core'=2,'tensor'=4] {'zlo','x'}, dimensions={0} | all-to-all | bytes 4194304 | tf_op jit(solution)/shard_map/all_to_all | solution.py:436
  441.7 3.9 collective-permute-start.73
  446.7 4.3 all-to-all-start.3
  455.6 2.8 maximum_convert_fusion
  458.3 9.3 %all-to-all-done.3 = bf16[8,272,256]{2,1,0:T(8,128)(2,1)} async-done(((bf16[8,272,256]{2,1,0:T(8,128)(2,1)}), bf16[8,272,256]{2,1,0:T(8,128)(2,1)}, u32[]{:S(2)}, u32[]{:S(2)}) %all-to-all-start.3) | async-done | bytes 1114144 | tf_op jit(solution)/shard_map/all_to_all | solution.py:436
  (554 shorter events, 206.3 us)
Async XLA Ops:
  7.2 324.8 %reduce-scatter.2.cloned.1.call-start = ((), (), s32[]{:S(2)}) async-start(), calls=%async_computation.5 | async-start | bytes 2359296 | tf_op jit(solution)/shard_map/reduce_scatter | solution.py:425
  8.4 22.8 %collective-permute-start.1 = (bf16[128,1024]{1,0:T(8,128)(2,1)S(1)}, bf16[128,1024]{1,0:T(8,128)(2,1)S(1)}, u32[]{:S(2)}, u32[]{:S(2)}) collective-permute-start(bf16[128,1024]{1,0:T(8,128)(2,1)S(1)} %get-tuple-element.221), channel_id=1, source_target_pairs={{0,1},{1,2},{2,3},{3,0},{4,5},{5,6},{6,7},{7,4},{8,9},{9,10},{10,1... | collective-permute-start | bytes 786440 | tf_op jit(solution)/shard_map/ppermute | solution.py:25
  10.6 20.6 %collective-permute-start = (bf16[128,1024]{1,0:T(8,128)(2,1)S(1)}, bf16[128,1024]{1,0:T(8,128)(2,1)S(1)}, u32[]{:S(2)}, u32[]{:S(2)}) collective-permute-start(bf16[128,1024]{1,0:T(8,128)(2,1)S(1)} %get-tuple-element.221), channel_id=1, source_target_pairs={{0,3},{1,0},{2,1},{3,2},{4,7},{5,4},{6,5},{7,6},{8,11},{9,8},{10,9... | collective-permute-start | bytes 786440 | tf_op jit(solution)/shard_map/ppermute | solution.py:25
  12.1 21.6 %collective-permute-start.2 = (bf16[128,1024]{1,0:T(8,128)(2,1)S(1)}, bf16[128,1024]{1,0:T(8,128)(2,1)S(1)}, u32[]{:S(2)}, u32[]{:S(2)}) collective-permute-start(bf16[128,1024]{1,0:T(8,128)(2,1)S(1)} %get-tuple-element.221), channel_id=1, source_target_pairs={{0,2},{1,3},{2,0},{3,1},{4,6},{5,7},{6,4},{7,5},{8,10},{9,11},{10,... | collective-permute-start | bytes 786440 | tf_op jit(solution)/shard_map/ppermute | solution.py:25
  14.7 12.0 %collective-permute-start.4 = (bf16[128,1024]{1,0:T(8,128)(2,1)S(1)}, bf16[128,1024]{1,0:T(8,128)(2,1)}, u32[]{:S(2)}, u32[]{:S(2)}) collective-permute-start(bf16[128,1024]{1,0:T(8,128)(2,1)S(1)} %constant_dynamic-slice_fusion.3), channel_id=1, source_target_pairs={{0,96},{32,64},{64,32},{96,0},{1,97},{33,65},{65,33},{97,1},{2,98}... | collective-permute-start | bytes 786440 | tf_op jit(solution)/shard_map/ppermute | solution.py:37
  24.0 18.7 %collective-permute-start.3 = (bf16[1536,256]{1,0:T(8,128)(2,1)}, bf16[1536,256]{1,0:T(8,128)(2,1)S(1)}, u32[]{:S(2)}, u32[]{:S(2)}) collective-permute-start(bf16[1536,256]{1,0:T(8,128)(2,1)} %constant_dynamic-slice_fusion.4), channel_id=1, source_target_pairs={{0,96},{32,64},{64,32},{96,0},{1,97},{33,65},{65,33},{97,1},{2,98}... | collective-permute-start | bytes 2359304 | tf_op jit(solution)/shard_map/ppermute | solution.py:37
  31.2 34.7 %collective-permute-start.13 = (bf16[328,1024]{1,0:T(8,128)(2,1)}, bf16[328,1024]{1,0:T(8,128)(2,1)}, u32[]{:S(2)}, u32[]{:S(2)}) collective-permute-start(bf16[328,1024]{1,0:T(8,128)(2,1)} %constant_dynamic-slice_fusion.2), channel_id=1, source_target_pairs={{0,96},{32,64},{64,32},{96,0},{1,97},{33,65},{65,33},{97,1},{2,98}... | collective-permute-start | bytes 2015240 | tf_op jit(solution)/shard_map/ppermute | solution.py:37
  64.5 13.2 %collective-permute-start.8 = (bf16[128,1024]{1,0:T(8,128)(2,1)S(1)}, bf16[128,1024]{1,0:T(8,128)(2,1)S(1)}, u32[]{:S(2)}, u32[]{:S(2)}) collective-permute-start(bf16[128,1024]{1,0:T(8,128)(2,1)S(1)} %get-tuple-element.101), channel_id=1, source_target_pairs={{0,2},{1,3},{2,0},{3,1},{4,6},{5,7},{6,4},{7,5},{8,10},{9,11},{10,... | collective-permute-start | bytes 786440 | tf_op jit(solution)/shard_map/ppermute | solution.py:25
  66.0 17.0 %collective-permute-start.15 = (bf16[328,1024]{1,0:T(8,128)(2,1)S(1)}, bf16[328,1024]{1,0:T(8,128)(2,1)S(1)}, u32[]{:S(2)}, u32[]{:S(2)}) collective-permute-start(bf16[328,1024]{1,0:T(8,128)(2,1)S(1)} %constant_dynamic-slice_fusion.1), channel_id=1, source_target_pairs={{0,96},{32,64},{64,32},{96,0},{1,97},{33,65},{65,33},{97,1},{2,98}... | collective-permute-start | bytes 2015240 | tf_op jit(solution)/shard_map/ppermute | solution.py:37
  68.7 21.8 %collective-permute-start.14 = (bf16[328,1024]{1,0:T(8,128)(2,1)}, bf16[328,1024]{1,0:T(8,128)(2,1)S(1)}, u32[]{:S(2)}, u32[]{:S(2)}) collective-permute-start(bf16[328,1024]{1,0:T(8,128)(2,1)} %collective-permute-done.13), channel_id=1, source_target_pairs={{0,4},{4,0},{1,5},{5,1},{2,6},{6,2},{3,7},{7,3},{8,12},{12,8},{9,1... | collective-permute-start | bytes 2015240 | tf_op jit(solution)/shard_map/ppermute | solution.py:29
  78.5 11.0 %collective-permute-start.11 = (bf16[128,1024]{1,0:T(8,128)(2,1)S(1)}, bf16[128,1024]{1,0:T(8,128)(2,1)S(1)}, u32[]{:S(2)}, u32[]{:S(2)}) collective-permute-start(bf16[128,1024]{1,0:T(8,128)(2,1)S(1)} %multiply_convert_fusion.5), channel_id=1, source_target_pairs={{0,3},{1,0},{2,1},{3,2},{4,7},{5,4},{6,5},{7,6},{8,11},{9,8},{10,9... | collective-permute-start | bytes 786440 | tf_op jit(solution)/shard_map/ppermute | solution.py:25
  83.0 16.1 %collective-permute-start.17 = (bf16[328,1024]{1,0:T(8,128)(2,1)S(1)}, bf16[328,1024]{1,0:T(8,128)(2,1)S(1)}, u32[]{:S(2)}, u32[]{:S(2)}) collective-permute-start(bf16[328,1024]{1,0:T(8,128)(2,1)S(1)} %constant_dynamic-slice_fusion), channel_id=1, source_target_pairs={{0,96},{32,64},{64,32},{96,0},{1,97},{33,65},{65,33},{97,1},{2,98}... | collective-permute-start | bytes 2015240 | tf_op jit(solution)/shard_map/ppermute | solution.py:37
  85.8 16.0 %collective-permute-start.16 = (bf16[328,1024]{1,0:T(8,128)(2,1)S(1)}, bf16[328,1024]{1,0:T(8,128)(2,1)S(1)}, u32[]{:S(2)}, u32[]{:S(2)}) collective-permute-start(bf16[328,1024]{1,0:T(8,128)(2,1)S(1)} %collective-permute-done.15), channel_id=1, source_target_pairs={{0,4},{4,0},{1,5},{5,1},{2,6},{6,2},{3,7},{7,3},{8,12},{12,8},{9,1... | collective-permute-start | bytes 2015240 | tf_op jit(solution)/shard_map/ppermute | solution.py:29
  113.8 14.4 %collective-permute-start.21 = (bf16[128,1024]{1,0:T(8,128)(2,1)S(1)}, bf16[128,1024]{1,0:T(8,128)(2,1)S(1)}, u32[]{:S(2)}, u32[]{:S(2)}) collective-permute-start(bf16[128,1024]{1,0:T(8,128)(2,1)S(1)} %get-tuple-element.304), channel_id=1, source_target_pairs={{0,1},{1,2},{2,3},{3,0},{4,5},{5,6},{6,7},{7,4},{8,9},{9,10},{10,1... | collective-permute-start | bytes 786440 | tf_op jit(solution)/shard_map/ppermute | solution.py:25
  116.5 11.7 %collective-permute-start.20 = (bf16[128,1024]{1,0:T(8,128)(2,1)S(1)}, bf16[128,1024]{1,0:T(8,128)(2,1)S(1)}, u32[]{:S(2)}, u32[]{:S(2)}) collective-permute-start(bf16[128,1024]{1,0:T(8,128)(2,1)S(1)} %convolution_convert_fusion.13), channel_id=1, source_target_pairs={{0,2},{1,3},{2,0},{3,1},{4,6},{5,7},{6,4},{7,5},{8,10},{9,11},{10,... | collective-permute-start | bytes 786440 | tf_op jit(solution)/shard_map/ppermute | solution.py:25
  130.2 10.9 %collective-permute-start.24 = (bf16[128,1024]{1,0:T(8,128)(2,1)}, bf16[128,1024]{1,0:T(8,128)(2,1)}, u32[]{:S(2)}, u32[]{:S(2)}) collective-permute-start(bf16[128,1024]{1,0:T(8,128)(2,1)} %fusion.46), channel_id=1, source_target_pairs={{0,1},{1,2},{2,3},{3,0},{4,5},{5,6},{6,7},{7,4},{8,9},{9,10},{10,1... | collective-permute-start | bytes 786440 | tf_op jit(solution)/shard_map/ppermute | solution.py:25
  130.2 10.9 %collective-permute-start.23 = (bf16[128,1024]{1,0:T(8,128)(2,1)}, bf16[128,1024]{1,0:T(8,128)(2,1)}, u32[]{:S(2)}, u32[]{:S(2)}) collective-permute-start(bf16[128,1024]{1,0:T(8,128)(2,1)} %fusion.46), channel_id=1, source_target_pairs={{0,3},{1,0},{2,1},{3,2},{4,7},{5,4},{6,5},{7,6},{8,11},{9,8},{10,9... | collective-permute-start | bytes 786440 | tf_op jit(solution)/shard_map/ppermute | solution.py:25
  154.3 19.1 %collective-permute-start.33 = (bf16[128,1024]{1,0:T(8,128)(2,1)S(1)}, bf16[128,1024]{1,0:T(8,128)(2,1)S(1)}, u32[]{:S(2)}, u32[]{:S(2)}) collective-permute-start(bf16[128,1024]{1,0:T(8,128)(2,1)S(1)} %select_bitcast_fusion.9), channel_id=1, source_target_pairs={{0,1},{1,2},{2,3},{3,0},{4,5},{5,6},{6,7},{7,4},{8,9},{9,10},{10,1... | collective-permute-start | bytes 786440 | tf_op jit(solution)/shard_map/ppermute | solution.py:25
  156.1 17.3 %collective-permute-start.32 = (bf16[128,1024]{1,0:T(8,128)(2,1)S(1)}, bf16[128,1024]{1,0:T(8,128)(2,1)S(1)}, u32[]{:S(2)}, u32[]{:S(2)}) collective-permute-start(bf16[128,1024]{1,0:T(8,128)(2,1)S(1)} %select_bitcast_fusion.9), channel_id=1, source_target_pairs={{0,3},{1,0},{2,1},{3,2},{4,7},{5,4},{6,5},{7,6},{8,11},{9,8},{10,9... | collective-permute-start | bytes 786440 | tf_op jit(solution)/shard_map/ppermute | solution.py:25
  157.7 16.8 %collective-permute-start.34 = (bf16[128,1024]{1,0:T(8,128)(2,1)S(1)}, bf16[128,1024]{1,0:T(8,128)(2,1)S(1)}, u32[]{:S(2)}, u32[]{:S(2)}) collective-permute-start(bf16[128,1024]{1,0:T(8,128)(2,1)S(1)} %select_bitcast_fusion.9), channel_id=1, source_target_pairs={{0,2},{1,3},{2,0},{3,1},{4,6},{5,7},{6,4},{7,5},{8,10},{9,11},{10,... | collective-permute-start | bytes 786440 | tf_op jit(solution)/shard_map/ppermute | solution.py:25
  164.0 20.6 %collective-permute-start.30 = (bf16[128,1024]{1,0:T(8,128)(2,1)S(1)}, bf16[128,1024]{1,0:T(8,128)(2,1)S(1)}, u32[]{:S(2)}, u32[]{:S(2)}) collective-permute-start(bf16[128,1024]{1,0:T(8,128)(2,1)S(1)} %multiply_convert_fusion.4), channel_id=1, source_target_pairs={{0,1},{1,2},{2,3},{3,0},{4,5},{5,6},{6,7},{7,4},{8,9},{9,10},{10,1... | collective-permute-start | bytes 786440 | tf_op jit(solution)/shard_map/ppermute | solution.py:25
  164.5 20.1 %collective-permute-start.29 = (bf16[128,1024]{1,0:T(8,128)(2,1)S(1)}, bf16[128,1024]{1,0:T(8,128)(2,1)S(1)}, u32[]{:S(2)}, u32[]{:S(2)}) collective-permute-start(bf16[128,1024]{1,0:T(8,128)(2,1)S(1)} %multiply_convert_fusion.4), channel_id=1, source_target_pairs={{0,3},{1,0},{2,1},{3,2},{4,7},{5,4},{6,5},{7,6},{8,11},{9,8},{10,9... | collective-permute-start | bytes 786440 | tf_op jit(solution)/shard_map/ppermute | solution.py:25
  174.5 15.0 %collective-permute-start.31 = (bf16[128,1024]{1,0:T(8,128)(2,1)S(1)}, bf16[128,1024]{1,0:T(8,128)(2,1)S(1)}, u32[]{:S(2)}, u32[]{:S(2)}) collective-permute-start(bf16[128,1024]{1,0:T(8,128)(2,1)S(1)} %multiply_convert_fusion.4), channel_id=1, source_target_pairs={{0,2},{1,3},{2,0},{3,1},{4,6},{5,7},{6,4},{7,5},{8,10},{9,11},{10,... | collective-permute-start | bytes 786440 | tf_op jit(solution)/shard_map/ppermute | solution.py:25
  205.9 11.8 %collective-permute-start.39 = (bf16[128,1024]{1,0:T(8,128)(2,1)S(1)}, bf16[128,1024]{1,0:T(8,128)(2,1)S(1)}, u32[]{:S(2)}, u32[]{:S(2)}) collective-permute-start(bf16[128,1024]{1,0:T(8,128)(2,1)S(1)} %get-tuple-element.230), channel_id=1, source_target_pairs={{0,1},{1,2},{2,3},{3,0},{4,5},{5,6},{6,7},{7,4},{8,9},{9,10},{10,1... | collective-permute-start | bytes 786440 | tf_op jit(solution)/shard_map/ppermute | solution.py:25
  205.9 11.7 %collective-permute-start.38 = (bf16[128,1024]{1,0:T(8,128)(2,1)S(1)}, bf16[128,1024]{1,0:T(8,128)(2,1)S(1)}, u32[]{:S(2)}, u32[]{:S(2)}) collective-permute-start(bf16[128,1024]{1,0:T(8,128)(2,1)S(1)} %get-tuple-element.230), channel_id=1, source_target_pairs={{0,3},{1,0},{2,1},{3,2},{4,7},{5,4},{6,5},{7,6},{8,11},{9,8},{10,9... | collective-permute-start | bytes 786440 | tf_op jit(solution)/shard_map/ppermute | solution.py:25
  210.4 43.0 %collective-permute-start.48 = (bf16[328,1024]{1,0:T(8,128)(2,1)}, bf16[328,1024]{1,0:T(8,128)(2,1)}, u32[]{:S(2)}, u32[]{:S(2)}) collective-permute-start(bf16[328,1024]{1,0:T(8,128)(2,1)} %convolution_convert_fusion.7), channel_id=1, source_target_pairs={{0,4},{4,0},{1,5},{5,1},{2,6},{6,2},{3,7},{7,3},{8,12},{12,8},{9,1... | collective-permute-start | bytes 2015240 | tf_op jit(solution)/shard_map/ppermute | solution.py:29
  216.9 43.5 %collective-permute-start.47 = (bf16[656,1024]{1,0:T(8,128)(2,1)}, bf16[656,1024]{1,0:T(8,128)(2,1)}, u32[]{:S(2)}, u32[]{:S(2)}) collective-permute-start(bf16[656,1024]{1,0:T(8,128)(2,1)} %convolution_convert_fusion.1), channel_id=1, source_target_pairs={{0,4},{4,0},{1,5},{5,1},{2,6},{6,2},{3,7},{7,3},{8,12},{12,8},{9,1... | collective-permute-start | bytes 4030472 | tf_op jit(solution)/shard_map/ppermute | solution.py:29
  226.1 11.9 %collective-permute-start.41 = (bf16[128,1024]{1,0:T(8,128)(2,1)S(1)}, bf16[128,1024]{1,0:T(8,128)(2,1)S(1)}, u32[]{:S(2)}, u32[]{:S(2)}) collective-permute-start(bf16[128,1024]{1,0:T(8,128)(2,1)S(1)} %get-tuple-element.134), channel_id=1, source_target_pairs={{0,2},{1,3},{2,0},{3,1},{4,6},{5,7},{6,4},{7,5},{8,10},{9,11},{10,... | collective-permute-start | bytes 786440 | tf_op jit(solution)/shard_map/ppermute | solution.py:25
  238.9 16.7 %collective-permute-start.45 = (bf16[128,1024]{1,0:T(8,128)(2,1)S(1)}, bf16[128,1024]{1,0:T(8,128)(2,1)}, u32[]{:S(2)}, u32[]{:S(2)}) collective-permute-start(bf16[128,1024]{1,0:T(8,128)(2,1)S(1)} %add_convert_fusion.9), channel_id=1, source_target_pairs={{0,1},{1,2},{2,3},{3,0},{4,5},{5,6},{6,7},{7,4},{8,9},{9,10},{10,1... | collective-permute-start | bytes 786440 | tf_op jit(solution)/shard_map/ppermute | solution.py:25
  239.0 16.9 %collective-permute-start.44 = (bf16[128,1024]{1,0:T(8,128)(2,1)S(1)}, bf16[128,1024]{1,0:T(8,128)(2,1)}, u32[]{:S(2)}, u32[]{:S(2)}) collective-permute-start(bf16[128,1024]{1,0:T(8,128)(2,1)S(1)} %add_convert_fusion.9), channel_id=1, source_target_pairs={{0,3},{1,0},{2,1},{3,2},{4,7},{5,4},{6,5},{7,6},{8,11},{9,8},{10,9... | collective-permute-start | bytes 786440 | tf_op jit(solution)/shard_map/ppermute | solution.py:25
  244.0 13.8 %collective-permute-start.67 = (bf16[1024,256]{1,0:T(8,128)(2,1)}, bf16[1024,256]{1,0:T(8,128)(2,1)}, u32[]{:S(2)}, u32[]{:S(2)}) collective-permute-start(bf16[1024,256]{1,0:T(8,128)(2,1)} %convolution_convert_fusion.9), channel_id=1, source_target_pairs={{0,4},{4,0},{1,5},{5,1},{2,6},{6,2},{3,7},{7,3},{8,12},{12,8},{9,1... | collective-permute-start | bytes 1572872 | tf_op jit(solution)/shard_map/ppermute | solution.py:29
  253.4 10.8 %collective-permute-start.46 = (bf16[128,1024]{1,0:T(8,128)(2,1)S(1)}, bf16[128,1024]{1,0:T(8,128)(2,1)}, u32[]{:S(2)}, u32[]{:S(2)}) collective-permute-start(bf16[128,1024]{1,0:T(8,128)(2,1)S(1)} %add_convert_fusion.9), channel_id=1, source_target_pairs={{0,2},{1,3},{2,0},{3,1},{4,6},{5,7},{6,4},{7,5},{8,10},{9,11},{10,... | collective-permute-start | bytes 786440 | tf_op jit(solution)/shard_map/ppermute | solution.py:25
  255.6 22.4 %collective-permute-start.68 = (bf16[1024,256]{1,0:T(8,128)(2,1)}, bf16[1024,256]{1,0:T(8,128)(2,1)S(1)}, u32[]{:S(2)}, u32[]{:S(2)}) collective-permute-start(bf16[1024,256]{1,0:T(8,128)(2,1)} %convolution_convert_fusion.8), channel_id=1, source_target_pairs={{0,4},{4,0},{1,5},{5,1},{2,6},{6,2},{3,7},{7,3},{8,12},{12,8},{9,1... | collective-permute-start | bytes 1572872 | tf_op jit(solution)/shard_map/ppermute | solution.py:29
  274.8 12.0 %collective-permute-start.49 = (bf16[128,1024]{1,0:T(8,128)(2,1)}, bf16[128,1024]{1,0:T(8,128)(2,1)}, u32[]{:S(2)}, u32[]{:S(2)}) collective-permute-start(bf16[128,1024]{1,0:T(8,128)(2,1)} %convolution_convert_fusion.14), channel_id=1, source_target_pairs={{0,2},{1,3},{2,0},{3,1},{4,6},{5,7},{6,4},{7,5},{8,10},{9,11},{10,... | collective-permute-start | bytes 786440 | tf_op jit(solution)/shard_map/ppermute | solution.py:25
  291.0 13.4 %collective-permute-start.53 = (bf16[128,1024]{1,0:T(8,128)(2,1)S(1)}, bf16[128,1024]{1,0:T(8,128)(2,1)S(1)}, u32[]{:S(2)}, u32[]{:S(2)}) collective-permute-start(bf16[128,1024]{1,0:T(8,128)(2,1)S(1)} %get-tuple-element.224), channel_id=1, source_target_pairs={{0,1},{1,2},{2,3},{3,0},{4,5},{5,6},{6,7},{7,4},{8,9},{9,10},{10,1... | collective-permute-start | bytes 786440 | tf_op jit(solution)/shard_map/ppermute | solution.py:25
  291.0 13.4 %collective-permute-start.52 = (bf16[128,1024]{1,0:T(8,128)(2,1)S(1)}, bf16[128,1024]{1,0:T(8,128)(2,1)S(1)}, u32[]{:S(2)}, u32[]{:S(2)}) collective-permute-start(bf16[128,1024]{1,0:T(8,128)(2,1)S(1)} %get-tuple-element.224), channel_id=1, source_target_pairs={{0,3},{1,0},{2,1},{3,2},{4,7},{5,4},{6,5},{7,6},{8,11},{9,8},{10,9... | collective-permute-start | bytes 786440 | tf_op jit(solution)/shard_map/ppermute | solution.py:25
  293.7 10.8 %collective-permute-start.54 = (bf16[128,1024]{1,0:T(8,128)(2,1)S(1)}, bf16[128,1024]{1,0:T(8,128)(2,1)S(1)}, u32[]{:S(2)}, u32[]{:S(2)}) collective-permute-start(bf16[128,1024]{1,0:T(8,128)(2,1)S(1)} %get-tuple-element.224), channel_id=1, source_target_pairs={{0,2},{1,3},{2,0},{3,1},{4,6},{5,7},{6,4},{7,5},{8,10},{9,11},{10,... | collective-permute-start | bytes 786440 | tf_op jit(solution)/shard_map/ppermute | solution.py:25
  298.6 18.3 %collective-permute-start.56 = (bf16[328,1024]{1,0:T(8,128)(2,1)S(1)}, bf16[328,1024]{1,0:T(8,128)(2,1)S(1)}, u32[]{:S(2)}, u32[]{:S(2)}) collective-permute-start(bf16[328,1024]{1,0:T(8,128)(2,1)S(1)} %convolution_convert_fusion.6), channel_id=1, source_target_pairs={{0,4},{4,0},{1,5},{5,1},{2,6},{6,2},{3,7},{7,3},{8,12},{12,8},{9,1... | collective-permute-start | bytes 2015240 | tf_op jit(solution)/shard_map/ppermute | solution.py:29
  300.6 19.1 %collective-permute-start.55 = (bf16[656,1024]{1,0:T(8,128)(2,1)S(1)}, bf16[656,1024]{1,0:T(8,128)(2,1)S(1)}, u32[]{:S(2)}, u32[]{:S(2)}) collective-permute-start(bf16[656,1024]{1,0:T(8,128)(2,1)S(1)} %convolution_convert_fusion), channel_id=1, source_target_pairs={{0,4},{4,0},{1,5},{5,1},{2,6},{6,2},{3,7},{7,3},{8,12},{12,8},{9,1... | collective-permute-start | bytes 4030472 | tf_op jit(solution)/shard_map/ppermute | solution.py:29
  322.3 31.6 %all-to-all-start = ((bf16[8,128,1024]{2,1,0:T(8,128)(2,1)}), bf16[8,128,1024]{2,1,0:T(8,128)(2,1)}, u32[]{:S(2)}, u32[]{:S(2)}) async-start(bf16[8,128,1024]{2,1,0:T(8,128)(2,1)} %bitcast.39), calls=%async_computation.1 | async-start | bytes 4194304 | tf_op jit(solution)/shard_map/all_to_all | solution.py:429
  329.3 39.6 %collective-permute-start.59 = (bf16[128,1024]{1,0:T(8,128)(2,1)}, bf16[128,1024]{1,0:T(8,128)(2,1)}, u32[]{:S(2)}, u32[]{:S(2)}) collective-permute-start(bf16[128,1024]{1,0:T(8,128)(2,1)} %get-tuple-element.295), channel_id=1, source_target_pairs={{0,3},{1,0},{2,1},{3,2},{4,7},{5,4},{6,5},{7,6},{8,11},{9,8},{10,9... | collective-permute-start | bytes 786440 | tf_op jit(solution)/shard_map/ppermute | solution.py:25
  332.0 37.0 %collective-permute-start.58 = (bf16[128,1024]{1,0:T(8,128)(2,1)}, bf16[128,1024]{1,0:T(8,128)(2,1)}, u32[]{:S(2)}, u32[]{:S(2)}) collective-permute-start(bf16[128,1024]{1,0:T(8,128)(2,1)} %get-tuple-element.294), channel_id=1, source_target_pairs={{0,1},{1,2},{2,3},{3,0},{4,5},{5,6},{6,7},{7,4},{8,9},{9,10},{10,1... | collective-permute-start | bytes 786440 | tf_op jit(solution)/shard_map/ppermute | solution.py:25
  353.9 35.4 %all-to-all-start.1 = ((bf16[8,544,256]{2,1,0:T(8,128)(2,1)}), bf16[8,544,256]{2,1,0:T(8,128)(2,1)}, u32[]{:S(2)}, u32[]{:S(2)}) async-start(bf16[8,544,256]{2,1,0:T(8,128)(2,1)} %pad_maximum_fusion.1), calls=%async_computation.2 | async-start | bytes 4456448 | tf_op jit(solution)/shard_map/all_to_all | solution.py:429
  362.4 20.4 %collective-permute-start.61 = (bf16[128,1024]{1,0:T(8,128)(2,1)S(1)}, bf16[128,1024]{1,0:T(8,128)(2,1)S(1)}, u32[]{:S(2)}, u32[]{:S(2)}) collective-permute-start(bf16[128,1024]{1,0:T(8,128)(2,1)S(1)} %copy-done.11), channel_id=1, source_target_pairs={{0,2},{1,3},{2,0},{3,1},{4,6},{5,7},{6,4},{7,5},{8,10},{9,11},{10,... | collective-permute-start | bytes 786440 | tf_op jit(solution)/shard_map/ppermute | solution.py:25
  366.3 16.1 %collective-permute-start.63 = (bf16[128,1024]{1,0:T(8,128)(2,1)}, bf16[128,1024]{1,0:T(8,128)(2,1)S(1)}, u32[]{:S(2)}, u32[]{:S(2)}) collective-permute-start(bf16[128,1024]{1,0:T(8,128)(2,1)} %get-tuple-element.293), channel_id=1, source_target_pairs={{0,3},{1,0},{2,1},{3,2},{4,7},{5,4},{6,5},{7,6},{8,11},{9,8},{10,9... | collective-permute-start | bytes 786440 | tf_op jit(solution)/shard_map/ppermute | solution.py:25
  368.9 13.8 %collective-permute-start.62 = (bf16[128,1024]{1,0:T(8,128)(2,1)S(1)}, bf16[128,1024]{1,0:T(8,128)(2,1)S(1)}, u32[]{:S(2)}, u32[]{:S(2)}) collective-permute-start(bf16[128,1024]{1,0:T(8,128)(2,1)S(1)} %get-tuple-element.292), channel_id=1, source_target_pairs={{0,1},{1,2},{2,3},{3,0},{4,5},{5,6},{6,7},{7,4},{8,9},{9,10},{10,1... | collective-permute-start | bytes 786440 | tf_op jit(solution)/shard_map/ppermute | solution.py:25
  371.8 26.8 %collective-permute-start.60 = (bf16[128,1024]{1,0:T(8,128)(2,1)}, bf16[128,1024]{1,0:T(8,128)(2,1)}, u32[]{:S(2)}, u32[]{:S(2)}) collective-permute-start(bf16[128,1024]{1,0:T(8,128)(2,1)} %get-tuple-element.222), channel_id=1, source_target_pairs={{0,64},{64,0},{1,65},{65,1},{2,66},{66,2},{3,67},{67,3},{4,68},{68... | collective-permute-start | bytes 786440 | tf_op jit(solution)/shard_map/ppermute | solution.py:33
  446.7 20.9 %all-to-all-start.3 = ((bf16[8,272,256]{2,1,0:T(8,128)(2,1)}), bf16[8,272,256]{2,1,0:T(8,128)(2,1)}, u32[]{:S(2)}, u32[]{:S(2)}) async-start(bf16[8,272,256]{2,1,0:T(8,128)(2,1)} %broadcast_in_dim.114), calls=%async_computation.4 | async-start | bytes 2228224 | tf_op jit(solution)/shard_map/all_to_all | solution.py:436
  (132 other events, 1556.0 us)
Sparse Core Ops, SparseCore 0:
  279.0 36.5 reduce-scatter.1

commit v4 on v3

--- a/solution.py
+++ b/solution.py
@@ -543,7 +543,8 @@
     attn_width = attn_pack0.shape[1]
     packs = [pack.reshape(8, -1, attn_width) for pack in (attn_pack0, attn_pack1)]
     attn_rows = packs[0].shape[1]
-    attn_both = reduce_part_now(joined(packs, 1).reshape(-1, attn_width))
+    attn_both = after_all(joined(packs, 1).reshape(-1, attn_width), in0, out1)
+    attn_both = reduce_part_now(attn_both)
     gain_start = 2 * model_width % attn_rows
     holds_gains = lax.axis_index(("zlo", "x")) == 2 * model_width // attn_rows
     attn_both = attn_both.reshape(2, attn_rows, attn_width)

time: 495 us -> 515 us (1.040)
  starting transfers between devices: 129 us -> 139 us
  waiting for transfers between devices: 143 us -> 152 us
    ppermute x51, waiting for transfers between devices: 84.6 us -> 93 us  [around(): lax.ppermute(block, axis, [(i, (i + distance) % count) for i in range(cou...]
    ppermute x51, starting transfers between devices: 61.5 us -> 69.1 us  [around(): lax.ppermute(block, axis, [(i, (i + distance) % count) for i in range(cou...]
  transfers between devices with their start and end apart: 79 -> 79, of which waited for: 32 -> 33; matrix products, arithmetic and copies ran while one was open for 26% -> 25% of each run, Pallas kernels for 4% -> 4%
where the time goes in v4:
time: 515 us; the launch traced here: 506 us
  waiting for transfers between devices  152 us (30%)
  starting transfers between devices  139 us (27%)
  other arithmetic  71.3 us (14%)
  matrix products  42.1 us (8%)
  local copies, waits for them, and re-layouts  34.6 us (7%)
  blocking collectives  27.1 us (5%)
  Pallas kernels  23.2 us (5%)
  between operations  16.5 us (3%)
    ppermute x51, waiting for transfers between devices, around(): lax.ppermute(block, axis, [(i, (i + distance) % count) for i in range(cou...  93 us
    ppermute x51, starting transfers between devices, around(): lax.ppermute(block, axis, [(i, (i + distance) % count) for i in range(cou...  69.1 us
    ppermute x15, starting transfers between devices, swap_core(): return lax.ppermute(block, 'core', [(0, 1), (1, 0)])  35 us
    all_to_all x1, blocking collectives, spread_part(): return lax.all_to_all(copies, ('zlo', 'x'), 0, 0, tiled=True)  27.1 us
    all_to_all x2, waiting for transfers between devices, reduce_part_now(): pieces = lax.all_to_all(grads, ('zlo', 'x'), 0, 0, tiled=True)  23.2 us
    pallas_call x4, Pallas kernels, whole_call(): pl.pallas_call(kernel, out_shape=[jax.ShapeDtypeStruct(*shape) for shape...  23.2 us
    dot_general x16, matrix products, contract_rows(): lax.dot_general(left_rows, right_rows, (((0,), (0,)), ((), ())), preferre...  19.9 us
    concatenate x16, other arithmetic, joined(): return jnp.concatenate(parts, axis=axis)  14.8 us
  transfers between devices with their start and end apart: 79, of which 33 were waited for; matrix products, arithmetic and copies ran while one was open for 25% of the time, Pallas kernels for 4%

profile of v4, /device:TPU:1, one launch (start us, length us, event | category | flops | bytes accessed | tf_op | source)
XLA Modules:
  0.0 505.5 jit_solution(14483775291174853072)
XLA Ops:
  14.7 3.8 collective-permute-start.4
  19.5 3.5 slice_bitcast_fusion.1
  34.4 9.4 %collective-permute-done.3 = bf16[1536,256]{1,0:T(8,128)(2,1)} collective-permute-done((bf16[1536,256]{1,0:T(8,128)(2,1)}, bf16[1536,256]{1,0:T(8,128)(2,1)}, u32[]{:S(2)}, u32[]{:S(2)}) %collective-permute-start.3) | collective-permute-done | bytes 786464 | tf_op jit(solution)/shard_map/ppermute | solution.py:37
  44.9 5.1 %collective-permute-start.6 = (bf16[1536,256]{1,0:T(8,128)(2,1)}, bf16[1536,256]{1,0:T(8,128)(2,1)}, u32[]{:S(2)}, u32[]{:S(2)}) collective-permute-start(bf16[1536,256]{1,0:T(8,128)(2,1)} %collective-permute-done.3), channel_id=1, source_target_pairs={{0,4},{4,0},{1,5},{5,1},{2,6},{6,2},{3,7},{7,3},{8,12},{12,8},{9,1... | collective-permute-start | bytes 2359304 | tf_op jit(solution)/shard_map/ppermute | solution.py:29
  59.4 4.9 shard_map.144
  67.2 2.9 collective-permute-start.15
  74.7 4.2 collective-permute-done.8
  93.2 5.1 %collective-permute-done.18 = bf16[128,1024]{1,0:T(8,128)(2,1)S(1)} collective-permute-done((bf16[128,1024]{1,0:T(8,128)(2,1)S(1)}, bf16[128,1024]{1,0:T(8,128)(2,1)S(1)}, u32[]{:S(2)}, u32[]{:S(2)}) %collective-permute-start.18) | collective-permute-done | bytes 262176 | tf_op jit(solution)/shard_map/ppermute | solution.py:25
  98.3 2.8 collective-permute-done.17
  103.6 2.7 bitcast_select_fusion
  107.9 3.0 multiply_convert_fusion.3
  121.7 8.0 %collective-permute-done.21 = bf16[128,1024]{1,0:T(8,128)(2,1)S(1)} collective-permute-done((bf16[128,1024]{1,0:T(8,128)(2,1)S(1)}, bf16[128,1024]{1,0:T(8,128)(2,1)S(1)}, u32[]{:S(2)}, u32[]{:S(2)}) %collective-permute-start.21) | collective-permute-done | bytes 262176 | tf_op jit(solution)/shard_map/ppermute | solution.py:25
  131.2 2.7 collective-permute-start.23
  140.5 12.5 %collective-permute-start.25 = (bf16[128,1024]{1,0:T(8,128)(2,1)}, bf16[128,1024]{1,0:T(8,128)(2,1)S(1)}, u32[]{:S(2)}, u32[]{:S(2)}) collective-permute-start(bf16[128,1024]{1,0:T(8,128)(2,1)} %fusion.46), channel_id=1, source_target_pairs={{0,2},{1,3},{2,0},{3,1},{4,6},{5,7},{6,4},{7,5},{8,10},{9,11},{10,... | collective-permute-start | bytes 786440 | tf_op jit(solution)/shard_map/ppermute | solution.py:25
  155.8 5.1 %collective-permute-done.25.far = bf16[128,1024]{1,0:T(8,128)(2,1)S(1)} collective-permute-done((bf16[128,1024]{1,0:T(8,128)(2,1)}, bf16[128,1024]{1,0:T(8,128)(2,1)S(1)}, u32[]{:S(2)}, u32[]{:S(2)}) %collective-permute-start.25) | collective-permute-done | bytes 262176 | tf_op jit(solution)/shard_map/ppermute | solution.py:25
  160.8 4.8 shard_map.145
  171.8 3.6 collective-permute-done.27
  180.3 6.4 %collective-permute-done.33 = bf16[128,1024]{1,0:T(8,128)(2,1)S(1)} collective-permute-done((bf16[128,1024]{1,0:T(8,128)(2,1)S(1)}, bf16[128,1024]{1,0:T(8,128)(2,1)S(1)}, u32[]{:S(2)}, u32[]{:S(2)}) %collective-permute-start.33) | collective-permute-done | bytes 262176 | tf_op jit(solution)/shard_map/ppermute | solution.py:25
  190.3 7.6 %collective-permute-done.30 = bf16[128,1024]{1,0:T(8,128)(2,1)S(1)} collective-permute-done((bf16[128,1024]{1,0:T(8,128)(2,1)S(1)}, bf16[128,1024]{1,0:T(8,128)(2,1)S(1)}, u32[]{:S(2)}, u32[]{:S(2)}) %collective-permute-start.30) | collective-permute-done | bytes 262176 | tf_op jit(solution)/shard_map/ppermute | solution.py:25
  199.6 3.0 add_convert_fusion.5
  211.8 6.6 %collective-permute-done.35 = bf16[128,1024]{1,0:T(8,128)(2,1)S(1)} collective-permute-done((bf16[128,1024]{1,0:T(8,128)(2,1)S(1)}, bf16[128,1024]{1,0:T(8,128)(2,1)S(1)}, u32[]{:S(2)}, u32[]{:S(2)}) %collective-permute-start.35) | collective-permute-done | bytes 262176 | tf_op jit(solution)/shard_map/ppermute | solution.py:25
  223.7 4.4 collective-permute-start.48
  231.1 6.7 %shard_map.146 = (bf16[512,768]{1,0:T(8,128)(2,1)S(1)}, bf16[384,1024]{1,0:T(8,128)(2,1)S(1)}, bf16[128,1024]{1,0:T(8,128)(2,1)S(1)}) custom-call(bf16[384,1024]{1,0:T(8,128)(2,1)S(1)} %pad_maximum_fusion.11.near, bf16[128,1024]{1,0:T(8,128)(2,1)S(1)} %collective-permute-done.40.far, bf16[1024,768]{1,0:T(8,128)(2,1)S(1)} %pad_maximum_fusion.4.w_qkv, ...), custom_call_target="tpu_custom_call" | custom-call | flops 4294967296 | bytes 8388608 | tf_op jit(solution)/shard_map/pallas_call | solution.py:239
  239.4 3.2 collective-permute-start.41
  245.6 5.6 %collective-permute-done.41 = bf16[128,1024]{1,0:T(8,128)(2,1)S(1)} collective-permute-done((bf16[128,1024]{1,0:T(8,128)(2,1)S(1)}, bf16[128,1024]{1,0:T(8,128)(2,1)S(1)}, u32[]{:S(2)}, u32[]{:S(2)}) %collective-permute-start.41) | collective-permute-done | bytes 262176 | tf_op jit(solution)/shard_map/ppermute | solution.py:25
  257.3 6.5 %collective-permute-start.67 = (bf16[1024,256]{1,0:T(8,128)(2,1)}, bf16[1024,256]{1,0:T(8,128)(2,1)}, u32[]{:S(2)}, u32[]{:S(2)}) collective-permute-start(bf16[1024,256]{1,0:T(8,128)(2,1)} %convolution_convert_fusion.9), channel_id=1, source_target_pairs={{0,4},{4,0},{1,5},{5,1},{2,6},{6,2},{3,7},{7,3},{8,12},{12,8},{9,1... | collective-permute-start | bytes 1572872 | tf_op jit(solution)/shard_map/ppermute | solution.py:29
  277.6 3.8 multiply_convert_fusion
  288.2 3.1 collective-permute-start.49
  293.9 6.4 %collective-permute-done.49 = bf16[128,1024]{1,0:T(8,128)(2,1)} collective-permute-done((bf16[128,1024]{1,0:T(8,128)(2,1)}, bf16[128,1024]{1,0:T(8,128)(2,1)}, u32[]{:S(2)}, u32[]{:S(2)}) %collective-permute-start.49) | collective-permute-done | bytes 262176 | tf_op jit(solution)/shard_map/ppermute | solution.py:25
  314.3 3.5 collective-permute-done.53
  317.9 6.8 %shard_map.147 = (bf16[512,768]{1,0:T(8,128)(2,1)S(1)}, bf16[384,1024]{1,0:T(8,128)(2,1)S(1)}, bf16[128,1024]{1,0:T(8,128)(2,1)S(1)}) custom-call(bf16[384,1024]{1,0:T(8,128)(2,1)S(1)} %pad_maximum_fusion.13.near, bf16[128,1024]{1,0:T(8,128)(2,1)S(1)} %collective-permute-done.54.far, bf16[1024,768]{1,0:T(8,128)(2,1)S(1)} %pad_maximum_fusion.3.w_qkv, ...), custom_call_target="tpu_custom_call" | custom-call | flops 4294967296 | bytes 8388608 | tf_op jit(solution)/shard_map/pallas_call | solution.py:239
  343.4 4.5 all-to-all-start
  347.9 3.5 collective-permute-done.59
  351.4 3.2 collective-permute-done.58
  364.2 6.3 %collective-permute-done.63 = bf16[128,1024]{1,0:T(8,128)(2,1)} collective-permute-done((bf16[128,1024]{1,0:T(8,128)(2,1)}, bf16[128,1024]{1,0:T(8,128)(2,1)}, u32[]{:S(2)}, u32[]{:S(2)}) %collective-permute-start.63) | collective-permute-done | bytes 262176 | tf_op jit(solution)/shard_map/ppermute | solution.py:25
  370.5 3.1 collective-permute-done.62
  377.3 4.3 all-to-all-start.1
  381.6 3.4 collective-permute-start.60
  387.0 23.2 %all-to-all-done.1 = bf16[8,544,256]{2,1,0:T(8,128)(2,1)S(1)} async-done(((bf16[8,544,256]{2,1,0:T(8,128)(2,1)}), bf16[8,544,256]{2,1,0:T(8,128)(2,1)S(1)}, u32[]{:S(2)}, u32[]{:S(2)}) %all-to-all-start.1) | async-done | bytes 2228256 | tf_op jit(solution)/shard_map/all_to_all | solution.py:429
  413.7 3.3 collective-permute-start.64
  417.6 4.5 collective-permute-done.64
  422.1 2.8 collective-permute-start.72
  424.9 7.1 %collective-permute-done.72 = bf16[196,1024]{1,0:T(8,128)(2,1)S(1)} collective-permute-done((bf16[196,1024]{1,0:T(8,128)(2,1)S(1)}, bf16[196,1024]{1,0:T(8,128)(2,1)S(1)}, u32[]{:S(2)}, u32[]{:S(2)}) %collective-permute-start.72) | collective-permute-done | bytes 401440 | tf_op jit(solution)/shard_map/ppermute | solution.py:33
  432.5 27.1 %all_to_all.36 = bf16[8,128,1024]{2,1,0:T(8,128)(2,1)} all-to-all(bf16[8,128,1024]{2,1,0:T(8,128)(2,1)S(1)} %broadcast_in_dim.113), channel_id=1, replica_groups=mesh['section'=2,'zlo'=2,'x'=4,'core'=2,'tensor'=4] {'zlo','x'}, dimensions={0} | all-to-all | bytes 4194304 | tf_op jit(solution)/shard_map/all_to_all | solution.py:436
  459.5 5.0 collective-permute-start.73
  465.7 4.3 all-to-all-start.3
  475.2 2.8 maximum_convert_fusion
  477.9 8.7 %all-to-all-done.3 = bf16[8,272,256]{2,1,0:T(8,128)(2,1)} async-done(((bf16[8,272,256]{2,1,0:T(8,128)(2,1)}), bf16[8,272,256]{2,1,0:T(8,128)(2,1)}, u32[]{:S(2)}, u32[]{:S(2)}) %all-to-all-start.3) | async-done | bytes 1114144 | tf_op jit(solution)/shard_map/all_to_all | solution.py:436
  (548 shorter events, 214.0 us)
Async XLA Ops:
  7.2 349.6 %reduce-scatter.2.cloned.1.call-start = ((), (), s32[]{:S(2)}) async-start(), calls=%async_computation.5 | async-start | bytes 2359296 | tf_op jit(solution)/shard_map/reduce_scatter | solution.py:425
  8.4 23.8 %collective-permute-start.1 = (bf16[128,1024]{1,0:T(8,128)(2,1)S(1)}, bf16[128,1024]{1,0:T(8,128)(2,1)S(1)}, u32[]{:S(2)}, u32[]{:S(2)}) collective-permute-start(bf16[128,1024]{1,0:T(8,128)(2,1)S(1)} %get-tuple-element.223), channel_id=1, source_target_pairs={{0,1},{1,2},{2,3},{3,0},{4,5},{5,6},{6,7},{7,4},{8,9},{9,10},{10,1... | collective-permute-start | bytes 786440 | tf_op jit(solution)/shard_map/ppermute | solution.py:25
  10.6 21.6 %collective-permute-start = (bf16[128,1024]{1,0:T(8,128)(2,1)S(1)}, bf16[128,1024]{1,0:T(8,128)(2,1)S(1)}, u32[]{:S(2)}, u32[]{:S(2)}) collective-permute-start(bf16[128,1024]{1,0:T(8,128)(2,1)S(1)} %get-tuple-element.223), channel_id=1, source_target_pairs={{0,3},{1,0},{2,1},{3,2},{4,7},{5,4},{6,5},{7,6},{8,11},{9,8},{10,9... | collective-permute-start | bytes 786440 | tf_op jit(solution)/shard_map/ppermute | solution.py:25
  12.1 22.3 %collective-permute-start.2 = (bf16[128,1024]{1,0:T(8,128)(2,1)S(1)}, bf16[128,1024]{1,0:T(8,128)(2,1)S(1)}, u32[]{:S(2)}, u32[]{:S(2)}) collective-permute-start(bf16[128,1024]{1,0:T(8,128)(2,1)S(1)} %get-tuple-element.223), channel_id=1, source_target_pairs={{0,2},{1,3},{2,0},{3,1},{4,6},{5,7},{6,4},{7,5},{8,10},{9,11},{10,... | collective-permute-start | bytes 786440 | tf_op jit(solution)/shard_map/ppermute | solution.py:25
  14.7 13.1 %collective-permute-start.4 = (bf16[128,1024]{1,0:T(8,128)(2,1)S(1)}, bf16[128,1024]{1,0:T(8,128)(2,1)S(1)}, u32[]{:S(2)}, u32[]{:S(2)}) collective-permute-start(bf16[128,1024]{1,0:T(8,128)(2,1)S(1)} %constant_dynamic-slice_fusion.3), channel_id=1, source_target_pairs={{0,96},{32,64},{64,32},{96,0},{1,97},{33,65},{65,33},{97,1},{2,98}... | collective-permute-start | bytes 786440 | tf_op jit(solution)/shard_map/ppermute | solution.py:37
  25.0 18.8 %collective-permute-start.3 = (bf16[1536,256]{1,0:T(8,128)(2,1)}, bf16[1536,256]{1,0:T(8,128)(2,1)}, u32[]{:S(2)}, u32[]{:S(2)}) collective-permute-start(bf16[1536,256]{1,0:T(8,128)(2,1)} %constant_dynamic-slice_fusion.4), channel_id=1, source_target_pairs={{0,96},{32,64},{64,32},{96,0},{1,97},{33,65},{65,33},{97,1},{2,98}... | collective-permute-start | bytes 2359304 | tf_op jit(solution)/shard_map/ppermute | solution.py:37
  32.2 35.0 %collective-permute-start.13 = (bf16[328,1024]{1,0:T(8,128)(2,1)}, bf16[328,1024]{1,0:T(8,128)(2,1)}, u32[]{:S(2)}, u32[]{:S(2)}) collective-permute-start(bf16[328,1024]{1,0:T(8,128)(2,1)} %constant_dynamic-slice_fusion.2), channel_id=1, source_target_pairs={{0,96},{32,64},{64,32},{96,0},{1,97},{33,65},{65,33},{97,1},{2,98}... | collective-permute-start | bytes 2015240 | tf_op jit(solution)/shard_map/ppermute | solution.py:37
  65.9 13.1 %collective-permute-start.8 = (bf16[128,1024]{1,0:T(8,128)(2,1)S(1)}, bf16[128,1024]{1,0:T(8,128)(2,1)S(1)}, u32[]{:S(2)}, u32[]{:S(2)}) collective-permute-start(bf16[128,1024]{1,0:T(8,128)(2,1)S(1)} %get-tuple-element.102), channel_id=1, source_target_pairs={{0,2},{1,3},{2,0},{3,1},{4,6},{5,7},{6,4},{7,5},{8,10},{9,11},{10,... | collective-permute-start | bytes 786440 | tf_op jit(solution)/shard_map/ppermute | solution.py:25
  67.2 17.4 %collective-permute-start.15 = (bf16[328,1024]{1,0:T(8,128)(2,1)S(1)}, bf16[328,1024]{1,0:T(8,128)(2,1)S(1)}, u32[]{:S(2)}, u32[]{:S(2)}) collective-permute-start(bf16[328,1024]{1,0:T(8,128)(2,1)S(1)} %constant_dynamic-slice_fusion.1), channel_id=1, source_target_pairs={{0,96},{32,64},{64,32},{96,0},{1,97},{33,65},{65,33},{97,1},{2,98}... | collective-permute-start | bytes 2015240 | tf_op jit(solution)/shard_map/ppermute | solution.py:37
  70.2 21.8 %collective-permute-start.14 = (bf16[328,1024]{1,0:T(8,128)(2,1)}, bf16[328,1024]{1,0:T(8,128)(2,1)S(1)}, u32[]{:S(2)}, u32[]{:S(2)}) collective-permute-start(bf16[328,1024]{1,0:T(8,128)(2,1)} %collective-permute-done.13), channel_id=1, source_target_pairs={{0,4},{4,0},{1,5},{5,1},{2,6},{6,2},{3,7},{7,3},{8,12},{12,8},{9,1... | collective-permute-start | bytes 2015240 | tf_op jit(solution)/shard_map/ppermute | solution.py:29
  84.7 16.3 %collective-permute-start.17 = (bf16[328,1024]{1,0:T(8,128)(2,1)S(1)}, bf16[328,1024]{1,0:T(8,128)(2,1)S(1)}, u32[]{:S(2)}, u32[]{:S(2)}) collective-permute-start(bf16[328,1024]{1,0:T(8,128)(2,1)S(1)} %constant_dynamic-slice_fusion), channel_id=1, source_target_pairs={{0,96},{32,64},{64,32},{96,0},{1,97},{33,65},{65,33},{97,1},{2,98}... | collective-permute-start | bytes 2015240 | tf_op jit(solution)/shard_map/ppermute | solution.py:37
  87.3 16.3 %collective-permute-start.16 = (bf16[328,1024]{1,0:T(8,128)(2,1)S(1)}, bf16[328,1024]{1,0:T(8,128)(2,1)S(1)}, u32[]{:S(2)}, u32[]{:S(2)}) collective-permute-start(bf16[328,1024]{1,0:T(8,128)(2,1)S(1)} %collective-permute-done.15), channel_id=1, source_target_pairs={{0,4},{4,0},{1,5},{5,1},{2,6},{6,2},{3,7},{7,3},{8,12},{12,8},{9,1... | collective-permute-start | bytes 2015240 | tf_op jit(solution)/shard_map/ppermute | solution.py:29
  115.3 14.4 %collective-permute-start.21 = (bf16[128,1024]{1,0:T(8,128)(2,1)S(1)}, bf16[128,1024]{1,0:T(8,128)(2,1)S(1)}, u32[]{:S(2)}, u32[]{:S(2)}) collective-permute-start(bf16[128,1024]{1,0:T(8,128)(2,1)S(1)} %get-tuple-element.306), channel_id=1, source_target_pairs={{0,1},{1,2},{2,3},{3,0},{4,5},{5,6},{6,7},{7,4},{8,9},{9,10},{10,1... | collective-permute-start | bytes 786440 | tf_op jit(solution)/shard_map/ppermute | solution.py:25
  118.1 11.7 %collective-permute-start.20 = (bf16[128,1024]{1,0:T(8,128)(2,1)S(1)}, bf16[128,1024]{1,0:T(8,128)(2,1)S(1)}, u32[]{:S(2)}, u32[]{:S(2)}) collective-permute-start(bf16[128,1024]{1,0:T(8,128)(2,1)S(1)} %convolution_convert_fusion.13), channel_id=1, source_target_pairs={{0,2},{1,3},{2,0},{3,1},{4,6},{5,7},{6,4},{7,5},{8,10},{9,11},{10,... | collective-permute-start | bytes 786440 | tf_op jit(solution)/shard_map/ppermute | solution.py:25
  131.2 23.3 %collective-permute-start.24 = (bf16[128,1024]{1,0:T(8,128)(2,1)}, bf16[128,1024]{1,0:T(8,128)(2,1)}, u32[]{:S(2)}, u32[]{:S(2)}) collective-permute-start(bf16[128,1024]{1,0:T(8,128)(2,1)} %fusion.46), channel_id=1, source_target_pairs={{0,1},{1,2},{2,3},{3,0},{4,5},{5,6},{6,7},{7,4},{8,9},{9,10},{10,1... | collective-permute-start | bytes 786440 | tf_op jit(solution)/shard_map/ppermute | solution.py:25
  131.2 23.3 %collective-permute-start.23 = (bf16[128,1024]{1,0:T(8,128)(2,1)}, bf16[128,1024]{1,0:T(8,128)(2,1)}, u32[]{:S(2)}, u32[]{:S(2)}) collective-permute-start(bf16[128,1024]{1,0:T(8,128)(2,1)} %fusion.46), channel_id=1, source_target_pairs={{0,3},{1,0},{2,1},{3,2},{4,7},{5,4},{6,5},{7,6},{8,11},{9,8},{10,9... | collective-permute-start | bytes 786440 | tf_op jit(solution)/shard_map/ppermute | solution.py:25
  140.5 20.3 %collective-permute-start.25 = (bf16[128,1024]{1,0:T(8,128)(2,1)}, bf16[128,1024]{1,0:T(8,128)(2,1)S(1)}, u32[]{:S(2)}, u32[]{:S(2)}) collective-permute-start(bf16[128,1024]{1,0:T(8,128)(2,1)} %fusion.46), channel_id=1, source_target_pairs={{0,2},{1,3},{2,0},{3,1},{4,6},{5,7},{6,4},{7,5},{8,10},{9,11},{10,... | collective-permute-start | bytes 786440 | tf_op jit(solution)/shard_map/ppermute | solution.py:25
  167.6 19.1 %collective-permute-start.33 = (bf16[128,1024]{1,0:T(8,128)(2,1)S(1)}, bf16[128,1024]{1,0:T(8,128)(2,1)S(1)}, u32[]{:S(2)}, u32[]{:S(2)}) collective-permute-start(bf16[128,1024]{1,0:T(8,128)(2,1)S(1)} %select_bitcast_fusion.9), channel_id=1, source_target_pairs={{0,1},{1,2},{2,3},{3,0},{4,5},{5,6},{6,7},{7,4},{8,9},{9,10},{10,1... | collective-permute-start | bytes 786440 | tf_op jit(solution)/shard_map/ppermute | solution.py:25
  169.5 17.2 %collective-permute-start.32 = (bf16[128,1024]{1,0:T(8,128)(2,1)S(1)}, bf16[128,1024]{1,0:T(8,128)(2,1)S(1)}, u32[]{:S(2)}, u32[]{:S(2)}) collective-permute-start(bf16[128,1024]{1,0:T(8,128)(2,1)S(1)} %select_bitcast_fusion.9), channel_id=1, source_target_pairs={{0,3},{1,0},{2,1},{3,2},{4,7},{5,4},{6,5},{7,6},{8,11},{9,8},{10,9... | collective-permute-start | bytes 786440 | tf_op jit(solution)/shard_map/ppermute | solution.py:25
  171.0 16.8 %collective-permute-start.34 = (bf16[128,1024]{1,0:T(8,128)(2,1)S(1)}, bf16[128,1024]{1,0:T(8,128)(2,1)S(1)}, u32[]{:S(2)}, u32[]{:S(2)}) collective-permute-start(bf16[128,1024]{1,0:T(8,128)(2,1)S(1)} %select_bitcast_fusion.9), channel_id=1, source_target_pairs={{0,2},{1,3},{2,0},{3,1},{4,6},{5,7},{6,4},{7,5},{8,10},{9,11},{10,... | collective-permute-start | bytes 786440 | tf_op jit(solution)/shard_map/ppermute | solution.py:25
  177.4 20.6 %collective-permute-start.30 = (bf16[128,1024]{1,0:T(8,128)(2,1)S(1)}, bf16[128,1024]{1,0:T(8,128)(2,1)S(1)}, u32[]{:S(2)}, u32[]{:S(2)}) collective-permute-start(bf16[128,1024]{1,0:T(8,128)(2,1)S(1)} %multiply_convert_fusion.4), channel_id=1, source_target_pairs={{0,1},{1,2},{2,3},{3,0},{4,5},{5,6},{6,7},{7,4},{8,9},{9,10},{10,1... | collective-permute-start | bytes 786440 | tf_op jit(solution)/shard_map/ppermute | solution.py:25
  177.8 20.1 %collective-permute-start.29 = (bf16[128,1024]{1,0:T(8,128)(2,1)S(1)}, bf16[128,1024]{1,0:T(8,128)(2,1)S(1)}, u32[]{:S(2)}, u32[]{:S(2)}) collective-permute-start(bf16[128,1024]{1,0:T(8,128)(2,1)S(1)} %multiply_convert_fusion.4), channel_id=1, source_target_pairs={{0,3},{1,0},{2,1},{3,2},{4,7},{5,4},{6,5},{7,6},{8,11},{9,8},{10,9... | collective-permute-start | bytes 786440 | tf_op jit(solution)/shard_map/ppermute | solution.py:25
  187.9 15.0 %collective-permute-start.31 = (bf16[128,1024]{1,0:T(8,128)(2,1)S(1)}, bf16[128,1024]{1,0:T(8,128)(2,1)S(1)}, u32[]{:S(2)}, u32[]{:S(2)}) collective-permute-start(bf16[128,1024]{1,0:T(8,128)(2,1)S(1)} %multiply_convert_fusion.4), channel_id=1, source_target_pairs={{0,2},{1,3},{2,0},{3,1},{4,6},{5,7},{6,4},{7,5},{8,10},{9,11},{10,... | collective-permute-start | bytes 786440 | tf_op jit(solution)/shard_map/ppermute | solution.py:25
  219.2 11.8 %collective-permute-start.39 = (bf16[128,1024]{1,0:T(8,128)(2,1)S(1)}, bf16[128,1024]{1,0:T(8,128)(2,1)S(1)}, u32[]{:S(2)}, u32[]{:S(2)}) collective-permute-start(bf16[128,1024]{1,0:T(8,128)(2,1)S(1)} %get-tuple-element.232), channel_id=1, source_target_pairs={{0,1},{1,2},{2,3},{3,0},{4,5},{5,6},{6,7},{7,4},{8,9},{9,10},{10,1... | collective-permute-start | bytes 786440 | tf_op jit(solution)/shard_map/ppermute | solution.py:25
  219.3 11.7 %collective-permute-start.38 = (bf16[128,1024]{1,0:T(8,128)(2,1)S(1)}, bf16[128,1024]{1,0:T(8,128)(2,1)S(1)}, u32[]{:S(2)}, u32[]{:S(2)}) collective-permute-start(bf16[128,1024]{1,0:T(8,128)(2,1)S(1)} %get-tuple-element.232), channel_id=1, source_target_pairs={{0,3},{1,0},{2,1},{3,2},{4,7},{5,4},{6,5},{7,6},{8,11},{9,8},{10,9... | collective-permute-start | bytes 786440 | tf_op jit(solution)/shard_map/ppermute | solution.py:25
  223.7 43.0 %collective-permute-start.48 = (bf16[328,1024]{1,0:T(8,128)(2,1)}, bf16[328,1024]{1,0:T(8,128)(2,1)}, u32[]{:S(2)}, u32[]{:S(2)}) collective-permute-start(bf16[328,1024]{1,0:T(8,128)(2,1)} %convolution_convert_fusion.7), channel_id=1, source_target_pairs={{0,4},{4,0},{1,5},{5,1},{2,6},{6,2},{3,7},{7,3},{8,12},{12,8},{9,1... | collective-permute-start | bytes 2015240 | tf_op jit(solution)/shard_map/ppermute | solution.py:29
  230.2 43.5 %collective-permute-start.47 = (bf16[656,1024]{1,0:T(8,128)(2,1)}, bf16[656,1024]{1,0:T(8,128)(2,1)}, u32[]{:S(2)}, u32[]{:S(2)}) collective-permute-start(bf16[656,1024]{1,0:T(8,128)(2,1)} %convolution_convert_fusion.1), channel_id=1, source_target_pairs={{0,4},{4,0},{1,5},{5,1},{2,6},{6,2},{3,7},{7,3},{8,12},{12,8},{9,1... | collective-permute-start | bytes 4030472 | tf_op jit(solution)/shard_map/ppermute | solution.py:29
  239.4 11.8 %collective-permute-start.41 = (bf16[128,1024]{1,0:T(8,128)(2,1)S(1)}, bf16[128,1024]{1,0:T(8,128)(2,1)S(1)}, u32[]{:S(2)}, u32[]{:S(2)}) collective-permute-start(bf16[128,1024]{1,0:T(8,128)(2,1)S(1)} %get-tuple-element.135), channel_id=1, source_target_pairs={{0,2},{1,3},{2,0},{3,1},{4,6},{5,7},{6,4},{7,5},{8,10},{9,11},{10,... | collective-permute-start | bytes 786440 | tf_op jit(solution)/shard_map/ppermute | solution.py:25
  252.2 16.7 %collective-permute-start.45 = (bf16[128,1024]{1,0:T(8,128)(2,1)S(1)}, bf16[128,1024]{1,0:T(8,128)(2,1)}, u32[]{:S(2)}, u32[]{:S(2)}) collective-permute-start(bf16[128,1024]{1,0:T(8,128)(2,1)S(1)} %add_convert_fusion.9), channel_id=1, source_target_pairs={{0,1},{1,2},{2,3},{3,0},{4,5},{5,6},{6,7},{7,4},{8,9},{9,10},{10,1... | collective-permute-start | bytes 786440 | tf_op jit(solution)/shard_map/ppermute | solution.py:25
  252.3 16.9 %collective-permute-start.44 = (bf16[128,1024]{1,0:T(8,128)(2,1)S(1)}, bf16[128,1024]{1,0:T(8,128)(2,1)}, u32[]{:S(2)}, u32[]{:S(2)}) collective-permute-start(bf16[128,1024]{1,0:T(8,128)(2,1)S(1)} %add_convert_fusion.9), channel_id=1, source_target_pairs={{0,3},{1,0},{2,1},{3,2},{4,7},{5,4},{6,5},{7,6},{8,11},{9,8},{10,9... | collective-permute-start | bytes 786440 | tf_op jit(solution)/shard_map/ppermute | solution.py:25
  257.3 13.9 %collective-permute-start.67 = (bf16[1024,256]{1,0:T(8,128)(2,1)}, bf16[1024,256]{1,0:T(8,128)(2,1)}, u32[]{:S(2)}, u32[]{:S(2)}) collective-permute-start(bf16[1024,256]{1,0:T(8,128)(2,1)} %convolution_convert_fusion.9), channel_id=1, source_target_pairs={{0,4},{4,0},{1,5},{5,1},{2,6},{6,2},{3,7},{7,3},{8,12},{12,8},{9,1... | collective-permute-start | bytes 1572872 | tf_op jit(solution)/shard_map/ppermute | solution.py:29
  268.9 22.5 %collective-permute-start.68 = (bf16[1024,256]{1,0:T(8,128)(2,1)}, bf16[1024,256]{1,0:T(8,128)(2,1)S(1)}, u32[]{:S(2)}, u32[]{:S(2)}) collective-permute-start(bf16[1024,256]{1,0:T(8,128)(2,1)} %convolution_convert_fusion.8), channel_id=1, source_target_pairs={{0,4},{4,0},{1,5},{5,1},{2,6},{6,2},{3,7},{7,3},{8,12},{12,8},{9,1... | collective-permute-start | bytes 1572872 | tf_op jit(solution)/shard_map/ppermute | solution.py:29
  288.2 12.1 %collective-permute-start.49 = (bf16[128,1024]{1,0:T(8,128)(2,1)}, bf16[128,1024]{1,0:T(8,128)(2,1)}, u32[]{:S(2)}, u32[]{:S(2)}) collective-permute-start(bf16[128,1024]{1,0:T(8,128)(2,1)} %convolution_convert_fusion.14), channel_id=1, source_target_pairs={{0,2},{1,3},{2,0},{3,1},{4,6},{5,7},{6,4},{7,5},{8,10},{9,11},{10,... | collective-permute-start | bytes 786440 | tf_op jit(solution)/shard_map/ppermute | solution.py:25
  304.4 13.4 %collective-permute-start.53 = (bf16[128,1024]{1,0:T(8,128)(2,1)S(1)}, bf16[128,1024]{1,0:T(8,128)(2,1)S(1)}, u32[]{:S(2)}, u32[]{:S(2)}) collective-permute-start(bf16[128,1024]{1,0:T(8,128)(2,1)S(1)} %get-tuple-element.226), channel_id=1, source_target_pairs={{0,1},{1,2},{2,3},{3,0},{4,5},{5,6},{6,7},{7,4},{8,9},{9,10},{10,1... | collective-permute-start | bytes 786440 | tf_op jit(solution)/shard_map/ppermute | solution.py:25
  304.4 13.4 %collective-permute-start.52 = (bf16[128,1024]{1,0:T(8,128)(2,1)S(1)}, bf16[128,1024]{1,0:T(8,128)(2,1)S(1)}, u32[]{:S(2)}, u32[]{:S(2)}) collective-permute-start(bf16[128,1024]{1,0:T(8,128)(2,1)S(1)} %get-tuple-element.226), channel_id=1, source_target_pairs={{0,3},{1,0},{2,1},{3,2},{4,7},{5,4},{6,5},{7,6},{8,11},{9,8},{10,9... | collective-permute-start | bytes 786440 | tf_op jit(solution)/shard_map/ppermute | solution.py:25
  312.0 18.4 %collective-permute-start.56 = (bf16[328,1024]{1,0:T(8,128)(2,1)S(1)}, bf16[328,1024]{1,0:T(8,128)(2,1)S(1)}, u32[]{:S(2)}, u32[]{:S(2)}) collective-permute-start(bf16[328,1024]{1,0:T(8,128)(2,1)S(1)} %convolution_convert_fusion.6), channel_id=1, source_target_pairs={{0,4},{4,0},{1,5},{5,1},{2,6},{6,2},{3,7},{7,3},{8,12},{12,8},{9,1... | collective-permute-start | bytes 2015240 | tf_op jit(solution)/shard_map/ppermute | solution.py:29
  314.0 19.2 %collective-permute-start.55 = (bf16[656,1024]{1,0:T(8,128)(2,1)S(1)}, bf16[656,1024]{1,0:T(8,128)(2,1)S(1)}, u32[]{:S(2)}, u32[]{:S(2)}) collective-permute-start(bf16[656,1024]{1,0:T(8,128)(2,1)S(1)} %convolution_convert_fusion), channel_id=1, source_target_pairs={{0,4},{4,0},{1,5},{5,1},{2,6},{6,2},{3,7},{7,3},{8,12},{12,8},{9,1... | collective-permute-start | bytes 4030472 | tf_op jit(solution)/shard_map/ppermute | solution.py:29
  327.0 15.4 %collective-permute-start.66 = (bf16[1024,256]{1,0:T(8,128)(2,1)S(1)}, bf16[1024,256]{1,0:T(8,128)(2,1)S(1)}, u32[]{:S(2)}, u32[]{:S(2)}) collective-permute-start(bf16[1024,256]{1,0:T(8,128)(2,1)S(1)} %convolution_convert_fusion.10), channel_id=1, source_target_pairs={{0,4},{4,0},{1,5},{5,1},{2,6},{6,2},{3,7},{7,3},{8,12},{12,8},{9,1... | collective-permute-start | bytes 1572872 | tf_op jit(solution)/shard_map/ppermute | solution.py:29
  337.5 14.0 %collective-permute-start.59 = (bf16[128,1024]{1,0:T(8,128)(2,1)}, bf16[128,1024]{1,0:T(8,128)(2,1)}, u32[]{:S(2)}, u32[]{:S(2)}) collective-permute-start(bf16[128,1024]{1,0:T(8,128)(2,1)} %get-tuple-element.297), channel_id=1, source_target_pairs={{0,3},{1,0},{2,1},{3,2},{4,7},{5,4},{6,5},{7,6},{8,11},{9,8},{10,9... | collective-permute-start | bytes 786440 | tf_op jit(solution)/shard_map/ppermute | solution.py:25
  340.1 14.5 %collective-permute-start.58 = (bf16[128,1024]{1,0:T(8,128)(2,1)}, bf16[128,1024]{1,0:T(8,128)(2,1)}, u32[]{:S(2)}, u32[]{:S(2)}) collective-permute-start(bf16[128,1024]{1,0:T(8,128)(2,1)} %get-tuple-element.296), channel_id=1, source_target_pairs={{0,1},{1,2},{2,3},{3,0},{4,5},{5,6},{6,7},{7,4},{8,9},{9,10},{10,1... | collective-permute-start | bytes 786440 | tf_op jit(solution)/shard_map/ppermute | solution.py:25
  341.3 13.4 %collective-permute-start.57 = (bf16[128,1024]{1,0:T(8,128)(2,1)}, bf16[128,1024]{1,0:T(8,128)(2,1)S(1)}, u32[]{:S(2)}, u32[]{:S(2)}) collective-permute-start(bf16[128,1024]{1,0:T(8,128)(2,1)} %convolution_convert_fusion.12), channel_id=1, source_target_pairs={{0,2},{1,3},{2,0},{3,1},{4,6},{5,7},{6,4},{7,5},{8,10},{9,11},{10,... | collective-permute-start | bytes 786440 | tf_op jit(solution)/shard_map/ppermute | solution.py:25
  343.4 33.9 %all-to-all-start = ((bf16[8,128,1024]{2,1,0:T(8,128)(2,1)}), bf16[8,128,1024]{2,1,0:T(8,128)(2,1)}, u32[]{:S(2)}, u32[]{:S(2)}) async-start(bf16[8,128,1024]{2,1,0:T(8,128)(2,1)} %bitcast.149), calls=%async_computation.1 | async-start | bytes 4194304 | tf_op jit(solution)/shard_map/all_to_all | solution.py:429
  358.0 15.5 %collective-permute-start.61 = (bf16[128,1024]{1,0:T(8,128)(2,1)S(1)}, bf16[128,1024]{1,0:T(8,128)(2,1)S(1)}, u32[]{:S(2)}, u32[]{:S(2)}) collective-permute-start(bf16[128,1024]{1,0:T(8,128)(2,1)S(1)} %copy-done.11), channel_id=1, source_target_pairs={{0,2},{1,3},{2,0},{3,1},{4,6},{5,7},{6,4},{7,5},{8,10},{9,11},{10,... | collective-permute-start | bytes 786440 | tf_op jit(solution)/shard_map/ppermute | solution.py:25
  358.8 11.7 %collective-permute-start.63 = (bf16[128,1024]{1,0:T(8,128)(2,1)}, bf16[128,1024]{1,0:T(8,128)(2,1)}, u32[]{:S(2)}, u32[]{:S(2)}) collective-permute-start(bf16[128,1024]{1,0:T(8,128)(2,1)} %get-tuple-element.295), channel_id=1, source_target_pairs={{0,3},{1,0},{2,1},{3,2},{4,7},{5,4},{6,5},{7,6},{8,11},{9,8},{10,9... | collective-permute-start | bytes 786440 | tf_op jit(solution)/shard_map/ppermute | solution.py:25
  359.2 14.4 %collective-permute-start.62 = (bf16[128,1024]{1,0:T(8,128)(2,1)}, bf16[128,1024]{1,0:T(8,128)(2,1)}, u32[]{:S(2)}, u32[]{:S(2)}) collective-permute-start(bf16[128,1024]{1,0:T(8,128)(2,1)} %get-tuple-element.294), channel_id=1, source_target_pairs={{0,1},{1,2},{2,3},{3,0},{4,5},{5,6},{6,7},{7,4},{8,9},{9,10},{10,1... | collective-permute-start | bytes 786440 | tf_op jit(solution)/shard_map/ppermute | solution.py:25
  377.3 32.9 %all-to-all-start.1 = ((bf16[8,544,256]{2,1,0:T(8,128)(2,1)}), bf16[8,544,256]{2,1,0:T(8,128)(2,1)S(1)}, u32[]{:S(2)}, u32[]{:S(2)}) async-start(bf16[8,544,256]{2,1,0:T(8,128)(2,1)} %bitcast.44), calls=%async_computation.2 | async-start | bytes 4456448 | tf_op jit(solution)/shard_map/all_to_all | solution.py:429
  381.6 36.0 %collective-permute-start.60 = (bf16[128,1024]{1,0:T(8,128)(2,1)S(1)}, bf16[128,1024]{1,0:T(8,128)(2,1)}, u32[]{:S(2)}, u32[]{:S(2)}) collective-permute-start(bf16[128,1024]{1,0:T(8,128)(2,1)S(1)} %copy-done.88), channel_id=1, source_target_pairs={{0,64},{64,0},{1,65},{65,1},{2,66},{66,2},{3,67},{67,3},{4,68},{68... | collective-permute-start | bytes 786440 | tf_op jit(solution)/shard_map/ppermute | solution.py:33
  465.7 20.9 %all-to-all-start.3 = ((bf16[8,272,256]{2,1,0:T(8,128)(2,1)}), bf16[8,272,256]{2,1,0:T(8,128)(2,1)}, u32[]{:S(2)}, u32[]{:S(2)}) async-start(bf16[8,272,256]{2,1,0:T(8,128)(2,1)} %broadcast_in_dim.114), calls=%async_computation.4 | async-start | bytes 2228224 | tf_op jit(solution)/shard_map/all_to_all | solution.py:436
  (129 other events, 1257.7 us)
Sparse Core Ops, SparseCore 0:
  292.5 36.2 reduce-scatter.1

commit v5 on v4

--- a/solution.py
+++ b/solution.py
@@ -543,7 +543,7 @@
     attn_width = attn_pack0.shape[1]
     packs = [pack.reshape(8, -1, attn_width) for pack in (attn_pack0, attn_pack1)]
     attn_rows = packs[0].shape[1]
-    attn_both = after_all(joined(packs, 1).reshape(-1, attn_width), in0, out1)
+    attn_both = after_all(joined(packs, 1).reshape(-1, attn_width), in0)
     attn_both = reduce_part_now(attn_both)
     gain_start = 2 * model_width % attn_rows
     holds_gains = lax.axis_index(("zlo", "x")) == 2 * model_width // attn_rows

time: 515 us -> 496 us (0.963)
  waiting for transfers between devices: 152 us -> 138 us
  starting transfers between devices: 139 us -> 130 us
    all_to_all x2, waiting for transfers between devices: 23.2 us -> 10.5 us  [reduce_part_now(): pieces = lax.all_to_all(grads, ('zlo', 'x'), 0, 0, tiled=True)]
    ppermute x51, starting transfers between devices: 69.1 us -> 60 us  [around(): lax.ppermute(block, axis, [(i, (i + distance) % count) for i in range(cou...]
  transfers between devices with their start and end apart: 79 -> 79, of which waited for: 33 -> 35; matrix products, arithmetic and copies ran while one was open for 25% -> 27% of each run, Pallas kernels for 4% -> 4%
where the time goes in v5:
time: 496 us; the launch traced here: 486 us
  waiting for transfers between devices  138 us (28%)
  starting transfers between devices  130 us (26%)
  other arithmetic  72.3 us (15%)
  matrix products  43.5 us (9%)
  local copies, waits for them, and re-layouts  35.1 us (7%)
  blocking collectives  27.1 us (5%)
  Pallas kernels  23.1 us (5%)
  between operations  16.7 us (3%)
    ppermute x51, waiting for transfers between devices, around(): lax.ppermute(block, axis, [(i, (i + distance) % count) for i in range(cou...  93.1 us
    ppermute x51, starting transfers between devices, around(): lax.ppermute(block, axis, [(i, (i + distance) % count) for i in range(cou...  60 us
    ppermute x15, starting transfers between devices, swap_core(): return lax.ppermute(block, 'core', [(0, 1), (1, 0)])  34.2 us
    all_to_all x1, blocking collectives, spread_part(): return lax.all_to_all(copies, ('zlo', 'x'), 0, 0, tiled=True)  27.1 us
    pallas_call x4, Pallas kernels, whole_call(): pl.pallas_call(kernel, out_shape=[jax.ShapeDtypeStruct(*shape) for shape...  23.1 us
    dot_general x16, matrix products, contract_rows(): lax.dot_general(left_rows, right_rows, (((0,), (0,)), ((), ())), preferre...  19.9 us
    concatenate x16, other arithmetic, joined(): return jnp.concatenate(parts, axis=axis)  14.4 us
    dot_general x8, matrix products, contract_last(): lax.dot_general(left_rows, weight, (((1,), (1,)), ((), ())), preferred_el...  14.3 us
  transfers between devices with their start and end apart: 79, of which 35 were waited for; matrix products, arithmetic and copies ran while one was open for 27% of the time, Pallas kernels for 4%

profile of v5, /device:TPU:1, one launch (start us, length us, event | category | flops | bytes accessed | tf_op | source)
XLA Modules:
  0.0 486.1 jit_solution(12973048221122396072)
XLA Ops:
  15.2 3.8 collective-permute-start.4
  20.0 3.6 slice_bitcast_fusion.1
  34.2 9.0 %collective-permute-done.3 = bf16[1536,256]{1,0:T(8,128)(2,1)S(1)} collective-permute-done((bf16[1536,256]{1,0:T(8,128)(2,1)}, bf16[1536,256]{1,0:T(8,128)(2,1)S(1)}, u32[]{:S(2)}, u32[]{:S(2)}) %collective-permute-start.3) | collective-permute-done | bytes 786464 | tf_op jit(solution)/shard_map/ppermute | solution.py:37
  44.2 5.2 %collective-permute-start.6 = (bf16[1536,256]{1,0:T(8,128)(2,1)S(1)}, bf16[1536,256]{1,0:T(8,128)(2,1)}, u32[]{:S(2)}, u32[]{:S(2)}) collective-permute-start(bf16[1536,256]{1,0:T(8,128)(2,1)S(1)} %collective-permute-done.3), channel_id=1, source_target_pairs={{0,4},{4,0},{1,5},{5,1},{2,6},{6,2},{3,7},{7,3},{8,12},{12,8},{9,1... | collective-permute-start | bytes 2359304 | tf_op jit(solution)/shard_map/ppermute | solution.py:29
  58.5 4.8 shard_map.144
  66.4 2.8 collective-permute-start.15
  73.8 4.3 collective-permute-done.8
  78.9 2.7 collective-permute-start.11
  92.2 5.0 %collective-permute-done.18 = bf16[128,1024]{1,0:T(8,128)(2,1)S(1)} collective-permute-done((bf16[128,1024]{1,0:T(8,128)(2,1)S(1)}, bf16[128,1024]{1,0:T(8,128)(2,1)S(1)}, u32[]{:S(2)}, u32[]{:S(2)}) %collective-permute-start.18) | collective-permute-done | bytes 262176 | tf_op jit(solution)/shard_map/ppermute | solution.py:25
  106.8 3.0 multiply_convert_fusion.3
  120.6 8.1 %collective-permute-done.21 = bf16[128,1024]{1,0:T(8,128)(2,1)S(1)} collective-permute-done((bf16[128,1024]{1,0:T(8,128)(2,1)S(1)}, bf16[128,1024]{1,0:T(8,128)(2,1)S(1)}, u32[]{:S(2)}, u32[]{:S(2)}) %collective-permute-start.21) | collective-permute-done | bytes 262176 | tf_op jit(solution)/shard_map/ppermute | solution.py:25
  130.2 2.7 collective-permute-start.23
  142.4 5.1 %collective-permute-done.25.far = bf16[128,1024]{1,0:T(8,128)(2,1)S(1)} collective-permute-done((bf16[128,1024]{1,0:T(8,128)(2,1)}, bf16[128,1024]{1,0:T(8,128)(2,1)S(1)}, u32[]{:S(2)}, u32[]{:S(2)}) %collective-permute-start.25) | collective-permute-done | bytes 262176 | tf_op jit(solution)/shard_map/ppermute | solution.py:25
  147.5 4.9 shard_map.145
  158.5 3.6 collective-permute-done.27
  167.5 5.8 %collective-permute-done.33 = bf16[128,1024]{1,0:T(8,128)(2,1)S(1)} collective-permute-done((bf16[128,1024]{1,0:T(8,128)(2,1)S(1)}, bf16[128,1024]{1,0:T(8,128)(2,1)S(1)}, u32[]{:S(2)}, u32[]{:S(2)}) %collective-permute-start.33) | collective-permute-done | bytes 262176 | tf_op jit(solution)/shard_map/ppermute | solution.py:25
  177.2 7.4 %collective-permute-done.30 = bf16[128,1024]{1,0:T(8,128)(2,1)S(1)} collective-permute-done((bf16[128,1024]{1,0:T(8,128)(2,1)S(1)}, bf16[128,1024]{1,0:T(8,128)(2,1)S(1)}, u32[]{:S(2)}, u32[]{:S(2)}) %collective-permute-start.30) | collective-permute-done | bytes 262176 | tf_op jit(solution)/shard_map/ppermute | solution.py:25
  186.2 3.0 add_convert_fusion.5
  198.4 6.5 %collective-permute-done.35 = bf16[128,1024]{1,0:T(8,128)(2,1)S(1)} collective-permute-done((bf16[128,1024]{1,0:T(8,128)(2,1)S(1)}, bf16[128,1024]{1,0:T(8,128)(2,1)S(1)}, u32[]{:S(2)}, u32[]{:S(2)}) %collective-permute-start.35) | collective-permute-done | bytes 262176 | tf_op jit(solution)/shard_map/ppermute | solution.py:25
  205.9 2.7 collective-permute-start.38
  210.4 4.4 collective-permute-start.48
  217.8 6.7 %shard_map.146 = (bf16[512,768]{1,0:T(8,128)(2,1)S(1)}, bf16[384,1024]{1,0:T(8,128)(2,1)S(1)}, bf16[128,1024]{1,0:T(8,128)(2,1)S(1)}) custom-call(bf16[384,1024]{1,0:T(8,128)(2,1)S(1)} %pad_maximum_fusion.11.near, bf16[128,1024]{1,0:T(8,128)(2,1)S(1)} %collective-permute-done.40.far, bf16[1024,768]{1,0:T(8,128)(2,1)S(1)} %pad_maximum_fusion.4.w_qkv, ...), custom_call_target="tpu_custom_call" | custom-call | flops 4294967296 | bytes 8388608 | tf_op jit(solution)/shard_map/pallas_call | solution.py:239
  226.1 3.2 collective-permute-start.41
  232.3 5.7 %collective-permute-done.41 = bf16[128,1024]{1,0:T(8,128)(2,1)S(1)} collective-permute-done((bf16[128,1024]{1,0:T(8,128)(2,1)S(1)}, bf16[128,1024]{1,0:T(8,128)(2,1)S(1)}, u32[]{:S(2)}, u32[]{:S(2)}) %collective-permute-start.41) | collective-permute-done | bytes 262176 | tf_op jit(solution)/shard_map/ppermute | solution.py:25
  239.0 2.7 collective-permute-start.44
  244.1 6.4 %collective-permute-start.67 = (bf16[1024,256]{1,0:T(8,128)(2,1)}, bf16[1024,256]{1,0:T(8,128)(2,1)}, u32[]{:S(2)}, u32[]{:S(2)}) collective-permute-start(bf16[1024,256]{1,0:T(8,128)(2,1)} %convolution_convert_fusion.9), channel_id=1, source_target_pairs={{0,4},{4,0},{1,5},{5,1},{2,6},{6,2},{3,7},{7,3},{8,12},{12,8},{9,1... | collective-permute-start | bytes 1572872 | tf_op jit(solution)/shard_map/ppermute | solution.py:29
  264.2 3.8 multiply_convert_fusion
  274.9 3.1 collective-permute-start.49
  280.5 6.4 %collective-permute-done.49 = bf16[128,1024]{1,0:T(8,128)(2,1)} collective-permute-done((bf16[128,1024]{1,0:T(8,128)(2,1)}, bf16[128,1024]{1,0:T(8,128)(2,1)}, u32[]{:S(2)}, u32[]{:S(2)}) %collective-permute-start.49) | collective-permute-done | bytes 262176 | tf_op jit(solution)/shard_map/ppermute | solution.py:25
  291.0 2.7 collective-permute-start.52
  301.5 2.8 collective-permute-done.53
  304.5 6.7 %shard_map.147 = (bf16[512,768]{1,0:T(8,128)(2,1)S(1)}, bf16[384,1024]{1,0:T(8,128)(2,1)S(1)}, bf16[128,1024]{1,0:T(8,128)(2,1)S(1)}) custom-call(bf16[384,1024]{1,0:T(8,128)(2,1)S(1)} %pad_maximum_fusion.13.near, bf16[128,1024]{1,0:T(8,128)(2,1)S(1)} %collective-permute-done.54.far, bf16[1024,768]{1,0:T(8,128)(2,1)S(1)} %pad_maximum_fusion.3.w_qkv, ...), custom_call_target="tpu_custom_call" | custom-call | flops 4294967296 | bytes 8388608 | tf_op jit(solution)/shard_map/pallas_call | solution.py:239
  322.2 4.4 all-to-all-start
  328.8 2.8 collective-permute-start.63
  335.3 8.4 %collective-permute-done.63 = bf16[128,1024]{1,0:T(8,128)(2,1)S(1)} collective-permute-done((bf16[128,1024]{1,0:T(8,128)(2,1)}, bf16[128,1024]{1,0:T(8,128)(2,1)S(1)}, u32[]{:S(2)}, u32[]{:S(2)}) %collective-permute-start.63) | collective-permute-done | bytes 262176 | tf_op jit(solution)/shard_map/ppermute | solution.py:25
  347.5 6.2 %all-to-all-done = bf16[8,128,1024]{2,1,0:T(8,128)(2,1)} async-done(((bf16[8,128,1024]{2,1,0:T(8,128)(2,1)}), bf16[8,128,1024]{2,1,0:T(8,128)(2,1)}, u32[]{:S(2)}, u32[]{:S(2)}) %all-to-all-start) | async-done | bytes 2097184 | tf_op jit(solution)/shard_map/all_to_all | solution.py:429
  353.7 8.4 %all-to-all-start.1 = ((bf16[8,544,256]{2,1,0:T(8,128)(2,1)}), bf16[8,544,256]{2,1,0:T(8,128)(2,1)S(1)}, u32[]{:S(2)}, u32[]{:S(2)}) async-start(bf16[8,544,256]{2,1,0:T(8,128)(2,1)} %bitcast.44), calls=%async_computation.2 | async-start | bytes 4456448 | tf_op jit(solution)/shard_map/all_to_all | solution.py:429
  372.4 4.3 collective-permute-done.58
  376.8 3.3 collective-permute-done.57
  386.3 4.3 all-to-all-done.1
  391.0 2.7 collective-permute-start.71
  401.5 2.8 collective-permute-done.64
  406.6 7.7 %collective-permute-done.72 = bf16[196,1024]{1,0:T(8,128)(2,1)S(1)} collective-permute-done((bf16[196,1024]{1,0:T(8,128)(2,1)S(1)}, bf16[196,1024]{1,0:T(8,128)(2,1)S(1)}, u32[]{:S(2)}, u32[]{:S(2)}) %collective-permute-start.72) | collective-permute-done | bytes 401440 | tf_op jit(solution)/shard_map/ppermute | solution.py:33
  414.8 27.1 %all_to_all.36 = bf16[8,128,1024]{2,1,0:T(8,128)(2,1)S(1)} all-to-all(bf16[8,128,1024]{2,1,0:T(8,128)(2,1)S(1)} %broadcast_in_dim.113), channel_id=1, replica_groups=mesh['section'=2,'zlo'=2,'x'=4,'core'=2,'tensor'=4] {'zlo','x'}, dimensions={0} | all-to-all | bytes 4194304 | tf_op jit(solution)/shard_map/all_to_all | solution.py:436
  442.0 3.8 collective-permute-start.73
  447.0 4.3 all-to-all-start.3
  455.8 2.8 maximum_convert_fusion
  458.5 9.4 %all-to-all-done.3 = bf16[8,272,256]{2,1,0:T(8,128)(2,1)} async-done(((bf16[8,272,256]{2,1,0:T(8,128)(2,1)}), bf16[8,272,256]{2,1,0:T(8,128)(2,1)}, u32[]{:S(2)}, u32[]{:S(2)}) %all-to-all-start.3) | async-done | bytes 1114144 | tf_op jit(solution)/shard_map/all_to_all | solution.py:436
  (568 shorter events, 218.2 us)
Async XLA Ops:
  7.2 319.4 %reduce-scatter.2.cloned.1.call-start = ((), (), s32[]{:S(2)}) async-start(), calls=%async_computation.5 | async-start | bytes 2359296 | tf_op jit(solution)/shard_map/reduce_scatter | solution.py:425
  9.0 22.7 %collective-permute-start.1 = (bf16[128,1024]{1,0:T(8,128)(2,1)S(1)}, bf16[128,1024]{1,0:T(8,128)(2,1)S(1)}, u32[]{:S(2)}, u32[]{:S(2)}) collective-permute-start(bf16[128,1024]{1,0:T(8,128)(2,1)S(1)} %get-tuple-element.223), channel_id=1, source_target_pairs={{0,1},{1,2},{2,3},{3,0},{4,5},{5,6},{6,7},{7,4},{8,9},{9,10},{10,1... | collective-permute-start | bytes 786440 | tf_op jit(solution)/shard_map/ppermute | solution.py:25
  11.1 20.6 %collective-permute-start = (bf16[128,1024]{1,0:T(8,128)(2,1)S(1)}, bf16[128,1024]{1,0:T(8,128)(2,1)S(1)}, u32[]{:S(2)}, u32[]{:S(2)}) collective-permute-start(bf16[128,1024]{1,0:T(8,128)(2,1)S(1)} %get-tuple-element.223), channel_id=1, source_target_pairs={{0,3},{1,0},{2,1},{3,2},{4,7},{5,4},{6,5},{7,6},{8,11},{9,8},{10,9... | collective-permute-start | bytes 786440 | tf_op jit(solution)/shard_map/ppermute | solution.py:25
  12.6 21.7 %collective-permute-start.2 = (bf16[128,1024]{1,0:T(8,128)(2,1)S(1)}, bf16[128,1024]{1,0:T(8,128)(2,1)S(1)}, u32[]{:S(2)}, u32[]{:S(2)}) collective-permute-start(bf16[128,1024]{1,0:T(8,128)(2,1)S(1)} %get-tuple-element.223), channel_id=1, source_target_pairs={{0,2},{1,3},{2,0},{3,1},{4,6},{5,7},{6,4},{7,5},{8,10},{9,11},{10,... | collective-permute-start | bytes 786440 | tf_op jit(solution)/shard_map/ppermute | solution.py:25
  15.2 12.0 %collective-permute-start.4 = (bf16[128,1024]{1,0:T(8,128)(2,1)S(1)}, bf16[128,1024]{1,0:T(8,128)(2,1)}, u32[]{:S(2)}, u32[]{:S(2)}) collective-permute-start(bf16[128,1024]{1,0:T(8,128)(2,1)S(1)} %constant_dynamic-slice_fusion.3), channel_id=1, source_target_pairs={{0,96},{32,64},{64,32},{96,0},{1,97},{33,65},{65,33},{97,1},{2,98}... | collective-permute-start | bytes 786440 | tf_op jit(solution)/shard_map/ppermute | solution.py:37
  24.5 18.7 %collective-permute-start.3 = (bf16[1536,256]{1,0:T(8,128)(2,1)}, bf16[1536,256]{1,0:T(8,128)(2,1)S(1)}, u32[]{:S(2)}, u32[]{:S(2)}) collective-permute-start(bf16[1536,256]{1,0:T(8,128)(2,1)} %constant_dynamic-slice_fusion.4), channel_id=1, source_target_pairs={{0,96},{32,64},{64,32},{96,0},{1,97},{33,65},{65,33},{97,1},{2,98}... | collective-permute-start | bytes 2359304 | tf_op jit(solution)/shard_map/ppermute | solution.py:37
  31.7 34.6 %collective-permute-start.13 = (bf16[328,1024]{1,0:T(8,128)(2,1)}, bf16[328,1024]{1,0:T(8,128)(2,1)}, u32[]{:S(2)}, u32[]{:S(2)}) collective-permute-start(bf16[328,1024]{1,0:T(8,128)(2,1)} %constant_dynamic-slice_fusion.2), channel_id=1, source_target_pairs={{0,96},{32,64},{64,32},{96,0},{1,97},{33,65},{65,33},{97,1},{2,98}... | collective-permute-start | bytes 2015240 | tf_op jit(solution)/shard_map/ppermute | solution.py:37
  65.0 13.1 %collective-permute-start.8 = (bf16[128,1024]{1,0:T(8,128)(2,1)S(1)}, bf16[128,1024]{1,0:T(8,128)(2,1)S(1)}, u32[]{:S(2)}, u32[]{:S(2)}) collective-permute-start(bf16[128,1024]{1,0:T(8,128)(2,1)S(1)} %get-tuple-element.102), channel_id=1, source_target_pairs={{0,2},{1,3},{2,0},{3,1},{4,6},{5,7},{6,4},{7,5},{8,10},{9,11},{10,... | collective-permute-start | bytes 786440 | tf_op jit(solution)/shard_map/ppermute | solution.py:25
  66.4 17.2 %collective-permute-start.15 = (bf16[328,1024]{1,0:T(8,128)(2,1)S(1)}, bf16[328,1024]{1,0:T(8,128)(2,1)S(1)}, u32[]{:S(2)}, u32[]{:S(2)}) collective-permute-start(bf16[328,1024]{1,0:T(8,128)(2,1)S(1)} %constant_dynamic-slice_fusion.1), channel_id=1, source_target_pairs={{0,96},{32,64},{64,32},{96,0},{1,97},{33,65},{65,33},{97,1},{2,98}... | collective-permute-start | bytes 2015240 | tf_op jit(solution)/shard_map/ppermute | solution.py:37
  69.2 21.8 %collective-permute-start.14 = (bf16[328,1024]{1,0:T(8,128)(2,1)}, bf16[328,1024]{1,0:T(8,128)(2,1)S(1)}, u32[]{:S(2)}, u32[]{:S(2)}) collective-permute-start(bf16[328,1024]{1,0:T(8,128)(2,1)} %collective-permute-done.13), channel_id=1, source_target_pairs={{0,4},{4,0},{1,5},{5,1},{2,6},{6,2},{3,7},{7,3},{8,12},{12,8},{9,1... | collective-permute-start | bytes 2015240 | tf_op jit(solution)/shard_map/ppermute | solution.py:29
  78.9 11.1 %collective-permute-start.11 = (bf16[128,1024]{1,0:T(8,128)(2,1)S(1)}, bf16[128,1024]{1,0:T(8,128)(2,1)S(1)}, u32[]{:S(2)}, u32[]{:S(2)}) collective-permute-start(bf16[128,1024]{1,0:T(8,128)(2,1)S(1)} %multiply_convert_fusion.5), channel_id=1, source_target_pairs={{0,3},{1,0},{2,1},{3,2},{4,7},{5,4},{6,5},{7,6},{8,11},{9,8},{10,9... | collective-permute-start | bytes 786440 | tf_op jit(solution)/shard_map/ppermute | solution.py:25
  83.6 16.2 %collective-permute-start.17 = (bf16[328,1024]{1,0:T(8,128)(2,1)S(1)}, bf16[328,1024]{1,0:T(8,128)(2,1)S(1)}, u32[]{:S(2)}, u32[]{:S(2)}) collective-permute-start(bf16[328,1024]{1,0:T(8,128)(2,1)S(1)} %constant_dynamic-slice_fusion), channel_id=1, source_target_pairs={{0,96},{32,64},{64,32},{96,0},{1,97},{33,65},{65,33},{97,1},{2,98}... | collective-permute-start | bytes 2015240 | tf_op jit(solution)/shard_map/ppermute | solution.py:37
  86.3 16.1 %collective-permute-start.16 = (bf16[328,1024]{1,0:T(8,128)(2,1)S(1)}, bf16[328,1024]{1,0:T(8,128)(2,1)S(1)}, u32[]{:S(2)}, u32[]{:S(2)}) collective-permute-start(bf16[328,1024]{1,0:T(8,128)(2,1)S(1)} %collective-permute-done.15), channel_id=1, source_target_pairs={{0,4},{4,0},{1,5},{5,1},{2,6},{6,2},{3,7},{7,3},{8,12},{12,8},{9,1... | collective-permute-start | bytes 2015240 | tf_op jit(solution)/shard_map/ppermute | solution.py:29
  114.3 14.5 %collective-permute-start.21 = (bf16[128,1024]{1,0:T(8,128)(2,1)S(1)}, bf16[128,1024]{1,0:T(8,128)(2,1)S(1)}, u32[]{:S(2)}, u32[]{:S(2)}) collective-permute-start(bf16[128,1024]{1,0:T(8,128)(2,1)S(1)} %get-tuple-element.306), channel_id=1, source_target_pairs={{0,1},{1,2},{2,3},{3,0},{4,5},{5,6},{6,7},{7,4},{8,9},{9,10},{10,1... | collective-permute-start | bytes 786440 | tf_op jit(solution)/shard_map/ppermute | solution.py:25
  117.1 11.6 %collective-permute-start.20 = (bf16[128,1024]{1,0:T(8,128)(2,1)S(1)}, bf16[128,1024]{1,0:T(8,128)(2,1)S(1)}, u32[]{:S(2)}, u32[]{:S(2)}) collective-permute-start(bf16[128,1024]{1,0:T(8,128)(2,1)S(1)} %convolution_convert_fusion.13), channel_id=1, source_target_pairs={{0,2},{1,3},{2,0},{3,1},{4,6},{5,7},{6,4},{7,5},{8,10},{9,11},{10,... | collective-permute-start | bytes 786440 | tf_op jit(solution)/shard_map/ppermute | solution.py:25
  130.2 10.9 %collective-permute-start.24 = (bf16[128,1024]{1,0:T(8,128)(2,1)}, bf16[128,1024]{1,0:T(8,128)(2,1)}, u32[]{:S(2)}, u32[]{:S(2)}) collective-permute-start(bf16[128,1024]{1,0:T(8,128)(2,1)} %fusion.46), channel_id=1, source_target_pairs={{0,1},{1,2},{2,3},{3,0},{4,5},{5,6},{6,7},{7,4},{8,9},{9,10},{10,1... | collective-permute-start | bytes 786440 | tf_op jit(solution)/shard_map/ppermute | solution.py:25
  130.2 10.9 %collective-permute-start.23 = (bf16[128,1024]{1,0:T(8,128)(2,1)}, bf16[128,1024]{1,0:T(8,128)(2,1)}, u32[]{:S(2)}, u32[]{:S(2)}) collective-permute-start(bf16[128,1024]{1,0:T(8,128)(2,1)} %fusion.46), channel_id=1, source_target_pairs={{0,3},{1,0},{2,1},{3,2},{4,7},{5,4},{6,5},{7,6},{8,11},{9,8},{10,9... | collective-permute-start | bytes 786440 | tf_op jit(solution)/shard_map/ppermute | solution.py:25
  154.3 19.1 %collective-permute-start.33 = (bf16[128,1024]{1,0:T(8,128)(2,1)S(1)}, bf16[128,1024]{1,0:T(8,128)(2,1)S(1)}, u32[]{:S(2)}, u32[]{:S(2)}) collective-permute-start(bf16[128,1024]{1,0:T(8,128)(2,1)S(1)} %select_bitcast_fusion.9), channel_id=1, source_target_pairs={{0,1},{1,2},{2,3},{3,0},{4,5},{5,6},{6,7},{7,4},{8,9},{9,10},{10,1... | collective-permute-start | bytes 786440 | tf_op jit(solution)/shard_map/ppermute | solution.py:25
  156.1 17.2 %collective-permute-start.32 = (bf16[128,1024]{1,0:T(8,128)(2,1)S(1)}, bf16[128,1024]{1,0:T(8,128)(2,1)S(1)}, u32[]{:S(2)}, u32[]{:S(2)}) collective-permute-start(bf16[128,1024]{1,0:T(8,128)(2,1)S(1)} %select_bitcast_fusion.9), channel_id=1, source_target_pairs={{0,3},{1,0},{2,1},{3,2},{4,7},{5,4},{6,5},{7,6},{8,11},{9,8},{10,9... | collective-permute-start | bytes 786440 | tf_op jit(solution)/shard_map/ppermute | solution.py:25
  157.7 16.9 %collective-permute-start.34 = (bf16[128,1024]{1,0:T(8,128)(2,1)S(1)}, bf16[128,1024]{1,0:T(8,128)(2,1)S(1)}, u32[]{:S(2)}, u32[]{:S(2)}) collective-permute-start(bf16[128,1024]{1,0:T(8,128)(2,1)S(1)} %select_bitcast_fusion.9), channel_id=1, source_target_pairs={{0,2},{1,3},{2,0},{3,1},{4,6},{5,7},{6,4},{7,5},{8,10},{9,11},{10,... | collective-permute-start | bytes 786440 | tf_op jit(solution)/shard_map/ppermute | solution.py:25
  164.0 20.5 %collective-permute-start.30 = (bf16[128,1024]{1,0:T(8,128)(2,1)S(1)}, bf16[128,1024]{1,0:T(8,128)(2,1)S(1)}, u32[]{:S(2)}, u32[]{:S(2)}) collective-permute-start(bf16[128,1024]{1,0:T(8,128)(2,1)S(1)} %multiply_convert_fusion.4), channel_id=1, source_target_pairs={{0,1},{1,2},{2,3},{3,0},{4,5},{5,6},{6,7},{7,4},{8,9},{9,10},{10,1... | collective-permute-start | bytes 786440 | tf_op jit(solution)/shard_map/ppermute | solution.py:25
  164.5 20.1 %collective-permute-start.29 = (bf16[128,1024]{1,0:T(8,128)(2,1)S(1)}, bf16[128,1024]{1,0:T(8,128)(2,1)S(1)}, u32[]{:S(2)}, u32[]{:S(2)}) collective-permute-start(bf16[128,1024]{1,0:T(8,128)(2,1)S(1)} %multiply_convert_fusion.4), channel_id=1, source_target_pairs={{0,3},{1,0},{2,1},{3,2},{4,7},{5,4},{6,5},{7,6},{8,11},{9,8},{10,9... | collective-permute-start | bytes 786440 | tf_op jit(solution)/shard_map/ppermute | solution.py:25
  174.5 15.0 %collective-permute-start.31 = (bf16[128,1024]{1,0:T(8,128)(2,1)S(1)}, bf16[128,1024]{1,0:T(8,128)(2,1)S(1)}, u32[]{:S(2)}, u32[]{:S(2)}) collective-permute-start(bf16[128,1024]{1,0:T(8,128)(2,1)S(1)} %multiply_convert_fusion.4), channel_id=1, source_target_pairs={{0,2},{1,3},{2,0},{3,1},{4,6},{5,7},{6,4},{7,5},{8,10},{9,11},{10,... | collective-permute-start | bytes 786440 | tf_op jit(solution)/shard_map/ppermute | solution.py:25
  205.8 11.9 %collective-permute-start.39 = (bf16[128,1024]{1,0:T(8,128)(2,1)S(1)}, bf16[128,1024]{1,0:T(8,128)(2,1)S(1)}, u32[]{:S(2)}, u32[]{:S(2)}) collective-permute-start(bf16[128,1024]{1,0:T(8,128)(2,1)S(1)} %get-tuple-element.232), channel_id=1, source_target_pairs={{0,1},{1,2},{2,3},{3,0},{4,5},{5,6},{6,7},{7,4},{8,9},{9,10},{10,1... | collective-permute-start | bytes 786440 | tf_op jit(solution)/shard_map/ppermute | solution.py:25
  205.9 11.8 %collective-permute-start.38 = (bf16[128,1024]{1,0:T(8,128)(2,1)S(1)}, bf16[128,1024]{1,0:T(8,128)(2,1)S(1)}, u32[]{:S(2)}, u32[]{:S(2)}) collective-permute-start(bf16[128,1024]{1,0:T(8,128)(2,1)S(1)} %get-tuple-element.232), channel_id=1, source_target_pairs={{0,3},{1,0},{2,1},{3,2},{4,7},{5,4},{6,5},{7,6},{8,11},{9,8},{10,9... | collective-permute-start | bytes 786440 | tf_op jit(solution)/shard_map/ppermute | solution.py:25
  210.4 43.1 %collective-permute-start.48 = (bf16[328,1024]{1,0:T(8,128)(2,1)}, bf16[328,1024]{1,0:T(8,128)(2,1)}, u32[]{:S(2)}, u32[]{:S(2)}) collective-permute-start(bf16[328,1024]{1,0:T(8,128)(2,1)} %convolution_convert_fusion.7), channel_id=1, source_target_pairs={{0,4},{4,0},{1,5},{5,1},{2,6},{6,2},{3,7},{7,3},{8,12},{12,8},{9,1... | collective-permute-start | bytes 2015240 | tf_op jit(solution)/shard_map/ppermute | solution.py:29
  216.9 43.4 %collective-permute-start.47 = (bf16[656,1024]{1,0:T(8,128)(2,1)}, bf16[656,1024]{1,0:T(8,128)(2,1)}, u32[]{:S(2)}, u32[]{:S(2)}) collective-permute-start(bf16[656,1024]{1,0:T(8,128)(2,1)} %convolution_convert_fusion.1), channel_id=1, source_target_pairs={{0,4},{4,0},{1,5},{5,1},{2,6},{6,2},{3,7},{7,3},{8,12},{12,8},{9,1... | collective-permute-start | bytes 4030472 | tf_op jit(solution)/shard_map/ppermute | solution.py:29
  226.1 11.9 %collective-permute-start.41 = (bf16[128,1024]{1,0:T(8,128)(2,1)S(1)}, bf16[128,1024]{1,0:T(8,128)(2,1)S(1)}, u32[]{:S(2)}, u32[]{:S(2)}) collective-permute-start(bf16[128,1024]{1,0:T(8,128)(2,1)S(1)} %get-tuple-element.135), channel_id=1, source_target_pairs={{0,2},{1,3},{2,0},{3,1},{4,6},{5,7},{6,4},{7,5},{8,10},{9,11},{10,... | collective-permute-start | bytes 786440 | tf_op jit(solution)/shard_map/ppermute | solution.py:25
  239.0 16.6 %collective-permute-start.45 = (bf16[128,1024]{1,0:T(8,128)(2,1)S(1)}, bf16[128,1024]{1,0:T(8,128)(2,1)}, u32[]{:S(2)}, u32[]{:S(2)}) collective-permute-start(bf16[128,1024]{1,0:T(8,128)(2,1)S(1)} %add_convert_fusion.9), channel_id=1, source_target_pairs={{0,1},{1,2},{2,3},{3,0},{4,5},{5,6},{6,7},{7,4},{8,9},{9,10},{10,1... | collective-permute-start | bytes 786440 | tf_op jit(solution)/shard_map/ppermute | solution.py:25
  239.0 16.8 %collective-permute-start.44 = (bf16[128,1024]{1,0:T(8,128)(2,1)S(1)}, bf16[128,1024]{1,0:T(8,128)(2,1)}, u32[]{:S(2)}, u32[]{:S(2)}) collective-permute-start(bf16[128,1024]{1,0:T(8,128)(2,1)S(1)} %add_convert_fusion.9), channel_id=1, source_target_pairs={{0,3},{1,0},{2,1},{3,2},{4,7},{5,4},{6,5},{7,6},{8,11},{9,8},{10,9... | collective-permute-start | bytes 786440 | tf_op jit(solution)/shard_map/ppermute | solution.py:25
  244.1 13.7 %collective-permute-start.67 = (bf16[1024,256]{1,0:T(8,128)(2,1)}, bf16[1024,256]{1,0:T(8,128)(2,1)}, u32[]{:S(2)}, u32[]{:S(2)}) collective-permute-start(bf16[1024,256]{1,0:T(8,128)(2,1)} %convolution_convert_fusion.9), channel_id=1, source_target_pairs={{0,4},{4,0},{1,5},{5,1},{2,6},{6,2},{3,7},{7,3},{8,12},{12,8},{9,1... | collective-permute-start | bytes 1572872 | tf_op jit(solution)/shard_map/ppermute | solution.py:29
  253.4 10.8 %collective-permute-start.46 = (bf16[128,1024]{1,0:T(8,128)(2,1)S(1)}, bf16[128,1024]{1,0:T(8,128)(2,1)}, u32[]{:S(2)}, u32[]{:S(2)}) collective-permute-start(bf16[128,1024]{1,0:T(8,128)(2,1)S(1)} %add_convert_fusion.9), channel_id=1, source_target_pairs={{0,2},{1,3},{2,0},{3,1},{4,6},{5,7},{6,4},{7,5},{8,10},{9,11},{10,... | collective-permute-start | bytes 786440 | tf_op jit(solution)/shard_map/ppermute | solution.py:25
  255.6 22.4 %collective-permute-start.68 = (bf16[1024,256]{1,0:T(8,128)(2,1)}, bf16[1024,256]{1,0:T(8,128)(2,1)S(1)}, u32[]{:S(2)}, u32[]{:S(2)}) collective-permute-start(bf16[1024,256]{1,0:T(8,128)(2,1)} %convolution_convert_fusion.8), channel_id=1, source_target_pairs={{0,4},{4,0},{1,5},{5,1},{2,6},{6,2},{3,7},{7,3},{8,12},{12,8},{9,1... | collective-permute-start | bytes 1572872 | tf_op jit(solution)/shard_map/ppermute | solution.py:29
  274.9 12.0 %collective-permute-start.49 = (bf16[128,1024]{1,0:T(8,128)(2,1)}, bf16[128,1024]{1,0:T(8,128)(2,1)}, u32[]{:S(2)}, u32[]{:S(2)}) collective-permute-start(bf16[128,1024]{1,0:T(8,128)(2,1)} %convolution_convert_fusion.14), channel_id=1, source_target_pairs={{0,2},{1,3},{2,0},{3,1},{4,6},{5,7},{6,4},{7,5},{8,10},{9,11},{10,... | collective-permute-start | bytes 786440 | tf_op jit(solution)/shard_map/ppermute | solution.py:25
  291.0 13.4 %collective-permute-start.53 = (bf16[128,1024]{1,0:T(8,128)(2,1)S(1)}, bf16[128,1024]{1,0:T(8,128)(2,1)S(1)}, u32[]{:S(2)}, u32[]{:S(2)}) collective-permute-start(bf16[128,1024]{1,0:T(8,128)(2,1)S(1)} %get-tuple-element.226), channel_id=1, source_target_pairs={{0,1},{1,2},{2,3},{3,0},{4,5},{5,6},{6,7},{7,4},{8,9},{9,10},{10,1... | collective-permute-start | bytes 786440 | tf_op jit(solution)/shard_map/ppermute | solution.py:25
  291.0 13.4 %collective-permute-start.52 = (bf16[128,1024]{1,0:T(8,128)(2,1)S(1)}, bf16[128,1024]{1,0:T(8,128)(2,1)S(1)}, u32[]{:S(2)}, u32[]{:S(2)}) collective-permute-start(bf16[128,1024]{1,0:T(8,128)(2,1)S(1)} %get-tuple-element.226), channel_id=1, source_target_pairs={{0,3},{1,0},{2,1},{3,2},{4,7},{5,4},{6,5},{7,6},{8,11},{9,8},{10,9... | collective-permute-start | bytes 786440 | tf_op jit(solution)/shard_map/ppermute | solution.py:25
  293.7 10.7 %collective-permute-start.54 = (bf16[128,1024]{1,0:T(8,128)(2,1)S(1)}, bf16[128,1024]{1,0:T(8,128)(2,1)S(1)}, u32[]{:S(2)}, u32[]{:S(2)}) collective-permute-start(bf16[128,1024]{1,0:T(8,128)(2,1)S(1)} %get-tuple-element.226), channel_id=1, source_target_pairs={{0,2},{1,3},{2,0},{3,1},{4,6},{5,7},{6,4},{7,5},{8,10},{9,11},{10,... | collective-permute-start | bytes 786440 | tf_op jit(solution)/shard_map/ppermute | solution.py:25
  298.6 18.3 %collective-permute-start.56 = (bf16[328,1024]{1,0:T(8,128)(2,1)S(1)}, bf16[328,1024]{1,0:T(8,128)(2,1)S(1)}, u32[]{:S(2)}, u32[]{:S(2)}) collective-permute-start(bf16[328,1024]{1,0:T(8,128)(2,1)S(1)} %convolution_convert_fusion.6), channel_id=1, source_target_pairs={{0,4},{4,0},{1,5},{5,1},{2,6},{6,2},{3,7},{7,3},{8,12},{12,8},{9,1... | collective-permute-start | bytes 2015240 | tf_op jit(solution)/shard_map/ppermute | solution.py:29
  300.6 19.0 %collective-permute-start.55 = (bf16[656,1024]{1,0:T(8,128)(2,1)S(1)}, bf16[656,1024]{1,0:T(8,128)(2,1)S(1)}, u32[]{:S(2)}, u32[]{:S(2)}) collective-permute-start(bf16[656,1024]{1,0:T(8,128)(2,1)S(1)} %convolution_convert_fusion), channel_id=1, source_target_pairs={{0,4},{4,0},{1,5},{5,1},{2,6},{6,2},{3,7},{7,3},{8,12},{12,8},{9,1... | collective-permute-start | bytes 4030472 | tf_op jit(solution)/shard_map/ppermute | solution.py:29
  322.2 31.5 %all-to-all-start = ((bf16[8,128,1024]{2,1,0:T(8,128)(2,1)}), bf16[8,128,1024]{2,1,0:T(8,128)(2,1)}, u32[]{:S(2)}, u32[]{:S(2)}) async-start(bf16[8,128,1024]{2,1,0:T(8,128)(2,1)} %bitcast.39), calls=%async_computation.1 | async-start | bytes 4194304 | tf_op jit(solution)/shard_map/all_to_all | solution.py:429
  328.3 15.5 %collective-permute-start.61 = (bf16[128,1024]{1,0:T(8,128)(2,1)S(1)}, bf16[128,1024]{1,0:T(8,128)(2,1)S(1)}, u32[]{:S(2)}, u32[]{:S(2)}) collective-permute-start(bf16[128,1024]{1,0:T(8,128)(2,1)S(1)} %copy-done.11), channel_id=1, source_target_pairs={{0,2},{1,3},{2,0},{3,1},{4,6},{5,7},{6,4},{7,5},{8,10},{9,11},{10,... | collective-permute-start | bytes 786440 | tf_op jit(solution)/shard_map/ppermute | solution.py:25
  328.8 14.9 %collective-permute-start.63 = (bf16[128,1024]{1,0:T(8,128)(2,1)}, bf16[128,1024]{1,0:T(8,128)(2,1)S(1)}, u32[]{:S(2)}, u32[]{:S(2)}) collective-permute-start(bf16[128,1024]{1,0:T(8,128)(2,1)} %get-tuple-element.295), channel_id=1, source_target_pairs={{0,3},{1,0},{2,1},{3,2},{4,7},{5,4},{6,5},{7,6},{8,11},{9,8},{10,9... | collective-permute-start | bytes 786440 | tf_op jit(solution)/shard_map/ppermute | solution.py:25
  331.5 12.3 %collective-permute-start.62 = (bf16[128,1024]{1,0:T(8,128)(2,1)}, bf16[128,1024]{1,0:T(8,128)(2,1)}, u32[]{:S(2)}, u32[]{:S(2)}) collective-permute-start(bf16[128,1024]{1,0:T(8,128)(2,1)} %get-tuple-element.294), channel_id=1, source_target_pairs={{0,1},{1,2},{2,3},{3,0},{4,5},{5,6},{6,7},{7,4},{8,9},{9,10},{10,1... | collective-permute-start | bytes 786440 | tf_op jit(solution)/shard_map/ppermute | solution.py:25
  353.7 36.9 %all-to-all-start.1 = ((bf16[8,544,256]{2,1,0:T(8,128)(2,1)}), bf16[8,544,256]{2,1,0:T(8,128)(2,1)S(1)}, u32[]{:S(2)}, u32[]{:S(2)}) async-start(bf16[8,544,256]{2,1,0:T(8,128)(2,1)} %bitcast.44), calls=%async_computation.2 | async-start | bytes 4456448 | tf_op jit(solution)/shard_map/all_to_all | solution.py:429
  369.0 11.0 %collective-permute-start.57 = (bf16[128,1024]{1,0:T(8,128)(2,1)}, bf16[128,1024]{1,0:T(8,128)(2,1)}, u32[]{:S(2)}, u32[]{:S(2)}) collective-permute-start(bf16[128,1024]{1,0:T(8,128)(2,1)} %convolution_convert_fusion.12), channel_id=1, source_target_pairs={{0,2},{1,3},{2,0},{3,1},{4,6},{5,7},{6,4},{7,5},{8,10},{9,11},{10,... | collective-permute-start | bytes 786440 | tf_op jit(solution)/shard_map/ppermute | solution.py:25
  382.2 19.3 %collective-permute-start.60 = (bf16[128,1024]{1,0:T(8,128)(2,1)}, bf16[128,1024]{1,0:T(8,128)(2,1)}, u32[]{:S(2)}, u32[]{:S(2)}) collective-permute-start(bf16[128,1024]{1,0:T(8,128)(2,1)} %get-tuple-element.224), channel_id=1, source_target_pairs={{0,64},{64,0},{1,65},{65,1},{2,66},{66,2},{3,67},{67,3},{4,68},{68... | collective-permute-start | bytes 786440 | tf_op jit(solution)/shard_map/ppermute | solution.py:33
  404.2 10.1 %collective-permute-start.72 = (bf16[196,1024]{1,0:T(8,128)(2,1)S(1)}, bf16[196,1024]{1,0:T(8,128)(2,1)S(1)}, u32[]{:S(2)}, u32[]{:S(2)}) collective-permute-start(bf16[196,1024]{1,0:T(8,128)(2,1)S(1)} %broadcast_select_fusion.20), channel_id=1, source_target_pairs={{0,64},{64,0},{1,65},{65,1},{2,66},{66,2},{3,67},{67,3},{4,68},{68... | collective-permute-start | bytes 1204232 | tf_op jit(solution)/shard_map/ppermute | solution.py:33
  447.0 20.9 %all-to-all-start.3 = ((bf16[8,272,256]{2,1,0:T(8,128)(2,1)}), bf16[8,272,256]{2,1,0:T(8,128)(2,1)}, u32[]{:S(2)}, u32[]{:S(2)}) async-start(bf16[8,272,256]{2,1,0:T(8,128)(2,1)} %broadcast_in_dim.114), calls=%async_computation.4 | async-start | bytes 2228224 | tf_op jit(solution)/shard_map/all_to_all | solution.py:436
  (139 other events, 1273.2 us)
Sparse Core Ops, SparseCore 0:
  279.1 36.3 reduce-scatter.1
